TPU v7x, 32 devices: a whole 2x2x4 slice. The times are simulated.
32 devices in a mesh: stream: 4 (over y, x), tok: 8 (over z, core).
Axes of the slice: x: 2, y: 2, z: 4, core: 2. Of those that a mesh axis runs over, the one named last changes fastest.
Arguments:
- latents: bfloat16 [32, 128, 768], P('stream'), may hold values from -6 to 6
- tokens: bfloat16 [32768, 768], P(('stream', 'tok')), may hold values from -6 to 6
- token_sample: int32 [32768], P(('stream', 'tok')), may hold values from 0 to 31, as said below
- token_mask: int32 [32768], P(('stream', 'tok')), may hold values from 0 to 1, as said below
- drop_mask: int32 [32], replicated, may hold values from 0 to 1, as said below
- gain_query: float32 [768], replicated, may hold values from 0.25 to 1.75
- w_query: bfloat16 [768, 768], replicated, may hold values from -0.21875 to 0.21875
- gain_token: float32 [768], replicated, may hold values from 0.25 to 1.75
- w_key: bfloat16 [768, 768], replicated, may hold values from -0.21875 to 0.21875
- w_value: bfloat16 [768, 768], replicated, may hold values from -0.21875 to 0.21875
- w_out: bfloat16 [768, 768], replicated, may hold values from -6 to 6
- gain_mlp: float32 [768], replicated, may hold values from 0.25 to 1.75
- w_up: bfloat16 [768, 3072], replicated, may hold values from -0.21875 to 0.21875
- b_up: float32 [3072], replicated, may hold values from -3 to 3
- w_down: bfloat16 [3072, 768], replicated, may hold values from -0.109375 to 0.109375
- b_down: float32 [768], replicated, may hold values from -3 to 3
- cotangent: bfloat16 [32, 128, 768], P('stream'), may hold values from -6 to 6
Outputs:
- result: bfloat16 [32, 128, 768], P('stream')
- d_latents: float32 [32, 128, 768], P('stream')
- d_tokens: float32 [32768, 768], P(('stream', 'tok'))
- d_gain_query: float32 [768], P('stream')
- d_w_query: float32 [768, 768], P(None, 'stream')
- d_gain_token: float32 [768], replicated
- d_w_key: float32 [768, 768], replicated
- d_w_value: float32 [768, 768], replicated
- d_w_out: float32 [768, 768], P(None, 'stream')
- d_gain_mlp: float32 [768], P('stream')
- d_w_up: float32 [768, 3072], P(None, 'stream')
- d_b_up: float32 [3072], P('stream')
- d_w_down: float32 [3072, 768], P('stream')
- d_b_down: float32 [768], P('stream')
Inputs may be any that keep to these rules, and one draw needn't show every extreme that they name: `token_sample`: tokens on devices of stream index s name only samples s * 8 to s * 8 + 7, and every sample has real tokens on some device of its group. `token_mask`: on each device the real tokens come first; the last stream index holds text and is mostly padding, the first device of each group is full. `drop_mask`: at least one sample applies the block.
All inputs are finite; a program needn't handle non-finite values.
Results may differ from a plain program's by a relative error of at most 0.015.
Values sent between devices are 32-bit elements; how exact they have to be, the bound alone decides.
A program may use at most 192 MiB of HBM per device.

v0:
```python
import jax
import jax.numpy as jnp
from jax import lax
from jax.sharding import PartitionSpec as P

HEADS = 12
HEAD_DIM = 64


def layer_norm(values, gain):
    center = values - jnp.mean(values, -1, keepdims=True)
    spread = jnp.mean(center * center, -1, keepdims=True)
    return center * lax.rsqrt(spread + 1e-05) * gain


def local(
    latents,
    tokens,
    token_sample,
    token_mask,
    drop_mask,
    gain_query,
    w_query,
    gain_token,
    w_key,
    w_value,
    w_out,
    gain_mlp,
    w_up,
    b_up,
    w_down,
    b_down,
    cotangent,
):
    f32 = jnp.float32
    bf16 = jnp.bfloat16
    samples, lat_rows, width = latents.shape
    token_rows = tokens.shape[0]
    group_index = lax.axis_index("stream")
    samples_all = drop_mask.shape[0]
    scale_all = drop_mask.astype(f32) * samples_all / jnp.sum(drop_mask).astype(f32)
    factor = lax.dynamic_slice_in_dim(scale_all, group_index * samples, samples)[:, None, None]
    local_ids = token_sample - group_index * samples
    valid = (local_ids[None, :] == jnp.arange(samples, dtype=jnp.int32)[:, None]) & (
        token_mask[None, :] == 1
    )
    lat_f = latents.astype(f32)
    normed, query_norm_back = jax.vjp(layer_norm, lat_f, gain_query)
    normed_low = normed.astype(bf16).reshape(samples * lat_rows, width)
    query = (
        jnp.dot(normed_low, w_query, preferred_element_type=f32)
        .astype(bf16)
        .reshape(samples, lat_rows, HEADS, HEAD_DIM)
    )
    tnorm, token_norm_back = jax.vjp(layer_norm, tokens.astype(f32), gain_token)
    tnorm_low = tnorm.astype(bf16)
    keys = (
        jnp.dot(tnorm_low, w_key, preferred_element_type=f32)
        .astype(bf16)
        .reshape(token_rows, HEADS, HEAD_DIM)
    )
    values = (
        jnp.dot(tnorm_low, w_value, preferred_element_type=f32)
        .astype(bf16)
        .reshape(token_rows, HEADS, HEAD_DIM)
    )

    def sample_scores(query_one, valid_one):
        raw = jnp.einsum("lhd,thd->hlt", query_one, keys, preferred_element_type=f32)
        return jnp.where(valid_one[None, None, :], 0.125 * raw, -1e30)

    def sample_top(item):
        query_one, valid_one = item
        return jnp.max(sample_scores(query_one, valid_one), -1)

    def sample_sums(item):
        query_one, valid_one, top_one = item
        scores = sample_scores(query_one, valid_one)
        weight = jnp.where(valid_one[None, None, :], jnp.exp(scores - top_one[..., None]), 0.0)
        numer = jnp.einsum("hlt,thd->lhd", weight.astype(bf16), values, preferred_element_type=f32)
        return (numer, jnp.sum(weight, -1))

    local_top = lax.map(sample_top, (query, valid))
    top = lax.pmax(local_top, "tok")
    numer, denom = lax.map(sample_sums, (query, valid, top))
    numer, denom = lax.psum((numer, denom), "tok")
    denom_t = jnp.transpose(denom, (0, 2, 1))[..., None]
    attended = numer / denom_t
    attended_low = attended.astype(bf16).reshape(samples * lat_rows, width)
    branch = jnp.dot(attended_low, w_out, preferred_element_type=f32).reshape(
        samples, lat_rows, width
    )
    middle = lat_f + factor * branch
    hnorm, mlp_norm_back = jax.vjp(layer_norm, middle, gain_mlp)
    hnorm_low = hnorm.astype(bf16).reshape(samples * lat_rows, width)
    pre = jnp.dot(hnorm_low, w_up, preferred_element_type=f32) + b_up
    activated, gelu_back = jax.vjp(jax.nn.gelu, pre)
    hidden_low = activated.astype(bf16)
    mlp_out = (jnp.dot(hidden_low, w_down, preferred_element_type=f32) + b_down).reshape(
        samples, lat_rows, width
    )
    result = (middle + factor * mlp_out).astype(bf16)
    d_result = cotangent.astype(f32)
    d_mlp = (factor * d_result).astype(bf16).reshape(samples * lat_rows, width)
    grad_down = jnp.einsum("rf,rd->fd", hidden_low, d_mlp, preferred_element_type=f32)
    grad_bdown = jnp.sum(d_mlp.astype(f32), 0)
    d_hidden = jnp.einsum("rd,fd->rf", d_mlp, w_down, preferred_element_type=f32)
    d_pre = gelu_back(d_hidden)[0].astype(bf16)
    grad_up = jnp.einsum("rd,rf->df", hnorm_low, d_pre, preferred_element_type=f32)
    grad_bup = jnp.sum(d_pre.astype(f32), 0)
    d_hnorm = jnp.einsum("rf,df->rd", d_pre, w_up, preferred_element_type=f32).reshape(
        samples, lat_rows, width
    )
    d_middle_part, grad_gmlp = mlp_norm_back(d_hnorm)
    d_middle = d_result + d_middle_part
    d_branch = (factor * d_middle).astype(bf16).reshape(samples * lat_rows, width)
    grad_out = jnp.einsum("re,rd->ed", attended_low, d_branch, preferred_element_type=f32)
    d_att = (
        jnp.einsum("rd,ed->re", d_branch, w_out, preferred_element_type=f32)
        .astype(bf16)
        .reshape(samples, lat_rows, HEADS, HEAD_DIM)
    )
    d_att_f = d_att.astype(f32)
    d_numer = (d_att_f / denom_t).astype(bf16)
    delta = jnp.transpose(jnp.sum(d_att_f * attended, -1) / denom_t[..., 0], (0, 2, 1))

    def back_step(carry, item):
        value_acc, key_acc = carry
        query_one, valid_one, top_one, d_numer_one, delta_one = item
        scores = sample_scores(query_one, valid_one)
        weight = jnp.where(valid_one[None, None, :], jnp.exp(scores - top_one[..., None]), 0.0)
        d_prob = jnp.einsum("lhd,thd->hlt", d_numer_one, values, preferred_element_type=f32)
        raw_grad = (weight * (d_prob - delta_one[..., None])).astype(bf16)
        d_score = raw_grad * jnp.asarray(0.125, bf16)
        value_acc = value_acc + jnp.einsum(
            "hlt,lhd->thd", weight.astype(bf16), d_numer_one, preferred_element_type=f32
        )
        key_acc = key_acc + jnp.einsum(
            "hlt,lhd->thd", d_score, query_one, preferred_element_type=f32
        )
        d_query_one = jnp.einsum("hlt,thd->lhd", raw_grad, keys, preferred_element_type=f32)
        return ((value_acc, key_acc), d_query_one)

    empty = jnp.zeros((token_rows, HEADS, HEAD_DIM), f32)
    (value_sum, key_sum), d_query_part = lax.scan(
        back_step, (empty, empty), (query, valid, top, d_numer, delta)
    )
    d_value = value_sum.astype(bf16).reshape(token_rows, width)
    d_key = key_sum.astype(bf16).reshape(token_rows, width)
    d_query_part = d_query_part.reshape(samples, lat_rows, width)
    grad_key = jnp.einsum("td,te->de", tnorm_low, d_key, preferred_element_type=f32)
    grad_value = jnp.einsum("td,te->de", tnorm_low, d_value, preferred_element_type=f32)
    d_tnorm = jnp.einsum("te,de->td", d_key, w_key, preferred_element_type=f32) + jnp.einsum(
        "te,de->td", d_value, w_value, preferred_element_type=f32
    )
    d_tokens, grad_gtoken = token_norm_back(d_tnorm)
    d_query_sum = lax.psum(d_query_part, "tok")
    grad_key, grad_value, grad_gtoken = lax.psum(
        (grad_key, grad_value, grad_gtoken), ("stream", "tok")
    )
    d_query_low = (0.125 * d_query_sum).astype(bf16).reshape(samples * lat_rows, width)
    grad_query = jnp.einsum("rd,re->de", normed_low, d_query_low, preferred_element_type=f32)
    d_normed = jnp.einsum("re,de->rd", d_query_low, w_query, preferred_element_type=f32).reshape(
        samples, lat_rows, width
    )
    d_lat_part, grad_gquery = query_norm_back(d_normed)
    d_latents = d_middle + d_lat_part
    shares = (
        lax.psum_scatter(grad_query, "stream", scatter_dimension=1, tiled=True),
        lax.psum_scatter(grad_out, "stream", scatter_dimension=1, tiled=True),
        lax.psum_scatter(grad_up, "stream", scatter_dimension=1, tiled=True),
        lax.psum_scatter(grad_bup, "stream", scatter_dimension=0, tiled=True),
        lax.psum_scatter(grad_down, "stream", scatter_dimension=0, tiled=True),
        lax.psum_scatter(grad_bdown, "stream", scatter_dimension=0, tiled=True),
        lax.psum_scatter(grad_gquery, "stream", scatter_dimension=0, tiled=True),
        lax.psum_scatter(grad_gmlp, "stream", scatter_dimension=0, tiled=True),
    )
    return (
        result,
        d_latents,
        d_tokens,
        shares[6],
        shares[0],
        grad_gtoken,
        grad_key,
        grad_value,
        shares[1],
        shares[7],
        shares[2],
        shares[3],
        shares[4],
        shares[5],
    )


def solution(mesh):
    return jax.shard_map(
        local,
        mesh=mesh,
        in_specs=(
            P("stream", None, None),
            P(("stream", "tok"), None),
            P(("stream", "tok")),
            P(("stream", "tok")),
            P(),
            P(),
            P(),
            P(),
            P(),
            P(),
            P(),
            P(),
            P(),
            P(),
            P(),
            P(),
            P("stream", None, None),
        ),
        out_specs=(
            P("stream", None, None),
            P("stream", None, None),
            P(("stream", "tok"), None),
            P("stream"),
            P(None, "stream"),
            P(),
            P(),
            P(),
            P(None, "stream"),
            P("stream"),
            P(None, "stream"),
            P("stream"),
            P("stream", None),
            P("stream"),
        ),
        check_vma=False,
    )
```

profile of v0, /device:TPU:0, one launch (start us, length us, event | category | flops | bytes accessed | tf_op | source)
XLA Modules:
  0.0 986.5 jit_solution(6761116459866034333)
XLA Ops:
  26.2 16.8 %while.37 = (s32[]{:T(128)}, f32[8,12,128]{2,1,0:T(8,128)S(1)}, pred[8,1024]{1,0:T(8,128)(4,1)S(1)}, bf16[8,128,12,64]{1,3,2,0:T(8,128)(2,1)}, bf16[1024,12,64]{0,2,1:T(8,128)(2,1)S(1)}, /*index=5*/s32[]{:T(128)}) while((s32[]{:T(128)}, f32[8,12,128]{2,1,0:T(8,128)S(1)}, pred[8,1024]{1,0:T(8,128)(4,1)S(1)}, ...), condition=%wide.region_7.8_spmd, body=%wide.region_5.7_spmd.sunk | while | flops 206043648 | bytes 1795161 | solution.py:83
  43.0 30.9 %pmax.7 = f32[8,12,128]{2,1,0:T(8,128)S(1)} all-reduce(f32[8,12,128]{2,1,0:T(8,128)S(1)} %get-tuple-element.143), channel_id=1, replica_groups=mesh['stream'=4,'tok'=8] {'tok'}, use_global_device_ids=true, to_apply=%region_8.9 | all-reduce | flops 12288 | bytes 98304 | tf_op jit(solution)/shard_map/pmax | solution.py:84
  73.9 4.4 convolution_convert_fusion.1
  78.4 128.7 %while.38 = (s32[]{:T(128)}, f32[8,128,12,64]{1,0,3,2:T(8,128)}, f32[8,12,128]{2,0,1:T(8,128)S(1)}, pred[8,1024]{1,0:T(8,128)(4,1)S(1)}, bf16[8,128,12,64]{1,3,2...) while((s32[]{:T(128)}, f32[8,128,12,64]{1,0,3,2:T(8,128)}, ...), condition=%wide.region_11.12_spmd, body=%wide.region_9.11_spmd.sunk | while | flops 418380288 | bytes 23455900 | solution.py:85
  83.4 11.0 %dynamic_update_slice.22 = f32[8,128,12,64]{1,0,3,2:T(8,128)} dynamic-update-slice(f32[8,128,12,64]{1,0,3,2:T(8,128)} %get-tuple-element.563, f32[1,128,12,64]{1,0,3,2:T(1,128)S(1)} %bitcast.168, s32[]{:T(128)S(6)} %copy.121, s32[]{:T(128)} %constant.93.clone.1..sunk, s32[]{:T(128)} %constant.93.clone.1..sunk, s32[]{:T(128)} %constant.93.clone.1..sunk) | dynamic-update-slice | bytes 786436 | tf_op jit(solution)/shard_map/while/body/jit(dynamic_update_index_in_dim)/dynamic_update_slice | solution.py:85
  99.5 11.0 %dynamic_update_slice.22 = f32[8,128,12,64]{1,0,3,2:T(8,128)} dynamic-update-slice(f32[8,128,12,64]{1,0,3,2:T(8,128)} %get-tuple-element.563, f32[1,128,12,64]{1,0,3,2:T(1,128)S(1)} %bitcast.168, s32[]{:T(128)S(6)} %copy.121, s32[]{:T(128)} %constant.93.clone.1..sunk, s32[]{:T(128)} %constant.93.clone.1..sunk, s32[]{:T(128)} %constant.93.clone.1..sunk) | dynamic-update-slice | bytes 786436 | tf_op jit(solution)/shard_map/while/body/jit(dynamic_update_index_in_dim)/dynamic_update_slice | solution.py:85
  115.6 11.0 %dynamic_update_slice.22 = f32[8,128,12,64]{1,0,3,2:T(8,128)} dynamic-update-slice(f32[8,128,12,64]{1,0,3,2:T(8,128)} %get-tuple-element.563, f32[1,128,12,64]{1,0,3,2:T(1,128)S(1)} %bitcast.168, s32[]{:T(128)S(6)} %copy.121, s32[]{:T(128)} %constant.93.clone.1..sunk, s32[]{:T(128)} %constant.93.clone.1..sunk, s32[]{:T(128)} %constant.93.clone.1..sunk) | dynamic-update-slice | bytes 786436 | tf_op jit(solution)/shard_map/while/body/jit(dynamic_update_index_in_dim)/dynamic_update_slice | solution.py:85
  131.6 11.0 %dynamic_update_slice.22 = f32[8,128,12,64]{1,0,3,2:T(8,128)} dynamic-update-slice(f32[8,128,12,64]{1,0,3,2:T(8,128)} %get-tuple-element.563, f32[1,128,12,64]{1,0,3,2:T(1,128)S(1)} %bitcast.168, s32[]{:T(128)S(6)} %copy.121, s32[]{:T(128)} %constant.93.clone.1..sunk, s32[]{:T(128)} %constant.93.clone.1..sunk, s32[]{:T(128)} %constant.93.clone.1..sunk) | dynamic-update-slice | bytes 786436 | tf_op jit(solution)/shard_map/while/body/jit(dynamic_update_index_in_dim)/dynamic_update_slice | solution.py:85
  147.7 11.0 %dynamic_update_slice.22 = f32[8,128,12,64]{1,0,3,2:T(8,128)} dynamic-update-slice(f32[8,128,12,64]{1,0,3,2:T(8,128)} %get-tuple-element.563, f32[1,128,12,64]{1,0,3,2:T(1,128)S(1)} %bitcast.168, s32[]{:T(128)S(6)} %copy.121, s32[]{:T(128)} %constant.93.clone.1..sunk, s32[]{:T(128)} %constant.93.clone.1..sunk, s32[]{:T(128)} %constant.93.clone.1..sunk) | dynamic-update-slice | bytes 786436 | tf_op jit(solution)/shard_map/while/body/jit(dynamic_update_index_in_dim)/dynamic_update_slice | solution.py:85
  163.8 11.0 %dynamic_update_slice.22 = f32[8,128,12,64]{1,0,3,2:T(8,128)} dynamic-update-slice(f32[8,128,12,64]{1,0,3,2:T(8,128)} %get-tuple-element.563, f32[1,128,12,64]{1,0,3,2:T(1,128)S(1)} %bitcast.168, s32[]{:T(128)S(6)} %copy.121, s32[]{:T(128)} %constant.93.clone.1..sunk, s32[]{:T(128)} %constant.93.clone.1..sunk, s32[]{:T(128)} %constant.93.clone.1..sunk) | dynamic-update-slice | bytes 786436 | tf_op jit(solution)/shard_map/while/body/jit(dynamic_update_index_in_dim)/dynamic_update_slice | solution.py:85
  179.9 11.0 %dynamic_update_slice.22 = f32[8,128,12,64]{1,0,3,2:T(8,128)} dynamic-update-slice(f32[8,128,12,64]{1,0,3,2:T(8,128)} %get-tuple-element.563, f32[1,128,12,64]{1,0,3,2:T(1,128)S(1)} %bitcast.168, s32[]{:T(128)S(6)} %copy.121, s32[]{:T(128)} %constant.93.clone.1..sunk, s32[]{:T(128)} %constant.93.clone.1..sunk, s32[]{:T(128)} %constant.93.clone.1..sunk) | dynamic-update-slice | bytes 786436 | tf_op jit(solution)/shard_map/while/body/jit(dynamic_update_index_in_dim)/dynamic_update_slice | solution.py:85
  196.0 11.0 %dynamic_update_slice.22 = f32[8,128,12,64]{1,0,3,2:T(8,128)} dynamic-update-slice(f32[8,128,12,64]{1,0,3,2:T(8,128)} %get-tuple-element.563, f32[1,128,12,64]{1,0,3,2:T(1,128)S(1)} %bitcast.168, s32[]{:T(128)S(6)} %copy.121, s32[]{:T(128)} %constant.93.clone.1..sunk, s32[]{:T(128)} %constant.93.clone.1..sunk, s32[]{:T(128)} %constant.93.clone.1..sunk) | dynamic-update-slice | bytes 786436 | tf_op jit(solution)/shard_map/while/body/jit(dynamic_update_index_in_dim)/dynamic_update_slice | solution.py:85
  209.1 28.6 %psum.43 = f32[8,12,128]{2,0,1:T(8,128)S(1)} all-reduce(f32[8,12,128]{2,0,1:T(8,128)S(1)} %get-tuple-element.145), channel_id=1, replica_groups=mesh['stream'=4,'tok'=8] {'tok'}, use_global_device_ids=true, to_apply=%region_13.14 | all-reduce | flops 12288 | bytes 98304 | tf_op jit(solution)/shard_map/psum | solution.py:86
  241.3 42.2 %all-reduce.10.cloned.1.call-done = f32[8,128,12,64]{1,0,3,2:T(8,128)} async-done(((f32[8,128,12,64]{1,0,3,2:T(8,128)}), f32[8,128,12,64]{1,0,3,2:T(8,128)}) %all-reduce.10.cloned.1.call-update) | async-done | bytes 3145744 | tf_op jit(solution)/shard_map/psum | solution.py:86
  290.1 11.2 %multiply_convert_fusion.1 = (bf16[1024,3072]{1,0:T(8,128)(2,1)}, f32[1024,3072]{1,0:T(8,128)}) fusion(f32[3072]{0:T(1024)S(1)} %copy-done.46, bf16[1024,768]{1,0:T(8,128)(2,1)S(1)} %bitcast.180, bf16[768,3072]{1,0:T(8,128)(2,1)S(1)} %bitcast.190), kind=kOutput, calls=%fused_computation.67 | convolution fusion | flops 4863295488 | bytes 25178112 | tf_op jit(solution)/shard_map/dot_general | solution.py:96
  301.3 16.8 %convert_reduce_fusion = (f32[3072]{0:T(1024)}, bf16[1024,3072]{1,0:T(8,128)(2,1)}) fusion(f32[1024,3072]{1,0:T(8,128)} %get-tuple-element.372, f32[3072]{0:T(1024)S(1)} %copy-done.46, bf16[1024,768]{1,0:T(8,128)(2,1)S(1)} %bitcast.179, bf16[3072,768]{1,0:T(8,128)(2,1)S(1)} %bitcast.192), kind=kOutput, calls=%fused_computation.66 | convolution fusion | flops 4904186880 | bytes 25190400 | tf_op jit(solution)/shard_map/rd,fd->rf/dot_general | solution.py:107
  318.1 7.7 fusion.101
  328.6 5.0 convolution_add_fusion.1
  354.2 109.7 %while.39 = (s32[]{:T(128)}, f32[1024,12,64]{0,2,1:T(8,128)}, f32[1024,12,64]{0,2,1:T(8,128)}, f32[8,128,12,64]{1,3,2,0:T(8,128)}, bf16[8,128,12,64]{1,3,2,0:T(8...) while((s32[]{:T(128)}, f32[1024,12,64]{0,2,1:T(8,128)}, ...), condition=%wide.region_20.21_spmd.clone, body=%wide.region_19.20_spmd.clone.sunk | while | flops 1030225920 | bytes 103475520 | solution.py:145
  478.4 4.7 fusion.77
  483.4 61.0 %all-reduce.12.cloned.1.call-done = f32[8,128,768]{2,1,0:T(8,128)} async-done(((f32[8,128,768]{2,1,0:T(8,128)}), f32[8,128,768]{2,1,0:T(8,128)}) %all-reduce.12.cloned.1.call-update) | async-done | bytes 3145744 | tf_op jit(solution)/shard_map/psum | solution.py:157
  544.4 5.2 convolution_bitcast_fusion.1
  549.7 9.9 fusion.102
  559.6 9.9 %fusion.103 = f32[3072,768]{1,0:T(8,128)} fusion(bf16[1024,3072]{1,0:T(8,128)(2,1)} %get-tuple-element.371, bf16[1024,768]{1,0:T(8,128)(2,1)} %bitcast.178), kind=kOutput, calls=%fused_computation.158 | convolution fusion | flops 4831838208 | bytes 17301504 | tf_op jit(solution)/shard_map/rf,rd->fd/dot_general | solution.py:105
  584.7 40.3 %psum.45 = f32[768]{0:T(1024)} all-reduce(f32[768]{0:T(1024)S(1)} %get-tuple-element.299), channel_id=1, replica_groups=mesh['stream'=4,'tok'=8] {'stream','tok'}, use_global_device_ids=true, to_apply=%region_30.31 | all-reduce | flops 768 | bytes 6144 | tf_op jit(solution)/shard_map/psum | solution.py:158
  632.2 16.4 %all-reduce.5 = (f32[768]{0:T(1024)S(1)}, f32[768]{0:T(1024)S(1)}, f32[3072]{0:T(1024)S(1)}, f32[768]{0:T(1024)S(1)}) all-reduce(f32[768]{0:T(1024)S(1)} %get-tuple-element.301, f32[768]{0:T(1024)S(1)} %copy-done.42, f32[3072]{0:T(1024)S(1)} %copy-done.43, f32[768]{0:T(1024)S(1)} %copy-done.41), channel_id=2, replica_groups=mesh['stream'=4,'tok'=8] {'stream'}, use_global_device_ids=true, to_apply=%region_27.28.clone | all-reduce | flops 5376 | bytes 43008
  651.2 5.2 add_add_fusion.3
  656.4 39.3 %all-reduce.14.cloned.1.call-done = (f32[768,768]{1,0:T(8,128)}, f32[768,768]{1,0:T(8,128)}) async-done(((f32[768,768]{1,0:T(8,128)}, f32[768,768]{1,0:T(8,128)}), (f32[768,768]{1,0:T(8,128)}, f32[768,768]{1,0:T(8,128)})) %all-reduce.14.cloned.1.call-update) | async-done | bytes 4718608 | tf_op jit(solution)/shard_map/psum | solution.py:158
  695.7 40.0 %reduce-scatter.7.cloned.1.call-done = f32[768,192]{0,1:T(8,128)} async-done(((f32[768,768]{0,1:T(8,128)}), f32[768,192]{0,1:T(8,128)}) %reduce-scatter.7.cloned.1.call-update) | async-done | bytes 589840 | tf_op jit(solution)/shard_map/reduce_scatter | solution.py:170
  735.7 41.2 %reduce-scatter.5.cloned.1.call-done = f32[768,192]{0,1:T(8,128)} async-done(((f32[768,768]{0,1:T(8,128)}), f32[768,192]{0,1:T(8,128)}) %reduce-scatter.5.cloned.1.call-update) | async-done | bytes 589840 | tf_op jit(solution)/shard_map/reduce_scatter | solution.py:169
  776.8 98.8 %reduce-scatter.9.cloned.1.call-done = f32[768,768]{1,0:T(8,128)} async-done(((f32[768,3072]{1,0:T(8,128)}), f32[768,768]{1,0:T(8,128)}) %reduce-scatter.9.cloned.1.call-update) | async-done | bytes 2359312 | tf_op jit(solution)/shard_map/reduce_scatter | solution.py:171
  875.7 99.0 %reduce-scatter.11.cloned.1.call-done = f32[768,768]{1,0:T(8,128)} async-done(((f32[3072,768]{1,0:T(8,128)}), f32[768,768]{1,0:T(8,128)}) %reduce-scatter.11.cloned.1.call-update) | async-done | bytes 2359312 | tf_op jit(solution)/shard_map/reduce_scatter | solution.py:173
  (419 shorter events, 262.2 us)
Async XLA Ops:
  7.2 278.7 %copy-start = (bf16[768,768]{1,0:T(8,128)(2,1)S(1)}, bf16[768,768]{1,0:T(8,128)(2,1)}, u32[]{:S(2)}) copy-start(bf16[768,768]{1,0:T(8,128)(2,1)} %param.33) | copy-start | bytes 3538948
  7.2 4.8 copy-start.4
  7.2 4.8 copy-start.34
  7.2 276.3 %all-reduce.10.cloned.1.call-start = ((), (), s32[]{:S(2)}) async-start(), calls=%async_computation.4 | async-start | bytes 6291456 | tf_op jit(solution)/shard_map/psum | solution.py:86
  8.1 5.5 copy-start.45
  11.9 4.3 copy-start.36
  22.0 51.9 %copy-start.24 = (f32[1024]{0:T(1024)}, f32[1024]{0:T(1024)S(1)}, u32[]{:S(2)}) copy-start(f32[1024]{0:T(1024)S(1)} %broadcast_multiply_fusion) | copy-start | bytes 12292
  22.5 51.4 %copy-start.32 = (f32[1024]{0:T(1024)}, f32[1024]{0:T(1024)S(1)}, u32[]{:S(2)}) copy-start(f32[1024]{0:T(1024)S(1)} %fusion.89) | copy-start | bytes 12292
  207.1 337.3 %all-reduce.12.cloned.1.call-start = ((), (), s32[]{:S(2)}) async-start(), calls=%async_computation.5 | async-start | bytes 6291456 | tf_op jit(solution)/shard_map/psum | solution.py:157
  288.3 13.0 %slice-start.2 = ((s8[4718592]{0:T(1024)(128)(4,1)}), s8[4194304]{0:T(1024)(128)(4,1)S(1)}, s32[]{:S(2)}) async-start(s8[4718592]{0:T(1024)(128)(4,1)} %bitcast.191), calls=%async_computation.13 | async-start | bytes 8388608
  288.7 12.6 %copy-start.20 = (bf16[8,128,768]{2,1,0:T(8,128)(2,1)}, bf16[8,128,768]{2,1,0:T(8,128)(2,1)S(1)}, u32[]{:S(2)}) copy-start(bf16[8,128,768]{2,1,0:T(8,128)(2,1)S(1)} %multiply_convert_fusion.4) | copy-start | bytes 4718596
  290.1 11.2 %copy-start.19 = (bf16[8,128,768]{2,1,0:T(8,128)(2,1)S(1)}, bf16[8,128,768]{2,1,0:T(8,128)(2,1)}, u32[]{:S(2)}) copy-start(bf16[8,128,768]{2,1,0:T(8,128)(2,1)} %get-tuple-element.360) | copy-start | bytes 4718596
  290.1 11.2 %slice-start.3 = ((s8[4718592]{0:T(1024)(128)(4,1)}), s8[524288]{0:T(1024)(128)(4,1)S(1)}, s32[]{:S(2)}) async-start(s8[4718592]{0:T(1024)(128)(4,1)} %bitcast.191), calls=%async_computation.14 | async-start | bytes 1048576
  359.9 3.9 copy-start.15
  373.5 3.9 copy-start.15
  387.3 3.9 copy-start.15
  400.9 3.9 copy-start.15
  414.6 3.9 copy-start.15
  428.3 3.9 copy-start.15
  467.5 228.2 %all-reduce.14.cloned.1.call-start = ((), (), s32[]{:S(2)}) async-start(), calls=%async_computation.10 | async-start | bytes 9437184 | tf_op jit(solution)/shard_map/psum | solution.py:158
  469.8 5.6 copy-start.22
  470.6 4.8 copy-start.12
  478.3 257.3 %reduce-scatter.7.cloned.1.call-start = ((), (), s32[]{:S(2)}) async-start(), calls=%async_computation.7 | async-start | bytes 2949120 | tf_op jit(solution)/shard_map/reduce_scatter | solution.py:170
  483.1 293.7 %reduce-scatter.5.cloned.1.call-start = ((), (), s32[]{:S(2)}) async-start(), calls=%async_computation.6 | async-start | bytes 2949120 | tf_op jit(solution)/shard_map/reduce_scatter | solution.py:169
  549.6 326.0 %reduce-scatter.9.cloned.1.call-start = ((), (), s32[]{:S(2)}) async-start(), calls=%async_computation.8 | async-start | bytes 11796480 | tf_op jit(solution)/shard_map/reduce_scatter | solution.py:171
  559.6 415.1 %reduce-scatter.11.cloned.1.call-start = ((), (), s32[]{:S(2)}) async-start(), calls=%async_computation.9 | async-start | bytes 11796480 | tf_op jit(solution)/shard_map/reduce_scatter | solution.py:173
  581.0 44.0 %copy-start.6 = (bf16[8,128,768]{2,1,0:T(8,128)(2,1)S(1)}, bf16[8,128,768]{2,1,0:T(8,128)(2,1)}, u32[]{:S(2)}) copy-start(bf16[8,128,768]{2,1,0:T(8,128)(2,1)} %param.23) | copy-start | bytes 4718596
  581.0 44.0 %copy-start.27 = (f32[8,128]{1,0:T(8,128)S(1)}, f32[8,128]{1,0:T(8,128)}, u32[]{:S(2)}) copy-start(f32[8,128]{1,0:T(8,128)} %copy-done.26) | copy-start | bytes 12292
  581.0 44.0 %copy-start.35 = (f32[768]{0:T(1024)S(1)}, f32[768]{0:T(1024)}, u32[]{:S(2)}) copy-start(f32[768]{0:T(1024)} %param.28) | copy-start | bytes 9220
  625.0 5.6 copy-start.29
  695.7 282.3 %copy-start.17 = (f32[768,768]{1,0:T(8,128)S(1)}, f32[768,768]{1,0:T(8,128)}, u32[]{:S(2)}) copy-start(f32[768,768]{1,0:T(8,128)} %get-tuple-element.628) | copy-start | bytes 7077892
  974.7 4.7 copy-start.1
  (74 other events, 200.5 us)
Sparse Core Ops, SparseCore 0:
  207.2 76.2 all-reduce.9
  467.6 76.7 all-reduce.11
  550.8 144.8 all-reduce.13
  699.5 36.1 reduce-scatter.6
  739.4 37.3 reduce-scatter.4
  780.7 94.9 reduce-scatter.8
  879.6 95.0 reduce-scatter.10
where the time goes:
time: 995 us; the launch traced here: 987 us
  waiting for transfers between devices  422 us (42%)
  matrix products  264 us (27%)
  local copies, waits for them, and re-layouts  129 us (13%)
  blocking collectives  116 us (12%)
  other arithmetic  36.7 us (4%)
  between operations  17.2 us (2%)
    reduce_scatter x1, waiting for transfers between devices, local(): lax.psum_scatter(grad_down, 'stream', scatter_dimension=0, tiled=True)  99 us
    reduce_scatter x1, waiting for transfers between devices, local(): lax.psum_scatter(grad_up, 'stream', scatter_dimension=1, tiled=True)  98.8 us
    dynamic_update_slice x8, local copies, waits for them, and re-layouts, local(): numer, denom = lax.map(sample_sums, (query, valid, top))  87.7 us
    psum x1, waiting for transfers between devices, local(): d_query_sum = lax.psum(d_query_part, 'tok')  61 us
    dot_general x24, matrix products, sample_scores(): jnp.einsum('lhd,thd->hlt', query_one, keys, preferred_element_type=f32)  60.2 us
    psum x1, waiting for transfers between devices, local(): numer, denom = lax.psum((numer, denom), 'tok')  42.2 us
    reduce_scatter x1, waiting for transfers between devices, local(): lax.psum_scatter(grad_query, 'stream', scatter_dimension=1, tiled=True)  41.2 us
    psum x1, blocking collectives, local(): lax.psum((grad_key, grad_value, grad_gtoken), ('stream', 'tok'))  40.3 us
  transfers between devices with their start and end apart: 7, of which 7 were waited for; matrix products, arithmetic and copies ran while one was open for 7% of the time, Pallas kernels for 0%

commit v1 on v0

v1 whole, which is shorter than its diff:
```python
import functools

import jax
import jax.numpy as jnp
from jax import lax
from jax.experimental import pallas as pl
from jax.experimental.pallas import tpu as pltpu
from jax.sharding import PartitionSpec as P

HEADS = 12
HEAD_DIM = 64
PAIRS = HEADS // 2
PIECES = 4
PIECE_HEADS = HEADS // PIECES
NUM_ROWS = PIECE_HEADS * HEAD_DIM
PIECE_ROWS = NUM_ROWS + 8
BLOCK = 256
NEG = -1e30
F32 = jnp.float32
BF16 = jnp.bfloat16
VMEM_BYTES = 56 * 1024 * 1024


def norm_parts(values):
    center = values - jnp.mean(values, -1, keepdims=True)
    spread = jnp.mean(center * center, -1, keepdims=True)
    inv = lax.rsqrt(spread + 1e-05)
    return center * inv, inv


def norm_back(unit, inv, gain, grad):
    scaled = grad * gain
    inner = scaled - jnp.mean(scaled, -1, keepdims=True)
    return inv * (inner - unit * jnp.mean(scaled * unit, -1, keepdims=True))


def dot(a, b, contract=(1, 0)):
    return lax.dot_general(
        a, b, (((contract[0],), (contract[1],)), ((), ())), preferred_element_type=F32
    )


def piece_of(head):
    return head // PIECE_HEADS, head % PIECE_HEADS


def forward_kernel(
    ids_ref,
    tok_ref,
    lat_ref,
    gain_q_ref,
    wq_ref,
    gain_t_ref,
    wk_ref,
    wv_ref,
    part_ref,
    key_ref,
    val_ref,
    tsort_ref,
    query_ref,
    normed_ref,
    place_ref,
    bounds_ref,
    tnorm_ref,
    pos_ref,
    top_ref,
    den_ref,
    num_ref,
):
    samples = part_ref.shape[0]
    rows = tok_ref.shape[0]
    width = tok_ref.shape[1]
    lat_rows = 128
    step = 256

    ids = ids_ref[...]
    lane = lax.broadcasted_iota(jnp.int32, (samples, rows), 1)
    member = ids == lax.broadcasted_iota(jnp.int32, (samples, rows), 0)
    ones = jnp.where(member, 1.0, 0.0)
    count = ones
    shift = 1
    while shift < rows:
        count = count + jnp.where(lane >= shift, pltpu.roll(count, shift, 1), 0.0)
        shift *= 2
    rank = count - ones
    begin = jnp.int32(0)
    pos = jnp.full((1, rows), -1.0, F32)
    for s in range(samples):
        total = jnp.sum(ones[s : s + 1]).astype(jnp.int32)
        bounds_ref[s] = begin
        bounds_ref[samples + s] = total
        pos = jnp.where(member[s : s + 1], rank[s : s + 1] + begin.astype(F32), pos)
        begin = begin + total
    pos_ref[...] = jnp.broadcast_to(pos, (8, rows))
    place_ref[...] = jnp.broadcast_to(pos, (128, rows)).T

    def token_norm(i, carry):
        at = pl.ds(pl.multiple_of(i * step, step), step)
        unit, _ = norm_parts(tok_ref[at, :].astype(F32))
        tnorm_ref[at, :] = (unit * gain_t_ref[...]).astype(BF16)
        return carry

    lax.fori_loop(0, rows // step, token_norm, 0)

    def token_sort(i, carry):
        at = pl.ds(pl.multiple_of(i * step, step), step)
        target = lax.broadcasted_iota(jnp.int32, (step, rows), 0) + i * step
        chosen = target.astype(F32) == pos_ref[0:1, :]
        pick = jnp.where(chosen, 1.0, 0.0).astype(BF16)
        tsort = dot(pick, tnorm_ref[...]).astype(BF16)
        tsort_ref[at, :] = tsort
        key_ref[at, :] = dot(tsort, wk_ref[...]).astype(BF16)
        val_ref[at, :] = dot(tsort, wv_ref[...]).astype(BF16)
        return carry

    lax.fori_loop(0, rows // step, token_sort, 0)
    key_ref[rows:, :] = jnp.zeros((BLOCK, width), BF16)
    val_ref[rows:, :] = jnp.zeros((BLOCK, width), BF16)

    def sample_step(s, carry):
        at = pl.ds(pl.multiple_of(s * lat_rows, lat_rows), lat_rows)
        unit, _ = norm_parts(lat_ref[at, :].astype(F32))
        normed = (unit * gain_q_ref[...]).astype(BF16)
        normed_ref[at, :] = normed
        query = dot(normed, wq_ref[...]) * 0.125
        turned = query.T.astype(BF16)
        blank = jnp.zeros((HEAD_DIM, lat_rows), BF16)
        for p in range(PAIRS):
            lo = 2 * p * HEAD_DIM
            query_ref[s, p, :HEAD_DIM, :lat_rows] = turned[lo : lo + HEAD_DIM]
            query_ref[s, p, :HEAD_DIM, lat_rows:] = blank
            query_ref[s, p, HEAD_DIM:, :lat_rows] = blank
            query_ref[s, p, HEAD_DIM:, lat_rows:] = turned[lo + HEAD_DIM : lo + 2 * HEAD_DIM]
        start = bounds_ref[s]
        total = bounds_ref[samples + s]
        base = lax.div(start, 16) * 16
        blocks = jnp.where(total > 0, lax.div(start + total - base + BLOCK - 1, BLOCK), 0)
        num_ref[...] = jnp.zeros_like(num_ref)
        top_ref[...] = jnp.full_like(top_ref, NEG)
        den_ref[...] = jnp.zeros_like(den_ref)

        def block_step(b, carry):
            row = pl.multiple_of(base + b * BLOCK, 16)
            index = lax.broadcasted_iota(jnp.int32, (BLOCK, 2 * lat_rows), 0) + row
            inside = (index >= start) & (index < start + total)
            for p in range(PAIRS):
                cols = slice(p * 128, (p + 1) * 128)
                score = dot(key_ref[pl.ds(row, BLOCK), cols], query_ref[s, p])
                score = jnp.where(inside, score, NEG)
                old = top_ref[p : p + 1, :]
                new = jnp.maximum(old, jnp.max(score, 0, keepdims=True))
                fade = jnp.exp(old - new)
                weight = jnp.exp(score - new)
                top_ref[p : p + 1, :] = new
                den_ref[p : p + 1, :] = den_ref[p : p + 1, :] * fade + jnp.sum(
                    weight, 0, keepdims=True
                )
                both = dot(val_ref[pl.ds(row, BLOCK), cols], weight.astype(BF16), (0, 0))
                for half in range(2):
                    at_rows = slice(p * 128 + half * HEAD_DIM, p * 128 + (half + 1) * HEAD_DIM)
                    at_cols = slice(half * lat_rows, (half + 1) * lat_rows)
                    num_ref[at_rows, :] = (
                        num_ref[at_rows, :] * fade[:, at_cols]
                        + both[half * HEAD_DIM : (half + 1) * HEAD_DIM, at_cols]
                    )
            return carry

        lax.fori_loop(0, blocks, block_step, 0)
        for h in range(HEADS):
            piece, i = piece_of(h)
            p, half = h // 2, h % 2
            at_cols = slice(half * lat_rows, (half + 1) * lat_rows)
            part_ref[s, piece, i * HEAD_DIM : (i + 1) * HEAD_DIM, :] = num_ref[
                h * HEAD_DIM : (h + 1) * HEAD_DIM, :
            ]
            part_ref[s, piece, NUM_ROWS + i : NUM_ROWS + i + 1, :] = top_ref[p : p + 1, at_cols]
            part_ref[
                s, piece, NUM_ROWS + PIECE_HEADS + i : NUM_ROWS + PIECE_HEADS + i + 1, :
            ] = den_ref[p : p + 1, at_cols]
        for piece in range(PIECES):
            part_ref[s, piece, NUM_ROWS + 2 * PIECE_HEADS :, :] = jnp.zeros(
                (8 - 2 * PIECE_HEADS, lat_rows), F32
            )
        return carry

    lax.fori_loop(0, samples, sample_step, 0)


def vmem():
    return pl.BlockSpec(memory_space=pltpu.VMEM)


def smem():
    return pl.BlockSpec(memory_space=pltpu.SMEM)


def attend_forward(ids, tokens, latents, gain_q, wq, gain_t, wk, wv):
    samples, lat_rows, width = latents.shape
    rows = tokens.shape[0]
    sds = jax.ShapeDtypeStruct
    return pl.pallas_call(
        forward_kernel,
        name="attend_forward",
        out_shape=(
            sds((samples, PIECES, PIECE_ROWS, lat_rows), F32),
            sds((rows + BLOCK, width), BF16),
            sds((rows + BLOCK, width), BF16),
            sds((rows, width), BF16),
            sds((samples, PAIRS, 128, 2 * lat_rows), BF16),
            sds((samples * lat_rows, width), BF16),
            sds((rows, 128), F32),
            sds((2 * samples,), jnp.int32),
        ),
        in_specs=[vmem()] * 8,
        out_specs=(vmem(),) * 7 + (smem(),),
        scratch_shapes=[
            pltpu.VMEM((rows, width), BF16),
            pltpu.VMEM((8, rows), F32),
            pltpu.VMEM((8, 2 * lat_rows), F32),
            pltpu.VMEM((8, 2 * lat_rows), F32),
            pltpu.VMEM((width, lat_rows), F32),
        ],
        compiler_params=pltpu.CompilerParams(vmem_limit_bytes=VMEM_BYTES),
    )(
        ids.reshape(1, rows),
        tokens,
        latents.reshape(samples * lat_rows, width),
        gain_q.reshape(1, width),
        wq,
        gain_t.reshape(1, width),
        wk,
        wv,
    )


def backward_kernel(
    bounds_ref,
    lat_ref,
    key_ref,
    val_ref,
    query_ref,
    normed_ref,
    dnum_ref,
    stat_ref,
    gain_q_ref,
    wq_ref,
    dkey_ref,
    dval_ref,
    dlat_ref,
    dgain_ref,
    dwq_ref,
    dk_ref,
    dv_ref,
    grad_ref,
    dquery_ref,
    turn_ref,
):
    samples = query_ref.shape[0]
    rows = dkey_ref.shape[0]
    lat_rows = 128
    step = 256
    for r in range(0, rows + BLOCK, step):
        dk_ref[r : r + step, :] = jnp.zeros((step, dk_ref.shape[1]), F32)
        dv_ref[r : r + step, :] = jnp.zeros((step, dv_ref.shape[1]), F32)
    grad_ref[...] = jnp.zeros_like(grad_ref)
    dgain_ref[...] = jnp.zeros_like(dgain_ref)

    def sample_step(s, carry):
        start = bounds_ref[s]
        total = bounds_ref[samples + s]
        base = lax.div(start, 16) * 16
        blocks = jnp.where(total > 0, lax.div(start + total - base + BLOCK - 1, BLOCK), 0)
        turn_ref[...] = jnp.zeros_like(turn_ref)
        for h in range(HEADS):
            p, half = h // 2, h % 2
            grad_ref[
                p,
                half * HEAD_DIM : (half + 1) * HEAD_DIM,
                half * lat_rows : (half + 1) * lat_rows,
            ] = dnum_ref[s, h * HEAD_DIM : (h + 1) * HEAD_DIM, :].astype(BF16)

        def block_step(b, carry):
            row = pl.multiple_of(base + b * BLOCK, 16)
            index = lax.broadcasted_iota(jnp.int32, (BLOCK, 2 * lat_rows), 0) + row
            inside = (index >= start) & (index < start + total)
            at = pl.ds(row, BLOCK)
            for p in range(PAIRS):
                cols = slice(p * 128, (p + 1) * 128)
                key = key_ref[at, cols]
                query = query_ref[s, p]
                grad = grad_ref[p]
                score = dot(key, query)
                weight = jnp.where(inside, jnp.exp(score - stat_ref[s, p : p + 1, :]), 0.0)
                dprob = dot(val_ref[at, cols], grad)
                dscore = (weight * (dprob - stat_ref[s, 8 + p : 9 + p, :])).astype(BF16)
                dv_ref[at, cols] += dot(weight.astype(BF16), grad, (1, 1))
                dk_ref[at, cols] += dot(dscore, query, (1, 1))
                both = dot(key, dscore, (0, 0))
                for half in range(2):
                    turn_ref[
                        p * 128 + half * HEAD_DIM : p * 128 + (half + 1) * HEAD_DIM, :
                    ] += both[
                        half * HEAD_DIM : (half + 1) * HEAD_DIM,
                        half * lat_rows : (half + 1) * lat_rows,
                    ]
            return carry

        lax.fori_loop(0, blocks, block_step, 0)
        at = pl.ds(pl.multiple_of(s * lat_rows, lat_rows), lat_rows)
        dquery = (turn_ref[...].T * 0.125).astype(BF16)
        dquery_ref[at, :] = dquery
        unit, inv = norm_parts(lat_ref[at, :].astype(F32))
        dnormed = dot(dquery, wq_ref[...], (1, 1))
        dgain_ref[0:1, :] += jnp.sum(dnormed * unit, 0, keepdims=True)
        dlat_ref[at, :] = norm_back(unit, inv, gain_q_ref[...], dnormed)
        return carry

    lax.fori_loop(0, samples, sample_step, 0)
    for r in range(0, rows, step):
        dkey_ref[r : r + step, :] = dk_ref[r : r + step, :].astype(BF16)
        dval_ref[r : r + step, :] = dv_ref[r : r + step, :].astype(BF16)
    width = dwq_ref.shape[0]
    for c in range(0, width, 256):
        dwq_ref[c : c + 256, :] = dot(normed_ref[:, c : c + 256], dquery_ref[...], (0, 0))


def attend_backward(bounds, latents, keys, values, query, normed, dnum, stat, gain_q, wq):
    samples, lat_rows, width = latents.shape
    rows = keys.shape[0] - BLOCK
    sds = jax.ShapeDtypeStruct
    return pl.pallas_call(
        backward_kernel,
        name="attend_backward",
        out_shape=(
            sds((rows, width), BF16),
            sds((rows, width), BF16),
            sds((samples * lat_rows, width), F32),
            sds((8, width), F32),
            sds((width, width), F32),
        ),
        in_specs=[smem()] + [vmem()] * 9,
        out_specs=(vmem(),) * 5,
        scratch_shapes=[
            pltpu.VMEM((rows + BLOCK, width), F32),
            pltpu.VMEM((rows + BLOCK, width), F32),
            pltpu.VMEM((PAIRS, 128, 2 * lat_rows), BF16),
            pltpu.VMEM((samples * lat_rows, width), BF16),
            pltpu.VMEM((width, lat_rows), F32),
        ],
        compiler_params=pltpu.CompilerParams(vmem_limit_bytes=VMEM_BYTES),
    )(
        bounds,
        latents.reshape(samples * lat_rows, width),
        keys,
        values,
        query,
        normed,
        dnum,
        stat,
        gain_q.reshape(1, width),
        wq,
    )


def token_kernel(
    place_ref,
    tok_ref,
    tsort_ref,
    dkey_ref,
    dval_ref,
    gain_t_ref,
    wk_ref,
    wv_ref,
    dtok_ref,
    dgain_ref,
    dwk_ref,
    dwv_ref,
):
    rows = tok_ref.shape[0]
    width = tok_ref.shape[1]
    step = 256
    for c in range(0, width, 256):
        dwk_ref[c : c + 256, :] = dot(tsort_ref[:, c : c + 256], dkey_ref[...], (0, 0))
        dwv_ref[c : c + 256, :] = dot(tsort_ref[:, c : c + 256], dval_ref[...], (0, 0))
    dgain_ref[...] = jnp.zeros_like(dgain_ref)

    def token_step(i, carry):
        at = pl.ds(pl.multiple_of(i * step, step), step)
        target = lax.broadcasted_iota(jnp.int32, (step, rows), 1).astype(F32)
        chosen = target == place_ref[at, 0:1]
        pick = jnp.where(chosen, 1.0, 0.0).astype(BF16)
        dkey = dot(pick, dkey_ref[...]).astype(BF16)
        dval = dot(pick, dval_ref[...]).astype(BF16)
        dnormed = dot(dkey, wk_ref[...], (1, 1)) + dot(dval, wv_ref[...], (1, 1))
        unit, inv = norm_parts(tok_ref[at, :].astype(F32))
        dgain_ref[0:1, :] += jnp.sum(dnormed * unit, 0, keepdims=True)
        dtok_ref[at, :] = norm_back(unit, inv, gain_t_ref[...], dnormed)
        return carry

    lax.fori_loop(0, rows // step, token_step, 0)


def token_backward(place, tokens, tsort, dkey, dval, gain_t, wk, wv):
    rows, width = tokens.shape
    sds = jax.ShapeDtypeStruct
    return pl.pallas_call(
        token_kernel,
        name="token_backward",
        out_shape=(
            sds((rows, width), F32),
            sds((8, width), F32),
            sds((width, width), F32),
            sds((width, width), F32),
        ),
        in_specs=[vmem()] * 8,
        out_specs=(vmem(),) * 4,
        compiler_params=pltpu.CompilerParams(vmem_limit_bytes=VMEM_BYTES),
    )(place, tokens, tsort, dkey, dval, gain_t.reshape(1, width), wk, wv)


def layer_norm(values, gain):
    center = values - jnp.mean(values, -1, keepdims=True)
    spread = jnp.mean(center * center, -1, keepdims=True)
    return center * lax.rsqrt(spread + 1e-05) * gain


def local(
    latents,
    tokens,
    token_sample,
    token_mask,
    drop_mask,
    gain_query,
    w_query,
    gain_token,
    w_key,
    w_value,
    w_out,
    gain_mlp,
    w_up,
    b_up,
    w_down,
    b_down,
    cotangent,
):
    samples, lat_rows, width = latents.shape
    group_index = lax.axis_index("stream")
    tok_index = lax.axis_index("tok")
    streams = lax.axis_size("stream")
    members = lax.axis_size("tok")
    samples_all = drop_mask.shape[0]
    scale_all = drop_mask.astype(F32) * samples_all / jnp.sum(drop_mask).astype(F32)
    factor = lax.dynamic_slice_in_dim(scale_all, group_index * samples, samples)[:, None, None]
    ids = jnp.where(token_mask == 1, token_sample - group_index * samples, -1)
    part, keys, values, tsort, query, normed, place, bounds = attend_forward(
        ids, tokens, latents, gain_query, w_query, gain_token, w_key, w_value
    )
    top_part = part[:, :, NUM_ROWS : NUM_ROWS + PIECE_HEADS]
    den_part = part[:, :, NUM_ROWS + PIECE_HEADS : NUM_ROWS + 2 * PIECE_HEADS]
    num_part = part[:, :, :NUM_ROWS].reshape(samples, PIECES, PIECE_HEADS, HEAD_DIM, lat_rows)
    top = lax.pmax(top_part, "tok")
    fade = jnp.exp(top_part - top)
    numer, denom = lax.psum((num_part * fade[:, :, :, None], den_part * fade), "tok")
    att_t = (numer / denom[:, :, :, None]).reshape(samples, width, lat_rows)
    attended = jnp.transpose(att_t, (0, 2, 1))
    attended_low = attended.astype(BF16).reshape(samples * lat_rows, width)
    lat_f = latents.astype(F32)
    branch = jnp.dot(attended_low, w_out, preferred_element_type=F32).reshape(
        samples, lat_rows, width
    )
    middle = lat_f + factor * branch
    hnorm, mlp_norm_back = jax.vjp(layer_norm, middle, gain_mlp)
    hnorm_low = hnorm.astype(BF16).reshape(samples * lat_rows, width)
    pre = jnp.dot(hnorm_low, w_up, preferred_element_type=F32) + b_up
    activated, gelu_back = jax.vjp(jax.nn.gelu, pre)
    hidden_low = activated.astype(BF16)
    mlp_out = (jnp.dot(hidden_low, w_down, preferred_element_type=F32) + b_down).reshape(
        samples, lat_rows, width
    )
    result = (middle + factor * mlp_out).astype(BF16)
    d_result = cotangent.astype(F32)
    d_mlp = (factor * d_result).astype(BF16).reshape(samples * lat_rows, width)
    grad_bdown = jnp.sum(d_mlp.astype(F32), 0)
    d_hidden = jnp.einsum("rd,fd->rf", d_mlp, w_down, preferred_element_type=F32)
    d_pre = gelu_back(d_hidden)[0].astype(BF16)
    grad_bup = jnp.sum(d_pre.astype(F32), 0)
    d_hnorm = jnp.einsum("rf,df->rd", d_pre, w_up, preferred_element_type=F32).reshape(
        samples, lat_rows, width
    )
    d_middle_part, grad_gmlp = mlp_norm_back(d_hnorm)
    d_middle = d_result + d_middle_part
    d_branch = (factor * d_middle).astype(BF16).reshape(samples * lat_rows, width)
    d_att = jnp.einsum("ed,brd->ber", w_out, d_branch.reshape(samples, lat_rows, width),
                       preferred_element_type=F32).astype(BF16).astype(F32)
    d_att = d_att.reshape(samples, HEADS, HEAD_DIM, lat_rows)
    den_h = denom.reshape(samples, HEADS, lat_rows)
    top_h = top.reshape(samples, HEADS, lat_rows)
    dnum = (d_att / den_h[:, :, None]).reshape(samples, width, lat_rows)
    delta = jnp.sum(d_att * att_t.reshape(d_att.shape), 2) / den_h
    blank = jnp.zeros((samples, 8 - PAIRS, 2 * lat_rows), F32)
    stat = jnp.concatenate(
        (
            top_h.reshape(samples, PAIRS, 2 * lat_rows),
            blank,
            delta.reshape(samples, PAIRS, 2 * lat_rows),
            blank,
        ),
        1,
    )

    shares = 8
    share = lax.rem(tok_index, shares)
    depth = width // shares
    hid_dim = w_up.shape[1]
    mine = lambda x: lax.dynamic_slice_in_dim(x, share * depth, depth, 1)
    grad_up = jnp.einsum("rd,rf->df", mine(hnorm_low), d_pre, preferred_element_type=F32)
    grad_down = jnp.einsum("rf,rd->df", hidden_low, mine(d_mlp), preferred_element_type=F32)
    grad_out = jnp.einsum("re,rd->ed", mine(attended_low), d_branch, preferred_element_type=F32)
    both = jnp.concatenate((grad_up, grad_down), 0)
    both = lax.psum_scatter(both, "stream", scatter_dimension=1, tiled=True)
    grad_out = lax.psum_scatter(grad_out, "stream", scatter_dimension=1, tiled=True)
    groups = [list(range(g, g + shares)) for g in range(0, members, shares)]
    both = lax.all_gather(both, "tok", axis_index_groups=groups)
    grad_up = both[:, :depth].reshape(width, -1)
    grad_down = both[:, depth:].reshape(width, -1).T
    grad_out = lax.all_gather(grad_out, "tok", axis_index_groups=groups, tiled=True)

    dkey, dval, dlat, dgain_q, grad_query = attend_backward(
        bounds, latents, keys, values, query, normed, dnum, stat, gain_query, w_query
    )
    d_tokens, dgain_t, grad_key, grad_value = token_backward(
        place, tokens, tsort, dkey, dval, gain_token, w_key, w_value
    )
    d_latents = d_middle + lax.psum(dlat, "tok").reshape(d_middle.shape)
    grad_key, grad_value, grad_query, grad_gtoken, grad_gquery = lax.psum(
        (grad_key, grad_value, grad_query, dgain_t[0], dgain_q[0]), ("stream", "tok")
    )
    grad_bup, grad_bdown, grad_gmlp = lax.psum((grad_bup, grad_bdown, grad_gmlp), "stream")

    def own(x, axis):
        size = x.shape[axis] // streams
        return lax.dynamic_slice_in_dim(x, group_index * size, size, axis)

    return (
        result,
        d_latents,
        d_tokens,
        own(grad_gquery, 0),
        own(grad_query, 1),
        grad_gtoken,
        grad_key,
        grad_value,
        grad_out,
        own(grad_gmlp, 0),
        grad_up,
        own(grad_bup, 0),
        grad_down,
        own(grad_bdown, 0),
    )


def solution(mesh):
    return jax.shard_map(
        local,
        mesh=mesh,
        in_specs=(
            P("stream", None, None),
            P(("stream", "tok"), None),
            P(("stream", "tok")),
            P(("stream", "tok")),
            P(),
            P(),
            P(),
            P(),
            P(),
            P(),
            P(),
            P(),
            P(),
            P(),
            P(),
            P(),
            P("stream", None, None),
        ),
        out_specs=(
            P("stream", None, None),
            P("stream", None, None),
            P(("stream", "tok"), None),
            P("stream"),
            P(None, "stream"),
            P(),
            P(),
            P(),
            P(None, "stream"),
            P("stream"),
            P(None, "stream"),
            P("stream"),
            P("stream", None),
            P("stream"),
        ),
        check_vma=False,
    )
```

time: 995 us -> 597 us (0.60)
  matrix products: 264 us -> 58.1 us
  waiting for transfers between devices: 422 us -> 248 us
  local copies, waits for them, and re-layouts: 129 us -> 34.7 us
  Pallas kernels: 0 us -> 74.1 us
  blocking collectives: 116 us -> 128 us
    reduce_scatter x4 -> x1, waiting for transfers between devices: 279 us -> 0.02 us  [local(): both = lax.psum_scatter(both, 'stream', scatter_dimension=1, tiled=True)]
    dot_general x82 -> x8, matrix products: 264 us -> 55.4 us  [the longest x1 17.2 us: local(): jnp.einsum('rd,fd->rf', d_mlp, w_down, preferred_element_type=F32)]
    dynamic_update_slice x32 -> x0, local copies, waits for them, and re-layouts: 88.2 us -> none  [the longest x8 87.7 us: local(): numer, denom = lax.map(sample_sums, (query, valid, top))]
    pallas_call x0 -> x3, Pallas kernels: none -> 74.1 us  [the longest x1 31.5 us: attend_forward(): pl.pallas_call(forward_kernel, name='attend_forward', out_shape=(sds((sam...]
    psum x3, waiting for transfers between devices: 142 us -> 197 us  [the longest x1 154 us: local(): lax.psum((grad_key, grad_value, grad_query, dgain_t[0], dgain_q[0]), ('st...]
    all_gather x0 -> x1, waiting for transfers between devices: none -> 50.8 us  [local(): both = lax.all_gather(both, 'tok', axis_index_groups=groups)]
    psum x2 -> x3, blocking collectives: 68.9 us -> 85.4 us  [the longest x1 40.5 us: local(): lax.psum((grad_key, grad_value, grad_query, dgain_t[0], dgain_q[0]), ('st...]
    unnamed x1 -> x0, blocking collectives: 16.4 us -> none
  transfers between devices with their start and end apart: 7 -> 6, of which waited for: 7 -> 3; matrix products, arithmetic and copies ran while one was open for 7% -> 9% of each run, Pallas kernels for 0% -> 7%
where the time goes in v1:
time: 597 us; the launch traced here: 591 us
  waiting for transfers between devices  248 us (42%)
  blocking collectives  128 us (21%)
  Pallas kernels  74.1 us (12%)
  matrix products  58.1 us (10%)
  local copies, waits for them, and re-layouts  34.7 us (6%)
  other arithmetic  31.7 us (5%)
  between operations  15.4 us (3%)
    psum x1, waiting for transfers between devices, local(): lax.psum((grad_key, grad_value, grad_query, dgain_t[0], dgain_q[0]), ('st...  154 us
    all_gather x1, waiting for transfers between devices, local(): both = lax.all_gather(both, 'tok', axis_index_groups=groups)  50.8 us
    psum x1, waiting for transfers between devices, local(): lax.psum((num_part * fade[:, :, :, None], den_part * fade), 'tok')  42.9 us
    psum x1, blocking collectives, local(): lax.psum((grad_key, grad_value, grad_query, dgain_t[0], dgain_q[0]), ('st...  40.5 us
    pallas_call x1, Pallas kernels, attend_forward(): pl.pallas_call(forward_kernel, name='attend_forward', out_shape=(sds((sam...  31.5 us
    psum x1, blocking collectives, local(): lax.psum((num_part * fade[:, :, :, None], den_part * fade), 'tok')  29.5 us
    pmax x1, blocking collectives, local(): top = lax.pmax(top_part, 'tok')  27.1 us
    pallas_call x1, Pallas kernels, attend_backward(): pl.pallas_call(backward_kernel, name='attend_backward', out_shape=(sds((r...  25.5 us
  transfers between devices with their start and end apart: 6, of which 3 were waited for; matrix products, arithmetic and copies ran while one was open for 9% of the time, Pallas kernels for 7%

profile of v1, /device:TPU:0, one launch (start us, length us, event | category | flops | bytes accessed | tf_op | source)
XLA Modules:
  0.0 590.9 jit_solution(3005388316964453754)
XLA Ops:
  11.2 31.5 %attend_forward.1 = (f32[8,4,200,128]{3,2,1,0:T(8,128)}, bf16[1280,768]{1,0:T(8,128)(2,1)}, bf16[1280,768]{1,0:T(8,128)(2,1)}, bf16[1024,768]{1,0:T(8,128)(2,1)}...) custom-call(s32[1,1024]{1,0:T(1,128)} %bitcast.80, ...), custom_call_target="tpu_custom_call" | custom-call | tf_op jit(solution)/shard_map/attend_forward/pallas_call | solution.py:201
  43.6 3.9 slice.21
  47.5 27.1 %pmax.7 = f32[8,4,3,128]{3,2,1,0:T(4,128)S(1)} all-reduce(f32[8,4,3,128]{3,2,1,0:T(4,128)S(1)} %slice.22), channel_id=1, replica_groups=mesh['stream'=4,'tok'=8] {'tok'}, use_global_device_ids=true, to_apply=%region_1.2 | all-reduce | flops 12288 | bytes 98304 | tf_op jit(solution)/shard_map/pmax | solution.py:461
  75.6 4.3 broadcast_multiply_fusion
  82.0 29.5 %psum.78 = f32[8,4,3,128]{3,2,1,0:T(4,128)S(1)} all-reduce(f32[8,4,3,128]{3,2,1,0:T(4,128)S(1)} %get-tuple-element.132), channel_id=1, replica_groups=mesh['stream'=4,'tok'=8] {'tok'}, use_global_device_ids=true, to_apply=%region_3.4 | all-reduce | flops 12288 | bytes 98304 | tf_op jit(solution)/shard_map/psum | solution.py:463
  111.5 1.7 convert_reduce_fusion.1
  113.2 42.9 %all-reduce.7.cloned.1.call-done = f32[8,4,3,64,128]{4,3,2,1,0:T(8,128)} async-done(((f32[8,4,3,64,128]{4,3,2,1,0:T(8,128)}), f32[8,4,3,64,128]{4,3,2,1,0:T(8,128)}) %all-reduce.7.cloned.1.call-update) | async-done | bytes 3145744 | tf_op jit(solution)/shard_map/psum | solution.py:463
  156.1 4.9 fusion.22
  161.0 2.8 copy.84
  163.8 3.3 fusion.24
  168.7 10.2 %multiply_convert_fusion = (bf16[1024,3072]{1,0:T(8,128)(2,1)S(1)}, f32[1024,3072]{1,0:T(8,128)}) fusion(f32[3072]{0:T(1024)S(1)} %copy-done.13, bf16[1024,768]{1,0:T(8,128)(2,1)S(1)} %bitcast.73, bf16[768,3072]{1,0:T(8,128)(2,1)S(1)} %bitcast.82), kind=kOutput, calls=%fused_computation.10 | convolution fusion | flops 4863295488 | bytes 25178112 | tf_op jit(solution)/shard_map/dot_general | solution.py:474
  179.0 17.2 %convert_reduce_fusion = (f32[3072]{0:T(1024)S(1)}, bf16[1024,3072]{1,0:T(8,128)(2,1)S(1)}) fusion(f32[1024,3072]{1,0:T(8,128)} %get-tuple-element.141, f32[3072]{0:T(1024)S(1)} %copy-done.13, bf16[1024,768]{1,0:T(8,128)(2,1)S(1)} %bitcast.71, bf16[3072,768]{1,0:T(8,128)(2,1)} %param.31), kind=kOutput, calls=%fused_computation.9 | convolution fusion | flops 4904186880 | bytes 25190400 | tf_op jit(solution)/shard_map/rd,fd->rf/dot_general | solution.py:484
  200.1 1.6 pad_maximum_fusion
  201.9 8.7 %fusion.25 = f32[1024,768]{1,0:T(8,128)S(1)} fusion(bf16[1024,3072]{1,0:T(8,128)(2,1)} %copy-done.9, bf16[768,3072]{1,0:T(8,128)(2,1)} %param.29), kind=kOutput, calls=%fused_computation.59 | convolution fusion | flops 4831838208 | bytes 14155776 | tf_op jit(solution)/shard_map/rf,df->rd/dot_general | solution.py:487
  211.9 8.7 %convolution_add_fusion = f32[1024,768]{1,0:T(8,128)S(1)} fusion(bf16[1024,3072]{1,0:T(8,128)(2,1)} %copy-done.8, bf16[3072,768]{1,0:T(8,128)(2,1)} %param.31, f32[768]{0:T(1024)S(1)} %copy-done.14), kind=kOutput, calls=%fused_computation.27 | convolution fusion | flops 4832624640 | bytes 14158848 | tf_op jit(solution)/shard_map/dot_general | solution.py:477
  220.7 2.8 add_add_fusion
  223.5 2.3 reduce_sum.99
  225.9 2.4 multiply_convert_fusion.1
  229.4 2.6 convolution_bitcast_fusion
  232.5 4.7 bitcast_divide_fusion
  238.9 25.5 %attend_backward.1 = (bf16[1024,768]{1,0:T(8,128)(2,1)}, bf16[1024,768]{1,0:T(8,128)(2,1)}, f32[1024,768]{1,0:T(8,128)}, f32[8,768]{1,0:T(8,128)}, f32[768,768]{1,0:T(8,128)}) custom-call(s32[16]{0:T(128)} %get-tuple-element.32.bounds_ref, bf16[1024,768]{1,0:T(8,128)(2,1)} %bitcast.58, bf16[1280,768]{1,0:T(8,128)(2,1)} %get-tuple-element.33.key_ref, ...), custom_call_target="tpu_custom_call" | custom-call | tf_op jit(solution)/shard_map/attend_backward/pallas_call | solution.py:331
  264.4 17.2 %token_backward.1 = (f32[1024,768]{1,0:T(8,128)}, f32[8,768]{1,0:T(8,128)}, f32[768,768]{1,0:T(8,128)}, f32[768,768]{1,0:T(8,128)}) custom-call(f32[1024,128]{1,0:T(8,128)} %get-tuple-element.38.place_ref, bf16[1024,768]{1,0:T(8,128)(2,1)} %tok_ref.3, bf16[1024,768]{1,0:T(8,128)(2,1)} %get-tuple-element.39.tsort_ref, ...), custom_call_target="tpu_custom_call" | custom-call | tf_op jit(solution)/shard_map/token_backward/pallas_call | solution.py:406
  282.2 15.4 %all-reduce.2 = (f32[768]{0:T(1024)S(1)}, f32[3072]{0:T(1024)S(1)}, f32[768]{0:T(1024)S(1)}) all-reduce(f32[768]{0:T(1024)S(1)} %get-tuple-element.118, f32[3072]{0:T(1024)S(1)} %get-tuple-element.144, f32[768]{0:T(1024)S(1)} %get-tuple-element.128), channel_id=1, replica_groups=mesh['stream'=4,'tok'=8] {'stream'}, use_global_device_ids=true, to_apply=%region_17.18 | all-reduce | flops 4608 | bytes 36864 | tf_op jit(solution)/shard_map/psum | solution.py:538
  300.4 40.5 %all-reduce = (f32[768]{0:T(1024)S(1)}, f32[768]{0:T(1024)}) all-reduce(f32[768]{0:T(1024)S(1)} %slice_reduce_fusion.1, f32[768]{0:T(1024)S(1)} %slice_reduce_fusion), channel_id=1, replica_groups=mesh['stream'=4,'tok'=8] {'stream','tok'}, use_global_device_ids=true, to_apply=%region_10.11 | all-reduce | flops 1536 | bytes 12288 | tf_op jit(solution)/shard_map/psum | solution.py:535
  342.2 1.6 copy.91
  343.8 15.9 %all_gather.9 = f32[768,192]{1,0:T(8,128)S(1)} all-gather(f32[96,192]{1,0:T(8,128)} %copy.91), channel_id=1, replica_groups={{0,1,2,3,4,5,6,7},{8,9,10,11,12,13,14,15},{16,17,18,19,20,21,22,23},{24..., dimensions={0}, use_global_device_ids=true | all-gather | bytes 663552 | tf_op jit(solution)/shard_map/all_gather | solution.py:526
  360.7 5.1 fusion.8
  365.8 153.7 %all-reduce.11.cloned.1.call-done = (f32[768,768]{1,0:T(8,128)}, f32[768,768]{1,0:T(8,128)}, f32[768,768]{1,0:T(8,128)}) async-done(((f32[768,768]{1,0:T(8,128)}, f32[768,768]{1,0:T(8,128)}, f32[768,768]{1,0:T(8,128)}), (f32[768,768]{1,0:T(8,128)}, f32[768,768]{1,0:T(8,128)}, f32[768,768]{1,0:T(8,128)})) %all-reduce.11.cloned.1.call-update) | async-done | bytes 7077904 | tf_op jit(solution)/shard_map/psum | solution.py:535
  522.1 50.8 %all-gather.3.cloned.1.call-done = f32[1536,768]{1,0:T(8,128)} async-done(((f32[192,768]{1,0:T(8,128)}), f32[1536,768]{1,0:T(8,128)}) %all-gather.3.cloned.1.call-update) | async-done | bytes 4718608 | tf_op jit(solution)/shard_map/all_gather | solution.py:523
  572.9 4.2 fusion.23
  577.1 1.9 copy.87
  579.0 3.4 copy.97
  (89 shorter events, 27.3 us)
Async XLA Ops:
  7.2 156.6 %copy-start = (bf16[768,768]{1,0:T(8,128)(2,1)S(1)}, bf16[768,768]{1,0:T(8,128)(2,1)}, u32[]{:S(2)}) copy-start(bf16[768,768]{1,0:T(8,128)(2,1)} %param.27) | copy-start | bytes 3538948
  7.2 148.9 %all-reduce.7.cloned.1.call-start = ((), (), s32[]{:S(2)}) async-start(), calls=%async_computation.2 | async-start | bytes 6291456 | tf_op jit(solution)/shard_map/psum | solution.py:463
  79.9 0.7 copy-start.15
  79.9 31.6 %copy-start.4 = (bf16[8,128,768]{2,1,0:T(8,128)(2,1)S(1)}, bf16[8,128,768]{2,1,0:T(8,128)(2,1)}, u32[]{:S(2)}) copy-start(bf16[8,128,768]{2,1,0:T(8,128)(2,1)} %param.33) | copy-start | bytes 4718596
  79.9 201.8 %reduce-scatter.5.cloned.1.call-start = ((), (), s32[]{:S(2)}) async-start(), calls=%async_computation.4 | async-start | bytes 2949120 | tf_op jit(solution)/shard_map/reduce_scatter | solution.py:520
  161.0 2.8 copy-start.3
  163.7 5.0 slice-start
  167.0 1.7 copy-start.1
  167.0 0.7 copy-start.12
  167.0 1.7 slice-start.1
  167.6 1.2 copy-start.13
  168.7 10.3 %copy-start.11 = (bf16[8,128,768]{2,1,0:T(8,128)(2,1)S(1)}, bf16[8,128,768]{2,1,0:T(8,128)(2,1)}, u32[]{:S(2)}) copy-start(bf16[8,128,768]{2,1,0:T(8,128)(2,1)} %get-tuple-element.129) | copy-start | bytes 4718596
  179.0 19.9 %copy-start.8 = (bf16[1024,3072]{1,0:T(8,128)(2,1)}, bf16[1024,3072]{1,0:T(8,128)(2,1)S(1)}, u32[]{:S(2)}) copy-start(bf16[1024,3072]{1,0:T(8,128)(2,1)S(1)} %get-tuple-element.140) | copy-start | bytes 18874372
  196.2 2.7 copy-start.9
  201.7 140.5 %reduce-scatter.7.cloned.1.call-start = ((), (), s32[]{:S(2)}) async-start(), calls=%async_computation.6 | async-start | bytes 491520
  201.9 8.8 %copy-start.2 = (f32[8,128,768]{2,1,0:T(8,128)S(1)}, f32[8,128,768]{2,1,0:T(8,128)}, u32[]{:S(2)}) copy-start(f32[8,128,768]{2,1,0:T(8,128)} %copy-done.1) | copy-start | bytes 9437188
  210.7 1.2 copy-start.14
  223.5 2.4 copy-start.5
  228.3 1.1 copy-start.6
  232.1 128.6 %all-reduce.9.cloned.1.call-start = ((), (), s32[]{:S(2)}) async-start(), calls=%async_computation.3 | async-start | bytes 6291456 | tf_op jit(solution)/shard_map/psum | solution.py:534
  232.5 4.7 copy-start.7
  264.4 255.1 %all-reduce.11.cloned.1.call-start = ((), (), s32[]{:S(2)}) async-start(), calls=%async_computation.7 | async-start | bytes 14155776 | tf_op jit(solution)/shard_map/psum | solution.py:535
  281.7 291.2 %all-gather.3.cloned.1.call-start = ((), (), s32[]{:S(2)}) async-start(), calls=%async_computation.5 | async-start | bytes 5308416 | tf_op jit(solution)/shard_map/all_gather | solution.py:523
  579.0 3.4 copy-start.10
Sparse Core Ops, SparseCore 0:
  80.1 75.9 all-reduce.6
  201.8 37.2 reduce-scatter.4
  242.5 24.4 reduce-scatter.6
  269.8 77.8 all-reduce.8
  354.8 164.6 all-reduce.10
  521.1 51.7 all-gather.2

commit v2 on v1

--- a/solution.py
+++ b/solution.py
@@ -13,7 +13,8 @@
 PIECES = 4
 PIECE_HEADS = HEADS // PIECES
 NUM_ROWS = PIECE_HEADS * HEAD_DIM
-PIECE_ROWS = NUM_ROWS + 8
+PIECE_ROWS = NUM_ROWS + 16
+MSG_ROWS = HEADS * HEAD_DIM + 32
 BLOCK = 256
 NEG = -1e30
 F32 = jnp.float32
@@ -135,6 +136,8 @@
         total = bounds_ref[samples + s]
         base = lax.div(start, 16) * 16
         blocks = jnp.where(total > 0, lax.div(start + total - base + BLOCK - 1, BLOCK), 0)
+        for piece in range(PIECES):
+            part_ref[s, piece, NUM_ROWS:, :] = jnp.zeros((16, lat_rows), F32)
         num_ref[...] = jnp.zeros_like(num_ref)
         top_ref[...] = jnp.full_like(top_ref, NEG)
         den_ref[...] = jnp.zeros_like(den_ref)
@@ -174,13 +177,9 @@
                 h * HEAD_DIM : (h + 1) * HEAD_DIM, :
             ]
             part_ref[s, piece, NUM_ROWS + i : NUM_ROWS + i + 1, :] = top_ref[p : p + 1, at_cols]
-            part_ref[
-                s, piece, NUM_ROWS + PIECE_HEADS + i : NUM_ROWS + PIECE_HEADS + i + 1, :
-            ] = den_ref[p : p + 1, at_cols]
-        for piece in range(PIECES):
-            part_ref[s, piece, NUM_ROWS + 2 * PIECE_HEADS :, :] = jnp.zeros(
-                (8 - 2 * PIECE_HEADS, lat_rows), F32
-            )
+            part_ref[s, piece, NUM_ROWS + 8 + i : NUM_ROWS + 9 + i, :] = den_ref[
+                p : p + 1, at_cols
+            ]
         return carry
 
     lax.fori_loop(0, samples, sample_step, 0)
@@ -240,8 +239,7 @@
     val_ref,
     query_ref,
     normed_ref,
-    dnum_ref,
-    stat_ref,
+    msg_ref,
     gain_q_ref,
     wq_ref,
     dkey_ref,
@@ -254,11 +252,13 @@
     grad_ref,
     dquery_ref,
     turn_ref,
+    stat_ref,
 ):
     samples = query_ref.shape[0]
     rows = dkey_ref.shape[0]
     lat_rows = 128
     step = 256
+    width = dwq_ref.shape[0]
     for r in range(0, rows + BLOCK, step):
         dk_ref[r : r + step, :] = jnp.zeros((step, dk_ref.shape[1]), F32)
         dv_ref[r : r + step, :] = jnp.zeros((step, dv_ref.shape[1]), F32)
@@ -277,7 +277,14 @@
                 p,
                 half * HEAD_DIM : (half + 1) * HEAD_DIM,
                 half * lat_rows : (half + 1) * lat_rows,
-            ] = dnum_ref[s, h * HEAD_DIM : (h + 1) * HEAD_DIM, :].astype(BF16)
+            ] = msg_ref[s, h * HEAD_DIM : (h + 1) * HEAD_DIM, :].astype(BF16)
+
+            stat_ref[p : p + 1, half * lat_rows : (half + 1) * lat_rows] = msg_ref[
+                s, width + h : width + h + 1, :
+            ]
+            stat_ref[8 + p : 9 + p, half * lat_rows : (half + 1) * lat_rows] = msg_ref[
+                s, width + 16 + h : width + 17 + h, :
+            ]
 
         def block_step(b, carry):
             row = pl.multiple_of(base + b * BLOCK, 16)
@@ -290,9 +297,9 @@
                 query = query_ref[s, p]
                 grad = grad_ref[p]
                 score = dot(key, query)
-                weight = jnp.where(inside, jnp.exp(score - stat_ref[s, p : p + 1, :]), 0.0)
+                weight = jnp.where(inside, jnp.exp(score - stat_ref[p : p + 1, :]), 0.0)
                 dprob = dot(val_ref[at, cols], grad)
-                dscore = (weight * (dprob - stat_ref[s, 8 + p : 9 + p, :])).astype(BF16)
+                dscore = (weight * (dprob - stat_ref[8 + p : 9 + p, :])).astype(BF16)
                 dv_ref[at, cols] += dot(weight.astype(BF16), grad, (1, 1))
                 dk_ref[at, cols] += dot(dscore, query, (1, 1))
                 both = dot(key, dscore, (0, 0))
@@ -319,12 +326,11 @@
     for r in range(0, rows, step):
         dkey_ref[r : r + step, :] = dk_ref[r : r + step, :].astype(BF16)
         dval_ref[r : r + step, :] = dv_ref[r : r + step, :].astype(BF16)
-    width = dwq_ref.shape[0]
     for c in range(0, width, 256):
         dwq_ref[c : c + 256, :] = dot(normed_ref[:, c : c + 256], dquery_ref[...], (0, 0))
 
 
-def attend_backward(bounds, latents, keys, values, query, normed, dnum, stat, gain_q, wq):
+def attend_backward(bounds, latents, keys, values, query, normed, msg, gain_q, wq):
     samples, lat_rows, width = latents.shape
     rows = keys.shape[0] - BLOCK
     sds = jax.ShapeDtypeStruct
@@ -338,7 +344,7 @@
             sds((8, width), F32),
             sds((width, width), F32),
         ),
-        in_specs=[smem()] + [vmem()] * 9,
+        in_specs=[smem()] + [vmem()] * 8,
         out_specs=(vmem(),) * 5,
         scratch_shapes=[
             pltpu.VMEM((rows + BLOCK, width), F32),
@@ -346,6 +352,7 @@
             pltpu.VMEM((PAIRS, 128, 2 * lat_rows), BF16),
             pltpu.VMEM((samples * lat_rows, width), BF16),
             pltpu.VMEM((width, lat_rows), F32),
+            pltpu.VMEM((16, 2 * lat_rows), F32),
         ],
         compiler_params=pltpu.CompilerParams(vmem_limit_bytes=VMEM_BYTES),
     )(
@@ -355,8 +362,7 @@
         values,
         query,
         normed,
-        dnum,
-        stat,
+        msg,
         gain_q.reshape(1, width),
         wq,
     )
@@ -418,10 +424,438 @@
     )(place, tokens, tsort, dkey, dval, gain_t.reshape(1, width), wk, wv)
 
 
-def layer_norm(values, gain):
-    center = values - jnp.mean(values, -1, keepdims=True)
-    spread = jnp.mean(center * center, -1, keepdims=True)
-    return center * lax.rsqrt(spread + 1e-05) * gain
+MESH = pl.DeviceIdType.MESH
+
+
+def merge(a_ref, b_ref, out_ref):
+    a_tail, b_tail = a_ref[NUM_ROWS : NUM_ROWS + 8, :], b_ref[NUM_ROWS : NUM_ROWS + 8, :]
+    top = jnp.maximum(a_tail, b_tail)
+    a_fade, b_fade = jnp.exp(a_tail - top), jnp.exp(b_tail - top)
+    den = a_ref[NUM_ROWS + 8 :, :] * a_fade + b_ref[NUM_ROWS + 8 :, :] * b_fade
+    for i in range(PIECE_HEADS):
+        at = slice(i * HEAD_DIM, (i + 1) * HEAD_DIM)
+        out_ref[at, :] = (
+            a_ref[at, :] * a_fade[i : i + 1, :] + b_ref[at, :] * b_fade[i : i + 1, :]
+        )
+    out_ref[NUM_ROWS : NUM_ROWS + 8, :] = top
+    out_ref[NUM_ROWS + 8 :, :] = den
+
+
+def gelu_parts(x):
+    c = 0.7978845608028654
+    square = x * x
+    t = jnp.tanh(c * x * (1.0 + 0.044715 * square))
+    half = 0.5 * (1.0 + t)
+    slope = half + (0.5 * c) * x * (1.0 - t * t) * (1.0 + (3 * 0.044715) * square)
+    return x * half, slope
+
+
+def latent_kernel(
+    part_ref,
+    drop_ref,
+    lat_ref,
+    cot_ref,
+    wo_hbm,
+    gain_ref,
+    wup_hbm,
+    bup_ref,
+    wdn_hbm,
+    bdn_ref,
+    msg_ref,
+    res_ref,
+    dmid_ref,
+    a_ref,
+    b_ref,
+    att_ref,
+    vec_ref,
+    wo_ref,
+    wup_ref,
+    wdn_ref,
+    pair_ref,
+    own_ref,
+    right_in,
+    right_out,
+    left_in,
+    left_out,
+    res_out,
+    res_in,
+    att_t_ref,
+    mid_ref,
+    acc_ref,
+    dacc_ref,
+    weight_sem,
+    pair_send,
+    pair_recv,
+    right_send,
+    right_recv,
+    left_send,
+    left_recv,
+    msg_send,
+    msg_recv,
+    res_send,
+    res_recv,
+):
+    samples = part_ref.shape[0]
+    half = samples // 2
+    lat_rows = 128
+    width = lat_ref.shape[1]
+    chunks = half * PIECES
+    stream = lax.axis_index("stream")
+    tok = lax.axis_index("tok")
+    chips = lax.axis_size("tok") // 2
+    core = lax.rem(tok, 2)
+    chip = lax.div(tok, 2)
+    partner = (stream, tok + 1 - 2 * core)
+    right = (stream, tok + 2)
+    left = (stream, tok - 2)
+    has_right = chip < chips - 1
+    has_left = chip > 0
+
+    barrier = pltpu.get_barrier_semaphore()
+    pl.semaphore_signal(barrier, inc=1, device_id=partner, device_id_type=MESH)
+
+    @pl.when(has_right)
+    def _():
+        pl.semaphore_signal(barrier, inc=1, device_id=right, device_id_type=MESH)
+
+    @pl.when(has_left)
+    def _():
+        pl.semaphore_signal(barrier, inc=1, device_id=left, device_id_type=MESH)
+
+    weights = [
+        pltpu.make_async_copy(src, dst, weight_sem.at[i])
+        for i, (src, dst) in enumerate(((wo_hbm, wo_ref), (wup_hbm, wup_ref), (wdn_hbm, wdn_ref)))
+    ]
+    for copy in weights:
+        copy.start()
+    pl.semaphore_wait(
+        barrier, 1 + has_right.astype(jnp.int32) + has_left.astype(jnp.int32)
+    )
+
+    def pair_copy(i):
+        j, q = lax.div(i, PIECES), lax.rem(i, PIECES)
+        return pltpu.make_async_remote_copy(
+            src_ref=part_ref.at[(1 - core) * half + j, q],
+            dst_ref=pair_ref.at[i],
+            send_sem=pair_send.at[i],
+            recv_sem=pair_recv.at[i],
+            device_id=partner,
+            device_id_type=MESH,
+        )
+
+    def right_copy(i):
+        return pltpu.make_async_remote_copy(
+            src_ref=right_out.at[i],
+            dst_ref=right_in.at[i],
+            send_sem=right_send.at[i],
+            recv_sem=right_recv.at[i],
+            device_id=right,
+            device_id_type=MESH,
+        )
+
+    def left_copy(i):
+        return pltpu.make_async_remote_copy(
+            src_ref=left_out.at[i],
+            dst_ref=left_in.at[i],
+            send_sem=left_send.at[i],
+            recv_sem=left_recv.at[i],
+            device_id=left,
+            device_id_type=MESH,
+        )
+
+    def msg_copy(j):
+        at = core * half + j
+        return pltpu.make_async_remote_copy(
+            src_ref=msg_ref.at[at],
+            dst_ref=msg_ref.at[at],
+            send_sem=msg_send.at[j],
+            recv_sem=msg_recv.at[j],
+            device_id=partner,
+            device_id_type=MESH,
+        )
+
+    def msg_arrival(j):
+        at = (1 - core) * half + j
+        return pltpu.make_async_remote_copy(
+            src_ref=msg_ref.at[at],
+            dst_ref=msg_ref.at[at],
+            send_sem=msg_send.at[j],
+            recv_sem=msg_recv.at[j],
+            device_id=partner,
+            device_id_type=MESH,
+        )
+
+    def res_copy(j):
+        return pltpu.make_async_remote_copy(
+            src_ref=res_out.at[j],
+            dst_ref=res_in.at[j],
+            send_sem=res_send.at[j],
+            recv_sem=res_recv.at[j],
+            device_id=partner,
+            device_id_type=MESH,
+        )
+
+    def start_pair(i, carry):
+        pair_copy(i).start()
+        return carry
+
+    lax.fori_loop(0, chunks, start_pair, 0)
+
+    drop = drop_ref[...].astype(F32)
+    scale_all = drop * drop.shape[1] / jnp.sum(drop, 1, keepdims=True)
+    drop_lane = lax.broadcasted_iota(jnp.int32, drop.shape, 1)
+    vec_ref[...] = jnp.zeros_like(vec_ref)
+
+    def mlp(j, q):
+        sample = core * half + j
+        rows = pl.ds(pl.multiple_of(sample * lat_rows, lat_rows), lat_rows)
+        mine = pl.ds(pl.multiple_of(j * lat_rows, lat_rows), lat_rows)
+        scale = jnp.sum(
+            jnp.where(drop_lane == stream * samples + sample, scale_all, 0.0), 1, keepdims=True
+        )
+
+        @pl.when(q == 0)
+        def _():
+            for h in range(HEADS):
+                piece, i = piece_of(h)
+                at = j * PIECES + piece
+                den = own_ref[at, NUM_ROWS + 8 + i : NUM_ROWS + 9 + i, :]
+                att_t_ref[h * HEAD_DIM : (h + 1) * HEAD_DIM, :] = own_ref[
+                    at, i * HEAD_DIM : (i + 1) * HEAD_DIM, :
+                ] * (1.0 / den)
+            att = att_t_ref[...].T.astype(BF16)
+            att_ref[mine, :] = att
+            mid = lat_ref[rows, :].astype(F32) + scale * dot(att, wo_ref[...])
+            mid_ref[...] = mid
+            unit, _ = norm_parts(mid)
+            a_ref[0, mine, :] = (unit * gain_ref[...]).astype(BF16)
+            dm = (scale * cot_ref[rows, :].astype(F32)).astype(BF16)
+            a_ref[1, mine, :] = dm
+            vec_ref[1:2, :width] += jnp.sum(dm.astype(F32), 0, keepdims=True)
+            acc_ref[...] = jnp.broadcast_to(bdn_ref[...], acc_ref.shape)
+            dacc_ref[...] = jnp.zeros_like(dacc_ref)
+
+        span = wup_ref.shape[1] // PIECES
+        cols = pl.ds(pl.multiple_of(q * span, 128), span)
+        pre = dot(a_ref[0, mine, :], wup_ref[:, cols]) + bup_ref[:, cols]
+        active, slope = gelu_parts(pre)
+        hidden = active.astype(BF16)
+        b_ref[1, mine, cols] = hidden
+        acc_ref[...] += dot(hidden, wdn_ref[cols, :])
+        dpre = (slope * dot(a_ref[1, mine, :], wdn_ref[cols, :], (1, 1))).astype(BF16)
+        b_ref[0, mine, cols] = dpre
+        vec_ref[0:1, cols] += jnp.sum(dpre.astype(F32), 0, keepdims=True)
+        dacc_ref[...] += dot(dpre, wup_ref[:, cols], (1, 1))
+
+        @pl.when(q == PIECES - 1)
+        def _():
+            mid = mid_ref[...]
+            res = (mid + scale * acc_ref[...]).astype(BF16)
+            res_ref[rows, :] = res
+            res_out[j] = res.astype(F32)
+            res_copy(j).start()
+            unit, inv = norm_parts(mid)
+            dhn = dacc_ref[...]
+            vec_ref[2:3, :width] += jnp.sum(dhn * unit, 0, keepdims=True)
+            dmid = cot_ref[rows, :].astype(F32) + norm_back(unit, inv, gain_ref[...], dhn)
+            dmid_ref[mine, :] = dmid
+            da = (scale * dmid).astype(BF16)
+            a_ref[2, mine, :] = da
+            datt_t = dot(wo_ref[...], da, (1, 1)).astype(BF16).astype(F32)
+            msg_ref[sample, width:, :] = jnp.zeros((MSG_ROWS - width, lat_rows), F32)
+            for h in range(HEADS):
+                piece, i = piece_of(h)
+                at = j * PIECES + piece
+                inverse = 1.0 / own_ref[at, NUM_ROWS + 8 + i : NUM_ROWS + 9 + i, :]
+                span_h = slice(h * HEAD_DIM, (h + 1) * HEAD_DIM)
+                one = datt_t[span_h]
+                msg_ref[sample, span_h, :] = (one * inverse).astype(BF16).astype(F32)
+                delta = jnp.sum(one * att_t_ref[span_h, :], 0, keepdims=True) * inverse
+                msg_ref[sample, width + h : width + h + 1, :] = own_ref[
+                    at, NUM_ROWS + i : NUM_ROWS + i + 1, :
+                ]
+                msg_ref[sample, width + 16 + h : width + 17 + h, :] = delta
+            msg_copy(j).start()
+
+    def step(t, carry):
+        @pl.when(t < chunks)
+        def _():
+            pair_copy(t).wait_recv()
+            j, q = lax.div(t, PIECES), lax.rem(t, PIECES)
+            merge(part_ref.at[core * half + j, q], pair_ref.at[t], own_ref.at[t])
+
+        r = t - chip
+
+        @pl.when((r >= 0) & (r < chunks))
+        def _():
+            @pl.when(has_left)
+            def _():
+                right_copy(r).wait_recv()
+                merge(own_ref.at[r], right_in.at[r], right_out.at[r])
+
+            @pl.when(jnp.logical_not(has_left))
+            def _():
+                right_out[r] = own_ref[r]
+
+            @pl.when(has_right)
+            def _():
+                right_copy(r).start()
+
+        u = t - (chips - 1 - chip)
+
+        @pl.when((u >= 0) & (u < chunks))
+        def _():
+            @pl.when(has_right)
+            def _():
+                left_copy(u).wait_recv()
+
+            @pl.when(has_left)
+            def _():
+                @pl.when(has_right)
+                def _():
+                    merge(own_ref.at[u], left_in.at[u], left_out.at[u])
+
+                @pl.when(jnp.logical_not(has_right))
+                def _():
+                    left_out[u] = own_ref[u]
+
+                left_copy(u).start()
+
+        w = t - (chips - 1)
+
+        @pl.when((w >= 0) & (w < chunks))
+        def _():
+            @pl.when(has_right)
+            def _():
+                merge(right_out.at[w], left_in.at[w], own_ref.at[w])
+
+            @pl.when(jnp.logical_not(has_right))
+            def _():
+                own_ref[w] = right_out[w]
+
+        m = w - (PIECES - 1)
+
+        @pl.when(m == 0)
+        def _():
+            for copy in weights:
+                copy.wait()
+
+        @pl.when(m >= 0)
+        def _():
+            mlp(lax.div(m, PIECES), lax.rem(m, PIECES))
+
+        return carry
+
+    lax.fori_loop(0, chunks + chips - 1 + PIECES - 1, step, 0)
+
+    def finish_chunk(i, carry):
+        pair_copy(i).wait_send()
+
+        @pl.when(has_right)
+        def _():
+            right_copy(i).wait_send()
+
+        @pl.when(has_left)
+        def _():
+            left_copy(i).wait_send()
+
+        return carry
+
+    lax.fori_loop(0, chunks, finish_chunk, 0)
+
+    def finish_sample(j, carry):
+        res_copy(j).wait_recv()
+        other = (1 - core) * half + j
+        rows = pl.ds(pl.multiple_of(other * lat_rows, lat_rows), lat_rows)
+        res_ref[rows, :] = res_in[j].astype(BF16)
+        res_copy(j).wait_send()
+        msg_copy(j).wait_send()
+        msg_arrival(j).wait_recv()
+        return carry
+
+    lax.fori_loop(0, half, finish_sample, 0)
+
+
+def anywhere():
+    return pl.BlockSpec(memory_space=pl.ANY)
+
+
+def latent_block(part, drop_mask, latents, cotangent, wo, gain, wup, bup, wdn, bdn):
+    samples, lat_rows, width = latents.shape
+    half = samples // 2
+    chunks = half * PIECES
+    hidden = wup.shape[1]
+    sds = jax.ShapeDtypeStruct
+    chunk = lambda: pltpu.VMEM((chunks, PIECE_ROWS, lat_rows), F32)
+    dma = pltpu.SemaphoreType.DMA
+    return pl.pallas_call(
+        latent_kernel,
+        name="latent_block",
+        out_shape=(
+            sds((samples, MSG_ROWS, lat_rows), F32),
+            sds((samples * lat_rows, width), BF16),
+            sds((half * lat_rows, width), F32),
+            sds((3, half * lat_rows, width), BF16),
+            sds((2, half * lat_rows, hidden), BF16),
+            sds((half * lat_rows, width), BF16),
+            sds((8, hidden), F32),
+        ),
+        in_specs=[
+            vmem(),
+            vmem(),
+            vmem(),
+            vmem(),
+            anywhere(),
+            vmem(),
+            anywhere(),
+            vmem(),
+            anywhere(),
+            vmem(),
+        ],
+        out_specs=(vmem(),) * 7,
+        scratch_shapes=[
+            pltpu.VMEM(wo.shape, BF16),
+            pltpu.VMEM(wup.shape, BF16),
+            pltpu.VMEM(wdn.shape, BF16),
+            chunk(),
+            chunk(),
+            chunk(),
+            chunk(),
+            chunk(),
+            chunk(),
+            pltpu.VMEM((half, lat_rows, width), F32),
+            pltpu.VMEM((half, lat_rows, width), F32),
+            pltpu.VMEM((width, lat_rows), F32),
+            pltpu.VMEM((lat_rows, width), F32),
+            pltpu.VMEM((lat_rows, width), F32),
+            pltpu.VMEM((lat_rows, width), F32),
+            dma((3,)),
+            dma((chunks,)),
+            dma((chunks,)),
+            dma((chunks,)),
+            dma((chunks,)),
+            dma((chunks,)),
+            dma((chunks,)),
+            dma((half,)),
+            dma((half,)),
+            dma((half,)),
+            dma((half,)),
+        ],
+        compiler_params=pltpu.CompilerParams(
+            vmem_limit_bytes=VMEM_BYTES, collective_id=1, has_side_effects=True
+        ),
+    )(
+        part,
+        drop_mask.reshape(1, -1),
+        latents.reshape(samples * lat_rows, width),
+        cotangent.reshape(samples * lat_rows, width),
+        wo,
+        gain.reshape(1, width),
+        wup,
+        bup.reshape(1, hidden),
+        wdn,
+        bdn.reshape(1, width),
+    )
 
 
 def local(
@@ -448,90 +882,47 @@
     tok_index = lax.axis_index("tok")
     streams = lax.axis_size("stream")
     members = lax.axis_size("tok")
-    samples_all = drop_mask.shape[0]
-    scale_all = drop_mask.astype(F32) * samples_all / jnp.sum(drop_mask).astype(F32)
-    factor = lax.dynamic_slice_in_dim(scale_all, group_index * samples, samples)[:, None, None]
     ids = jnp.where(token_mask == 1, token_sample - group_index * samples, -1)
     part, keys, values, tsort, query, normed, place, bounds = attend_forward(
         ids, tokens, latents, gain_query, w_query, gain_token, w_key, w_value
     )
-    top_part = part[:, :, NUM_ROWS : NUM_ROWS + PIECE_HEADS]
-    den_part = part[:, :, NUM_ROWS + PIECE_HEADS : NUM_ROWS + 2 * PIECE_HEADS]
-    num_part = part[:, :, :NUM_ROWS].reshape(samples, PIECES, PIECE_HEADS, HEAD_DIM, lat_rows)
-    top = lax.pmax(top_part, "tok")
-    fade = jnp.exp(top_part - top)
-    numer, denom = lax.psum((num_part * fade[:, :, :, None], den_part * fade), "tok")
-    att_t = (numer / denom[:, :, :, None]).reshape(samples, width, lat_rows)
-    attended = jnp.transpose(att_t, (0, 2, 1))
-    attended_low = attended.astype(BF16).reshape(samples * lat_rows, width)
-    lat_f = latents.astype(F32)
-    branch = jnp.dot(attended_low, w_out, preferred_element_type=F32).reshape(
-        samples, lat_rows, width
-    )
-    middle = lat_f + factor * branch
-    hnorm, mlp_norm_back = jax.vjp(layer_norm, middle, gain_mlp)
-    hnorm_low = hnorm.astype(BF16).reshape(samples * lat_rows, width)
-    pre = jnp.dot(hnorm_low, w_up, preferred_element_type=F32) + b_up
-    activated, gelu_back = jax.vjp(jax.nn.gelu, pre)
-    hidden_low = activated.astype(BF16)
-    mlp_out = (jnp.dot(hidden_low, w_down, preferred_element_type=F32) + b_down).reshape(
-        samples, lat_rows, width
-    )
-    result = (middle + factor * mlp_out).astype(BF16)
-    d_result = cotangent.astype(F32)
-    d_mlp = (factor * d_result).astype(BF16).reshape(samples * lat_rows, width)
-    grad_bdown = jnp.sum(d_mlp.astype(F32), 0)
-    d_hidden = jnp.einsum("rd,fd->rf", d_mlp, w_down, preferred_element_type=F32)
-    d_pre = gelu_back(d_hidden)[0].astype(BF16)
-    grad_bup = jnp.sum(d_pre.astype(F32), 0)
-    d_hnorm = jnp.einsum("rf,df->rd", d_pre, w_up, preferred_element_type=F32).reshape(
-        samples, lat_rows, width
-    )
-    d_middle_part, grad_gmlp = mlp_norm_back(d_hnorm)
-    d_middle = d_result + d_middle_part
-    d_branch = (factor * d_middle).astype(BF16).reshape(samples * lat_rows, width)
-    d_att = jnp.einsum("ed,brd->ber", w_out, d_branch.reshape(samples, lat_rows, width),
-                       preferred_element_type=F32).astype(BF16).astype(F32)
-    d_att = d_att.reshape(samples, HEADS, HEAD_DIM, lat_rows)
-    den_h = denom.reshape(samples, HEADS, lat_rows)
-    top_h = top.reshape(samples, HEADS, lat_rows)
-    dnum = (d_att / den_h[:, :, None]).reshape(samples, width, lat_rows)
-    delta = jnp.sum(d_att * att_t.reshape(d_att.shape), 2) / den_h
-    blank = jnp.zeros((samples, 8 - PAIRS, 2 * lat_rows), F32)
-    stat = jnp.concatenate(
-        (
-            top_h.reshape(samples, PAIRS, 2 * lat_rows),
-            blank,
-            delta.reshape(samples, PAIRS, 2 * lat_rows),
-            blank,
-        ),
-        1,
-    )
-
-    shares = 8
-    share = lax.rem(tok_index, shares)
+    msg, result, dmid, lefts, rights, attended, vec = latent_block(
+        part, drop_mask, latents, cotangent, w_out, gain_mlp, w_up, b_up, w_down, b_down
+    )
+    result = result.reshape(latents.shape)
+
+    core = lax.rem(tok_index, 2)
+    shares = 4
+    share = lax.rem(tok_index // 2, shares)
     depth = width // shares
-    hid_dim = w_up.shape[1]
     mine = lambda x: lax.dynamic_slice_in_dim(x, share * depth, depth, 1)
-    grad_up = jnp.einsum("rd,rf->df", mine(hnorm_low), d_pre, preferred_element_type=F32)
-    grad_down = jnp.einsum("rf,rd->df", hidden_low, mine(d_mlp), preferred_element_type=F32)
-    grad_out = jnp.einsum("re,rd->ed", mine(attended_low), d_branch, preferred_element_type=F32)
+    grad_up = jnp.einsum("rd,rf->df", mine(lefts[0]), rights[0], preferred_element_type=F32)
+    grad_down = jnp.einsum("rf,rd->df", rights[1], mine(lefts[1]), preferred_element_type=F32)
+    grad_out = jnp.einsum("re,rd->ed", mine(attended), lefts[2], preferred_element_type=F32)
     both = jnp.concatenate((grad_up, grad_down), 0)
     both = lax.psum_scatter(both, "stream", scatter_dimension=1, tiled=True)
     grad_out = lax.psum_scatter(grad_out, "stream", scatter_dimension=1, tiled=True)
-    groups = [list(range(g, g + shares)) for g in range(0, members, shares)]
+    size = 2 * shares
+    groups = [list(range(g, g + size)) for g in range(0, members, size)]
     both = lax.all_gather(both, "tok", axis_index_groups=groups)
+    both = both.reshape(shares, 2, 2 * depth, -1).sum(1)
     grad_up = both[:, :depth].reshape(width, -1)
     grad_down = both[:, depth:].reshape(width, -1).T
-    grad_out = lax.all_gather(grad_out, "tok", axis_index_groups=groups, tiled=True)
+    grad_out = lax.all_gather(grad_out, "tok", axis_index_groups=groups)
+    grad_out = grad_out.reshape(shares, 2, depth, -1).sum(1).reshape(width, -1)
 
     dkey, dval, dlat, dgain_q, grad_query = attend_backward(
-        bounds, latents, keys, values, query, normed, dnum, stat, gain_query, w_query
+        bounds, latents, keys, values, query, normed, msg, gain_query, w_query
     )
     d_tokens, dgain_t, grad_key, grad_value = token_backward(
         place, tokens, tsort, dkey, dval, gain_token, w_key, w_value
     )
-    d_latents = d_middle + lax.psum(dlat, "tok").reshape(d_middle.shape)
+    dlat = dlat.reshape(2, -1, width)
+    dlat = dlat.at[core].add(jnp.where(tok_index < 2, dmid, 0.0))
+    d_latents = lax.psum(dlat, "tok").reshape(latents.shape)
+    pairs = [[g, g + 1] for g in range(0, members, 2)]
+    vec = lax.psum(vec, "tok", axis_index_groups=pairs)
+    grad_bup, grad_bdown, grad_gmlp = vec[0], vec[1, :width], vec[2, :width]
     grad_key, grad_value, grad_query, grad_gtoken, grad_gquery = lax.psum(
         (grad_key, grad_value, grad_query, dgain_t[0], dgain_q[0]), ("stream", "tok")
     )

time: 597 us -> 562 us (0.941)
  Pallas kernels: 74.1 us -> 165 us
  blocking collectives: 128 us -> 57.3 us
  matrix products: 58.1 us -> 6.7 us
  waiting for transfers between devices: 248 us -> 266 us
  other arithmetic: 31.7 us -> 15.5 us
    pallas_call x0 -> x1, Pallas kernels: none -> 93.4 us  [latent_block(): pl.pallas_call(latent_kernel, name='latent_block', out_shape=(sds((sample...]
    dot_general x8 -> x2, matrix products: 55.4 us -> 3.84 us  [the longest x1 2.95 us: local(): jnp.einsum('rd,rf->df', mine(lefts[0]), rights[0], preferred_element_type...]
    all_gather x1, waiting for transfers between devices: 50.8 us -> 0.01 us  [local(): both = lax.all_gather(both, 'tok', axis_index_groups=groups)]
    psum x1 -> x0, blocking collectives: 29.5 us -> none  [local(): lax.psum((num_part * fade[:, :, :, None], den_part * fade), 'tok')]
    pmax x1 -> x0, blocking collectives: 27.1 us -> none  [local(): top = lax.pmax(top_part, 'tok')]
    psum x2, waiting for transfers between devices: 42.9 us -> 64 us  [the longest x1 64 us: local(): d_latents = lax.psum(dlat, 'tok').reshape(latents.shape)]
    reduce_scatter x1, waiting for transfers between devices: 0.02 us -> 17.2 us  [local(): both = lax.psum_scatter(both, 'stream', scatter_dimension=1, tiled=True)]
    unnamed x7 -> x8, waiting for transfers between devices: 0.58 us -> 16.6 us
  transfers between devices with their start and end apart: 6 -> 7, of which waited for: 3 -> 4; matrix products, arithmetic and copies ran while one was open for 9% -> 6% of each run, Pallas kernels for 7% -> 7%
where the time goes in v2:
time: 562 us; the launch traced here: 560 us
  waiting for transfers between devices  266 us (47%)
  Pallas kernels  165 us (29%)
  blocking collectives  57.3 us (10%)
  local copies, waits for them, and re-layouts  33.7 us (6%)
  between operations  15.6 us (3%)
  other arithmetic  15.5 us (3%)
  matrix products  6.7 us (1%)
    psum x1, waiting for transfers between devices, local(): lax.psum((grad_key, grad_value, grad_query, dgain_t[0], dgain_q[0]), ('st...  169 us
    pallas_call x1, Pallas kernels, latent_block(): pl.pallas_call(latent_kernel, name='latent_block', out_shape=(sds((sample...  93.4 us
    psum x1, waiting for transfers between devices, local(): d_latents = lax.psum(dlat, 'tok').reshape(latents.shape)  64 us
    psum x1, blocking collectives, local(): lax.psum((grad_key, grad_value, grad_query, dgain_t[0], dgain_q[0]), ('st...  39.9 us
    pallas_call x1, Pallas kernels, attend_forward(): pl.pallas_call(forward_kernel, name='attend_forward', out_shape=(sds((sam...  29.9 us
    pallas_call x1, Pallas kernels, attend_backward(): pl.pallas_call(backward_kernel, name='attend_backward', out_shape=(sds((r...  24 us
    unnamed x24, local copies, waits for them, and re-layouts  17.6 us
    psum x1, blocking collectives, local(): lax.psum((grad_bup, grad_bdown, grad_gmlp), 'stream')  17.4 us
  transfers between devices with their start and end apart: 7, of which 4 were waited for; matrix products, arithmetic and copies ran while one was open for 6% of the time, Pallas kernels for 7%

profile of v2, /device:TPU:0, one launch (start us, length us, event | category | flops | bytes accessed | tf_op | source)
XLA Modules:
  0.0 560.4 jit_solution(14765724397831394441)
XLA Ops:
  8.1 1.3 reshape.121.gain_q_ref
  9.4 1.3 reshape.122.gain_t_ref
  10.6 1.3 reshape.125.gain_ref
  11.9 1.3 reshape.127.bdn_ref
  13.2 1.3 subtract_select_fusion
  14.5 29.9 %attend_forward.1 = (f32[8,4,208,128]{3,2,1,0:T(8,128)}, bf16[1280,768]{1,0:T(8,128)(2,1)}, bf16[1280,768]{1,0:T(8,128)(2,1)}, bf16[1024,768]{1,0:T(8,128)(2,1)}...) custom-call(s32[1,1024]{1,0:T(1,128)} %bitcast.51, ...), custom_call_target="tpu_custom_call" | custom-call | tf_op jit(solution)/shard_map/attend_forward/pallas_call | solution.py:200
  44.3 93.4 %latent_block.1 = (f32[8,800,128]{2,1,0:T(8,128)}, bf16[1024,768]{1,0:T(8,128)(2,1)}, f32[512,768]{1,0:T(8,128)}, bf16[3,512,768]{2,1,0:T(8,128)(2,1)}, bf16[2,5...) custom-call(f32[8,4,208,128]{3,2,1,0:T(8,128)} %get-tuple-element.50.part_ref, ...), custom_call_target="tpu_custom_call" | custom-call | tf_op jit(solution)/shard_map/latent_block/pallas_call | solution.py:791
  137.7 2.9 convolution_bitcast_fusion
  140.8 3.0 fusion.2
  145.3 2.4 pad_maximum_fusion
  148.4 16.0 %reduce-scatter.7.cloned.1.call-done = f32[192,192]{1,0:T(8,128)} async-done(((f32[768,192]{1,0:T(8,128)}), f32[192,192]{1,0:T(8,128)}) %reduce-scatter.7.cloned.1.call-update) | async-done | bytes 147472
  164.4 1.7 copy.39
  166.4 24.0 %attend_backward.1 = (bf16[1024,768]{1,0:T(8,128)(2,1)}, bf16[1024,768]{1,0:T(8,128)(2,1)}, f32[1024,768]{1,0:T(8,128)}, f32[8,768]{1,0:T(8,128)}, f32[768,768]{1,0:T(8,128)}) custom-call(s32[16]{0:T(128)} %get-tuple-element.52.bounds_ref, bf16[1024,768]{1,0:T(8,128)(2,1)} %bitcast.39, bf16[1280,768]{1,0:T(8,128)(2,1)} %get-tuple-element.53.key_ref, ...), custom_call_target="tpu_custom_call" | custom-call | tf_op jit(solution)/shard_map/attend_backward/pallas_call | solution.py:337
  190.4 17.3 %token_backward.1 = (f32[1024,768]{1,0:T(8,128)}, f32[8,768]{1,0:T(8,128)}, f32[768,768]{1,0:T(8,128)}, f32[768,768]{1,0:T(8,128)}) custom-call(f32[1024,128]{1,0:T(8,128)} %get-tuple-element.60.place_ref, bf16[1024,768]{1,0:T(8,128)(2,1)} %tok_ref.3, bf16[1024,768]{1,0:T(8,128)(2,1)} %get-tuple-element.61.tsort_ref, ...), custom_call_target="tpu_custom_call" | custom-call | tf_op jit(solution)/shard_map/token_backward/pallas_call | solution.py:412
  207.8 17.2 %reduce-scatter.5.cloned.1.call-done = f32[384,768]{1,0:T(8,128)} async-done(((f32[384,3072]{1,0:T(8,128)}), f32[384,768]{1,0:T(8,128)}) %reduce-scatter.5.cloned.1.call-update) | async-done | bytes 1179664 | tf_op jit(solution)/shard_map/reduce_scatter | solution.py:903
  225.8 2.4 fusion.6
  228.2 1.7 copy-done.1
  230.6 39.9 %all-reduce = (f32[768]{0:T(1024)S(1)}, f32[768]{0:T(1024)}) all-reduce(f32[768]{0:T(1024)S(1)} %get-tuple-element.131, f32[768]{0:T(1024)S(1)} %get-tuple-element.130), channel_id=1, replica_groups=mesh['stream'=4,'tok'=8] {'stream','tok'}, use_global_device_ids=true, to_apply=%region_2.3 | all-reduce | flops 1536 | bytes 12288 | tf_op jit(solution)/shard_map/psum | solution.py:926
  273.0 17.4 %all-reduce.2 = (f32[768]{0:T(1024)S(1)}, f32[3072]{0:T(1024)S(1)}, f32[768]{0:T(1024)S(1)}) all-reduce(f32[768]{0:T(1024)S(1)} %get-tuple-element.117, f32[3072]{0:T(1024)S(1)} %bitcast.50, f32[768]{0:T(1024)S(1)} %get-tuple-element.116), channel_id=1, replica_groups=mesh['stream'=4,'tok'=8] {'stream'}, use_global_device_ids=true, to_apply=%region_10.11 | all-reduce | flops 4608 | bytes 36864 | tf_op jit(solution)/shard_map/psum | solution.py:929
  292.3 1.6 reduce_sum.18
  295.0 168.6 %all-reduce.11.cloned.1.call-done = (f32[768,768]{1,0:T(8,128)}, f32[768,768]{1,0:T(8,128)}, f32[768,768]{1,0:T(8,128)}) async-done(((f32[768,768]{1,0:T(8,128)}, f32[768,768]{1,0:T(8,128)}, f32[768,768]{1,0:T(8,128)}), (f32[768,768]{1,0:T(8,128)}, f32[768,768]{1,0:T(8,128)}, f32[768,768]{1,0:T(8,128)})) %all-reduce.11.cloned.1.call-update) | async-done | bytes 7077904 | tf_op jit(solution)/shard_map/psum | solution.py:926
  463.6 1.5 constant_dynamic-slice_fusion
  466.2 7.1 %reduce_sum.19 = f32[4,384,768]{2,1,0:T(8,128)} reduce(f32[4,2,384,768]{3,2,1,0:T(8,128)} %bitcast.40, f32[]{:T(128)} %constant.60.clone.1), dimensions={1}, to_apply=%region_12.13 | reduce | flops 1179648 | bytes 14155780 | tf_op jit(solution)/shard_map/reduce_sum | solution.py:908
  473.3 4.2 fusion.17
  477.6 1.9 copy.37
  479.5 64.0 %all-reduce.7.cloned.1.call-done = f32[8,128,768]{2,1,0:T(8,128)} async-done(((f32[8,128,768]{2,1,0:T(8,128)}), f32[8,128,768]{2,1,0:T(8,128)}) %all-reduce.7.cloned.1.call-update) | async-done | bytes 3145744 | tf_op jit(solution)/shard_map/psum | solution.py:922
  543.5 2.8 copy.47
  546.3 1.7 copy.48
  548.0 1.1 copy-done.6
  549.1 1.4 copy.49
  550.5 1.1 copy-done.5
  551.6 1.4 copy.50
  (42 shorter events, 10.7 us)
Async XLA Ops:
  8.0 156.4 %reduce-scatter.7.cloned.1.call-start = ((), (), s32[]{:S(2)}) async-start(), calls=%async_computation.7 | async-start | bytes 983040
  137.7 2.9 copy-start.4
  140.6 84.4 %reduce-scatter.5.cloned.1.call-start = ((), (), s32[]{:S(2)}) async-start(), calls=%async_computation.4 | async-start | bytes 5898240 | tf_op jit(solution)/shard_map/reduce_scatter | solution.py:903
  140.7 3.7 copy-start.2
  147.8 123.4 %all-reduce.9.cloned.1.call-start = ((), (), s32[]{:S(2)}) async-start(), calls=%async_computation.3 | async-start | bytes 196608 | tf_op jit(solution)/shard_map/psum | solution.py:924
  148.3 144.0 %all-gather.5.cloned.1.call-start = ((), (), s32[]{:S(2)}) async-start(), calls=%async_computation.5 | async-start | bytes 1769472 | tf_op jit(solution)/shard_map/all_gather | solution.py:911
  166.1 297.5 %all-reduce.11.cloned.1.call-start = ((), (), s32[]{:S(2)}) async-start(), calls=%async_computation.8 | async-start | bytes 14155776 | tf_op jit(solution)/shard_map/psum | solution.py:926
  207.7 17.4 %copy-start.7 = (s32[3]{0:T(128)S(1)}, s32[3]{0:T(128)}, u32[]{:S(2)}) copy-start(s32[3]{0:T(128)} %constant.58.clone.1) | copy-start | bytes 40
  207.7 18.1 %copy-start = (f32[1024,768]{1,0:T(8,128)S(1)}, f32[1024,768]{1,0:T(8,128)}, u32[]{:S(2)}) copy-start(f32[1024,768]{1,0:T(8,128)} %get-tuple-element.58) | copy-start | bytes 9437188
  207.7 258.5 %all-gather.7.cloned.1.call-start = ((), (), s32[]{:S(2)}) async-start(), calls=%async_computation.6 | async-start | bytes 10616832 | tf_op jit(solution)/shard_map/all_gather | solution.py:907
  225.0 318.5 %all-reduce.7.cloned.1.call-start = ((), (), s32[]{:S(2)}) async-start(), calls=%async_computation.2 | async-start | bytes 6291456 | tf_op jit(solution)/shard_map/psum | solution.py:922
  228.1 1.7 copy-start.1
  543.5 2.8 copy-start.3
  546.3 2.8 copy-start.6
  549.1 2.5 copy-start.5
Sparse Core Ops, SparseCore 0:
  140.7 23.5 reduce-scatter.6
  167.6 57.2 reduce-scatter.4
  227.3 35.9 all-gather.4
  264.8 96.8 all-gather.6
Sparse Core Ops, SparseCore 1:
  150.5 14.9 all-reduce.8
  207.8 255.7 all-reduce.10
  466.6 76.9 all-reduce.6

commit v3 on v2

--- a/solution.py
+++ b/solution.py
@@ -16,6 +16,14 @@
 PIECE_ROWS = NUM_ROWS + 16
 MSG_ROWS = HEADS * HEAD_DIM + 32
 BLOCK = 256
+LAG = 2
+TOKEN_TICKS = (1, 2, 3, 4, 5, 6, 7, 8)
+SMALL_TICK = 8
+PAIR_TICK = 9
+ONE_TICK = 12
+TWO_TICK = 15
+WIDE_ONE_TICKS = (7, 13)
+WIDE_TWO_TICKS = (11, 17)
 NEG = -1e30
 F32 = jnp.float32
 BF16 = jnp.bfloat16
@@ -242,8 +250,7 @@
     msg_ref,
     gain_q_ref,
     wq_ref,
-    dkey_ref,
-    dval_ref,
+    dkv_ref,
     dlat_ref,
     dgain_ref,
     dwq_ref,
@@ -255,7 +262,7 @@
     stat_ref,
 ):
     samples = query_ref.shape[0]
-    rows = dkey_ref.shape[0]
+    rows = dkv_ref.shape[1]
     lat_rows = 128
     step = 256
     width = dwq_ref.shape[0]
@@ -324,10 +331,10 @@
 
     lax.fori_loop(0, samples, sample_step, 0)
     for r in range(0, rows, step):
-        dkey_ref[r : r + step, :] = dk_ref[r : r + step, :].astype(BF16)
-        dval_ref[r : r + step, :] = dv_ref[r : r + step, :].astype(BF16)
+        dkv_ref[0, r : r + step, :] = dk_ref[r : r + step, :].astype(BF16)
+        dkv_ref[1, r : r + step, :] = dv_ref[r : r + step, :].astype(BF16)
     for c in range(0, width, 256):
-        dwq_ref[c : c + 256, :] = dot(normed_ref[:, c : c + 256], dquery_ref[...], (0, 0))
+        dwq_ref[c : c + 256, :] = dot(dquery_ref[:, c : c + 256], normed_ref[...], (0, 0))
 
 
 def attend_backward(bounds, latents, keys, values, query, normed, msg, gain_q, wq):
@@ -338,14 +345,13 @@
         backward_kernel,
         name="attend_backward",
         out_shape=(
-            sds((rows, width), BF16),
-            sds((rows, width), BF16),
+            sds((2, rows, width), BF16),
             sds((samples * lat_rows, width), F32),
             sds((8, width), F32),
             sds((width, width), F32),
         ),
         in_specs=[smem()] + [vmem()] * 8,
-        out_specs=(vmem(),) * 5,
+        out_specs=(vmem(),) * 4,
         scratch_shapes=[
             pltpu.VMEM((rows + BLOCK, width), F32),
             pltpu.VMEM((rows + BLOCK, width), F32),
@@ -366,62 +372,6 @@
         gain_q.reshape(1, width),
         wq,
     )
-
-
-def token_kernel(
-    place_ref,
-    tok_ref,
-    tsort_ref,
-    dkey_ref,
-    dval_ref,
-    gain_t_ref,
-    wk_ref,
-    wv_ref,
-    dtok_ref,
-    dgain_ref,
-    dwk_ref,
-    dwv_ref,
-):
-    rows = tok_ref.shape[0]
-    width = tok_ref.shape[1]
-    step = 256
-    for c in range(0, width, 256):
-        dwk_ref[c : c + 256, :] = dot(tsort_ref[:, c : c + 256], dkey_ref[...], (0, 0))
-        dwv_ref[c : c + 256, :] = dot(tsort_ref[:, c : c + 256], dval_ref[...], (0, 0))
-    dgain_ref[...] = jnp.zeros_like(dgain_ref)
-
-    def token_step(i, carry):
-        at = pl.ds(pl.multiple_of(i * step, step), step)
-        target = lax.broadcasted_iota(jnp.int32, (step, rows), 1).astype(F32)
-        chosen = target == place_ref[at, 0:1]
-        pick = jnp.where(chosen, 1.0, 0.0).astype(BF16)
-        dkey = dot(pick, dkey_ref[...]).astype(BF16)
-        dval = dot(pick, dval_ref[...]).astype(BF16)
-        dnormed = dot(dkey, wk_ref[...], (1, 1)) + dot(dval, wv_ref[...], (1, 1))
-        unit, inv = norm_parts(tok_ref[at, :].astype(F32))
-        dgain_ref[0:1, :] += jnp.sum(dnormed * unit, 0, keepdims=True)
-        dtok_ref[at, :] = norm_back(unit, inv, gain_t_ref[...], dnormed)
-        return carry
-
-    lax.fori_loop(0, rows // step, token_step, 0)
-
-
-def token_backward(place, tokens, tsort, dkey, dval, gain_t, wk, wv):
-    rows, width = tokens.shape
-    sds = jax.ShapeDtypeStruct
-    return pl.pallas_call(
-        token_kernel,
-        name="token_backward",
-        out_shape=(
-            sds((rows, width), F32),
-            sds((8, width), F32),
-            sds((width, width), F32),
-            sds((width, width), F32),
-        ),
-        in_specs=[vmem()] * 8,
-        out_specs=(vmem(),) * 4,
-        compiler_params=pltpu.CompilerParams(vmem_limit_bytes=VMEM_BYTES),
-    )(place, tokens, tsort, dkey, dval, gain_t.reshape(1, width), wk, wv)
 
 
 MESH = pl.DeviceIdType.MESH
@@ -684,7 +634,7 @@
             j, q = lax.div(t, PIECES), lax.rem(t, PIECES)
             merge(part_ref.at[core * half + j, q], pair_ref.at[t], own_ref.at[t])
 
-        r = t - chip
+        r = t - LAG * chip
 
         @pl.when((r >= 0) & (r < chunks))
         def _():
@@ -701,7 +651,7 @@
             def _():
                 right_copy(r).start()
 
-        u = t - (chips - 1 - chip)
+        u = t - LAG * (chips - 1 - chip)
 
         @pl.when((u >= 0) & (u < chunks))
         def _():
@@ -721,7 +671,7 @@
 
                 left_copy(u).start()
 
-        w = t - (chips - 1)
+        w = t - LAG * jnp.maximum(chip, chips - 1 - chip)
 
         @pl.when((w >= 0) & (w < chunks))
         def _():
@@ -740,13 +690,13 @@
             for copy in weights:
                 copy.wait()
 
-        @pl.when(m >= 0)
+        @pl.when((m >= 0) & (m < chunks))
         def _():
             mlp(lax.div(m, PIECES), lax.rem(m, PIECES))
 
         return carry
 
-    lax.fori_loop(0, chunks + chips - 1 + PIECES - 1, step, 0)
+    lax.fori_loop(0, chunks + LAG * (chips - 1) + PIECES - 1, step, 0)
 
     def finish_chunk(i, carry):
         pair_copy(i).wait_send()
@@ -858,6 +808,701 @@
     )
 
 
+ZROWS = 32
+SUBS = 2
+
+
+def gradient_kernel(
+    dlat_hbm,
+    dmid_ref,
+    latent_hbm,
+    dwq_ref,
+    vec_ref,
+    dgain_q_ref,
+    place_ref,
+    tok_ref,
+    tsort_ref,
+    dkv_ref,
+    gain_t_ref,
+    wk_ref,
+    wv_ref,
+    dlat_out,
+    gather_out,
+    kv_out,
+    query_out,
+    small_out,
+    dtok_ref,
+    line_ref,
+    right_ref,
+    left_ref,
+    dmine_ref,
+    wide_ref,
+    wide_one,
+    wide_two,
+    send_ref,
+    mine_ref,
+    pair_ref,
+    one_ref,
+    two_ref,
+    small_ref,
+    load_sem,
+    wide_load_sem,
+    dpair_send,
+    dpair_recv,
+    right_send,
+    right_recv,
+    left_send,
+    left_recv,
+    back_send,
+    back_recv,
+    back_local,
+    wide_one_send,
+    wide_one_recv,
+    wide_two_send,
+    wide_two_recv,
+    wide_z_send,
+    wide_z_recv,
+    wide_core_send,
+    wide_core_recv,
+    wide_local,
+    pair_send,
+    pair_recv,
+    one_send,
+    one_recv,
+    two_send,
+    two_recv,
+    spread_send,
+    spread_recv,
+    share_send,
+    share_recv,
+    query_send,
+    query_recv,
+    keep_local,
+):
+    width = tok_ref.shape[1]
+    rows = tok_ref.shape[0]
+    lat_chunks = dmine_ref.shape[0]
+    all_chunks = line_ref.shape[0]
+    kv_rows = send_ref.shape[2]
+    q_rows = query_out.shape[2]
+    mix = kv_rows + q_rows
+    half_chunks = (all_chunks - lat_chunks) // 2
+    kv_chunks = kv_rows // ZROWS
+    wide_half = wide_ref.shape[2]
+    sub_rows = wide_half // SUBS
+
+    stream = lax.axis_index("stream")
+    tok = lax.axis_index("tok")
+    chips = lax.axis_size("tok") // 2
+    core = lax.rem(tok, 2)
+    chip = lax.div(tok, 2)
+    other = 1 - core
+    parity = lax.rem(chip, 2)
+    flip_x = stream + 1 - 2 * lax.rem(stream, 2)
+    flip_y = lax.rem(stream + 2, 4)
+    flip_xy = 3 - stream
+    partner = (stream, tok + 1 - 2 * core)
+    right = (stream, tok + 2)
+    left = (stream, tok - 2)
+    beside = (stream, tok + 2 - 4 * parity)
+    near = ((flip_x, tok), (flip_y, tok))
+    first = (flip_x, flip_y)
+    has_right = chip < chips - 1
+    has_left = chip > 0
+
+    barrier = pltpu.get_barrier_semaphore()
+    for target in (partner,) + near:
+        pl.semaphore_signal(barrier, inc=1, device_id=target, device_id_type=MESH)
+
+    @pl.when(has_right)
+    def _():
+        pl.semaphore_signal(barrier, inc=1, device_id=right, device_id_type=MESH)
+
+    @pl.when(has_left)
+    def _():
+        pl.semaphore_signal(barrier, inc=1, device_id=left, device_id_type=MESH)
+
+    def remote(src, dst, send, recv, target):
+        return pltpu.make_async_remote_copy(
+            src_ref=src,
+            dst_ref=dst,
+            send_sem=send,
+            recv_sem=recv,
+            device_id=target,
+            device_id_type=MESH,
+        )
+
+    load = pltpu.make_async_copy(dlat_hbm.at[core], dmine_ref, load_sem)
+    load.start()
+    wide_loads = []
+    for h in range(2):
+        for n, block in enumerate((stream, first[1 - h])):
+            copy = pltpu.make_async_copy(
+                latent_hbm.at[block, pl.ds(h * wide_half, wide_half)],
+                wide_ref.at[h, n],
+                wide_load_sem.at[2 * h + n],
+            )
+            copy.start()
+            wide_loads.append(copy)
+    pl.semaphore_wait(barrier, 3 + has_right.astype(jnp.int32) + has_left.astype(jnp.int32))
+
+    def dpair_copy(i):
+        return remote(
+            dlat_hbm.at[other, i], line_ref.at[i], dpair_send.at[i], dpair_recv.at[i], partner
+        )
+
+    def start_dpair(i, carry):
+        dpair_copy(i).start()
+        return carry
+
+    lax.fori_loop(0, lat_chunks, start_dpair, 0)
+
+    def wide_one_copy(h, n, sub):
+        block = (first[h], flip_xy)[n]
+        at = pl.ds(h * wide_half + sub * sub_rows, sub_rows)
+        return remote(
+            latent_hbm.at[block, at],
+            wide_one.at[h, n, pl.ds(sub * sub_rows, sub_rows)],
+            wide_one_send.at[h, n, sub],
+            wide_one_recv.at[h, n, sub],
+            near[h],
+        )
+
+    def wide_two_copy(h, sub):
+        at = pl.ds(sub * sub_rows, sub_rows)
+        return remote(
+            wide_ref.at[h, 1, at],
+            wide_two.at[h, at],
+            wide_two_send.at[h, sub],
+            wide_two_recv.at[h, sub],
+            near[1 - h],
+        )
+
+    def gather_at(c, e, h, sub):
+        return gather_out.at[c, e, pl.ds(h * wide_half + sub * sub_rows, sub_rows)]
+
+    def wide_z_copy(h, sub):
+        return remote(
+            wide_ref.at[h, 0, pl.ds(sub * sub_rows, sub_rows)],
+            gather_at(core, parity, h, sub),
+            wide_z_send.at[h, sub],
+            wide_z_recv.at[h, sub],
+            beside,
+        )
+
+    def wide_z_arrival(h, sub):
+        return remote(
+            wide_ref.at[h, 0, pl.ds(sub * sub_rows, sub_rows)],
+            gather_at(core, 1 - parity, h, sub),
+            wide_z_send.at[h, sub],
+            wide_z_recv.at[h, sub],
+            beside,
+        )
+
+    def wide_core_copy(far, h, sub):
+        if far:
+            src = gather_at(core, 1 - parity, h, sub)
+            dst = gather_at(core, 1 - parity, h, sub)
+        else:
+            src = wide_ref.at[h, 0, pl.ds(sub * sub_rows, sub_rows)]
+            dst = gather_at(core, parity, h, sub)
+        return remote(
+            src, dst, wide_core_send.at[far, h, sub], wide_core_recv.at[far, h, sub], partner
+        )
+
+    def wide_core_arrival(far, h, sub):
+        place = gather_at(other, 1 - parity if far else parity, h, sub)
+        return remote(
+            place, place, wide_core_send.at[far, h, sub], wide_core_recv.at[far, h, sub], partner
+        )
+
+    def wide_keep(h, sub):
+        return pltpu.make_async_copy(
+            wide_ref.at[h, 0, pl.ds(sub * sub_rows, sub_rows)],
+            gather_at(core, parity, h, sub),
+            wide_local.at[h, sub],
+        )
+
+    for sub in range(SUBS):
+        for h in range(2):
+            for n in range(2):
+                wide_one_copy(h, n, sub).start()
+
+    def wide_event_one(sub):
+        at = slice(sub * sub_rows, (sub + 1) * sub_rows)
+        for h in range(2):
+            for n in range(2):
+                wide_one_copy(h, n, sub).wait_recv()
+            wide_ref[h, 1, at, :] += wide_one[h, 1, at, :]
+            wide_two_copy(h, sub).start()
+            wide_ref[h, 0, at, :] += wide_one[h, 0, at, :]
+
+    def wide_event_two(sub):
+        at = slice(sub * sub_rows, (sub + 1) * sub_rows)
+        for h in range(2):
+            wide_two_copy(h, sub).wait_recv()
+            wide_ref[h, 0, at, :] += wide_two[h, at, :]
+            wide_z_copy(h, sub).start()
+            wide_core_copy(0, h, sub).start()
+            wide_keep(h, sub).start()
+
+    def wide_event_three(sub):
+        for h in range(2):
+            wide_z_arrival(h, sub).wait_recv()
+            wide_core_copy(1, h, sub).start()
+
+    turned = tsort_ref[...].T
+    share = width // 4
+    for block in range(4):
+        at = slice(block * share, (block + 1) * share)
+        product = dot(turned[at], dkv_ref[other])
+        for h in range(2):
+            send_ref[h, block] = product[h * kv_rows : (h + 1) * kv_rows]
+
+    def pair_copies():
+        out = []
+        for h in range(2):
+            out.append(
+                remote(
+                    send_ref.at[h],
+                    pair_ref.at[h, :, pl.ds(0, kv_rows)],
+                    pair_send.at[h],
+                    pair_recv.at[h],
+                    partner,
+                )
+            )
+            out.append(
+                remote(
+                    dwq_ref.at[:, other, h],
+                    pair_ref.at[h, :, pl.ds(kv_rows, q_rows)],
+                    pair_send.at[2 + h],
+                    pair_recv.at[2 + h],
+                    partner,
+                )
+            )
+        out.append(
+            remote(
+                small_ref,
+                pair_ref.at[0, :, pl.ds(mix, 16)],
+                pair_send.at[4],
+                pair_recv.at[4],
+                partner,
+            )
+        )
+        return out
+
+    pairs = pair_copies()
+    for copy in pairs[:4]:
+        copy.start()
+
+    for block in range(4):
+        at = slice(block * share, (block + 1) * share)
+        product = dot(turned[at], dkv_ref[core])
+        for h in range(2):
+            piece = product[h * kv_rows : (h + 1) * kv_rows]
+            mine_ref[h, block, :kv_rows, :] = piece
+            mine_ref[h, block, kv_rows:mix, :] = dwq_ref[block, core, h]
+    mine_ref[1, :, mix:, :] = jnp.zeros((4, 16, width), F32)
+
+    here = (chip == 0).astype(F32)
+
+    token_step = 128
+    small_ref[...] = jnp.zeros_like(small_ref)
+
+    def token_part(i):
+        at = pl.ds(pl.multiple_of(i * token_step, token_step), token_step)
+        target = lax.broadcasted_iota(jnp.int32, (token_step, rows), 1).astype(F32)
+        pick = jnp.where(target == place_ref[at, 0:1], 1.0, 0.0).astype(BF16)
+        dkey = dot(pick, dkv_ref[0]).astype(BF16)
+        dval = dot(pick, dkv_ref[1]).astype(BF16)
+        dnormed = dot(dkey, wk_ref[...], (1, 1)) + dot(dval, wv_ref[...], (1, 1))
+        unit, inv = norm_parts(tok_ref[at, :].astype(F32))
+        small_ref[0, 4:5, :] += jnp.sum(dnormed * unit, 0, keepdims=True)
+        dtok_ref[at, :] = norm_back(unit, inv, gain_t_ref[...], dnormed)
+
+    def small_start():
+        for block in range(4):
+            small_ref[block, 0:1, :] = vec_ref[0:1, block * width : (block + 1) * width] * here
+            small_ref[block, 1:2, :] = dgain_q_ref[0:1, :]
+            small_ref[block, 2:3, :] = vec_ref[2:3, :width] * here
+            small_ref[block, 3:4, :] = vec_ref[1:2, :width] * here
+            if block:
+                small_ref[block, 4:5, :] = small_ref[0, 4:5, :]
+        pairs[4].start()
+
+    def one_copy(h, n):
+        block = (first[h], flip_xy)[n]
+        return remote(
+            mine_ref.at[h, block], one_ref.at[h, n], one_send.at[h, n], one_recv.at[h, n], near[h]
+        )
+
+    def two_copy(h):
+        return remote(
+            mine_ref.at[h, first[1 - h]], two_ref.at[h], two_send.at[h], two_recv.at[h], near[1 - h]
+        )
+
+    def pair_event():
+        for copy in pairs:
+            copy.wait_recv()
+        for h in range(2):
+            for block in range(4):
+                mine_ref[h, block, :mix, :] += pair_ref[h, block, :mix, :]
+                if h == 0:
+                    mine_ref[h, block, mix:, :] = small_ref[block] + pair_ref[h, block, mix:, :]
+        for h in range(2):
+            for n in range(2):
+                one_copy(h, n).start()
+
+    def one_event():
+        for h in range(2):
+            for n in range(2):
+                one_copy(h, n).wait_recv()
+            mine_ref[h, first[1 - h]] += one_ref[h, 1]
+            two_copy(h).start()
+
+    def two_event():
+        for h in range(2):
+            two_copy(h).wait_recv()
+            total = mine_ref[h, stream] + one_ref[h, 0] + two_ref[h]
+            for k in range(half_chunks):
+                line_ref[lat_chunks + h * half_chunks + k] = total[k * ZROWS : (k + 1) * ZROWS]
+
+    def right_copy(i):
+        return remote(right_ref.at[i], right_ref.at[i], right_send.at[i], right_recv.at[i], right)
+
+    def left_copy(i):
+        return remote(left_ref.at[i], left_ref.at[i], left_send.at[i], left_recv.at[i], left)
+
+    def back_copy(i):
+        return remote(
+            line_ref.at[i], dlat_out.at[core, i], back_send.at[i], back_recv.at[i], partner
+        )
+
+    def back_arrival(i):
+        return remote(
+            line_ref.at[i], dlat_out.at[other, i], back_send.at[i], back_recv.at[i], partner
+        )
+
+    def back_keep(i):
+        return pltpu.make_async_copy(line_ref.at[i], dlat_out.at[core, i], back_local.at[i])
+
+    def line_step(t):
+        @pl.when(t < lat_chunks)
+        def _():
+            dpair_copy(t).wait_recv()
+            line_ref[t] += dmine_ref[t] + dmid_ref[t] * here
+
+        r = t - LAG * chip
+
+        @pl.when((r >= 0) & (r < all_chunks))
+        def _():
+            @pl.when(has_left)
+            def _():
+                right_copy(r).wait_recv()
+                right_ref[r] += line_ref[r]
+
+            @pl.when(jnp.logical_not(has_left))
+            def _():
+                right_ref[r] = line_ref[r]
+
+            @pl.when(has_right)
+            def _():
+                right_copy(r).start()
+
+        u = t - LAG * (chips - 1 - chip)
+
+        @pl.when((u >= 0) & (u < all_chunks))
+        def _():
+            @pl.when(has_right)
+            def _():
+                left_copy(u).wait_recv()
+                left_ref[u] += line_ref[u]
+
+            @pl.when(jnp.logical_not(has_right))
+            def _():
+                left_ref[u] = line_ref[u]
+
+            @pl.when(has_left)
+            def _():
+                left_copy(u).start()
+
+        w = t - LAG * jnp.maximum(chip, chips - 1 - chip)
+
+        @pl.when((w >= 0) & (w < all_chunks))
+        def _():
+            line_ref[w] = right_ref[w] + left_ref[w] - line_ref[w]
+
+            @pl.when(w < lat_chunks)
+            def _():
+                back_copy(w).start()
+                back_keep(w).start()
+
+    def own_piece(h):
+        return line_ref.at[pl.ds(lat_chunks + h * half_chunks, kv_chunks)]
+
+    def spread_one(h):
+        return remote(
+            own_piece(h),
+            kv_out.at[core, stream, h],
+            spread_send.at[0, h],
+            spread_recv.at[0, h],
+            near[1 - h],
+        )
+
+    def spread_two(h, n):
+        block = (stream, first[1 - h])[n]
+        src = own_piece(h) if n == 0 else kv_out.at[core, block, h]
+        return remote(
+            src,
+            kv_out.at[core, block, h],
+            spread_send.at[1 + n, h],
+            spread_recv.at[1 + n, h],
+            near[h],
+        )
+
+    def spread_one_arrival(h):
+        place = kv_out.at[core, first[1 - h], h]
+        return remote(
+            place, place, spread_send.at[0, h], spread_recv.at[0, h], near[1 - h]
+        )
+
+    def spread_two_arrival(h, n):
+        place = kv_out.at[core, (first[h], flip_xy)[n], h]
+        return remote(place, place, spread_send.at[1 + n, h], spread_recv.at[1 + n, h], near[h])
+
+    def block_of(h, k):
+        return (stream, first[1 - h], first[h], flip_xy)[k]
+
+    def share_copy(h, k):
+        block = block_of(h, k)
+        src = own_piece(h) if k == 0 else kv_out.at[core, block, h]
+        return remote(
+            src, kv_out.at[core, block, h], share_send.at[h, k], share_recv.at[h, k], partner
+        )
+
+    def share_arrival(h, k):
+        place = kv_out.at[other, block_of(h, k), h]
+        return remote(place, place, share_send.at[h, k], share_recv.at[h, k], partner)
+
+    def kv_keep(h):
+        return pltpu.make_async_copy(own_piece(h), kv_out.at[core, stream, h], keep_local.at[h])
+
+    def query_piece(h):
+        return mine_ref.at[h, stream, pl.ds(kv_rows, q_rows)]
+
+    def query_copy(h):
+        return remote(
+            query_piece(h),
+            query_out.at[core, h],
+            query_send.at[h],
+            query_recv.at[h],
+            partner,
+        )
+
+    def query_arrival(h):
+        return remote(
+            query_piece(h),
+            query_out.at[other, h],
+            query_send.at[h],
+            query_recv.at[h],
+            partner,
+        )
+
+    def query_keep(h):
+        return pltpu.make_async_copy(query_piece(h), query_out.at[core, h], keep_local.at[2 + h])
+
+    def spread_event(h):
+        spread_one(h).start()
+        spread_two(h, 0).start()
+        share_copy(h, 0).start()
+        kv_keep(h).start()
+        flat = lat_chunks + h * half_chunks + kv_chunks
+        for k in range(0, q_rows, 16):
+            at = flat * ZROWS + kv_rows * 0 + k
+            chunk, row = at // ZROWS, at % ZROWS
+            mine_ref[h, stream, kv_rows + k : kv_rows + k + 16, :] = line_ref[
+                chunk, row : row + 16, :
+            ]
+        query_copy(h).start()
+        query_keep(h).start()
+        if h == 0:
+            at = flat * ZROWS + q_rows
+            chunk, row = at // ZROWS, at % ZROWS
+            small_out[...] = line_ref[chunk, row : row + 16, :]
+
+    tail = LAG * (chips - 1)
+    ready = lambda h: lat_chunks + (h + 1) * half_chunks - 1 + tail
+    events = {}
+
+    def at_tick(tick, run):
+        events.setdefault(tick, []).append(run)
+
+    parts = rows // token_step
+    for i in range(parts):
+        at_tick(TOKEN_TICKS[i % len(TOKEN_TICKS)], functools.partial(token_part, i))
+    at_tick(SMALL_TICK, small_start)
+    at_tick(PAIR_TICK, pair_event)
+    at_tick(ONE_TICK, one_event)
+    at_tick(TWO_TICK, two_event)
+    for sub in range(SUBS):
+        at_tick(WIDE_ONE_TICKS[sub], functools.partial(wide_event_one, sub))
+        at_tick(WIDE_TWO_TICKS[sub], functools.partial(wide_event_two, sub))
+    load.wait()
+    for copy in wide_loads:
+        copy.wait()
+
+    def step(t, carry):
+        line_step(t)
+        for tick in sorted(events):
+
+            @pl.when(t == tick)
+            def _(tick=tick):
+                for run in events[tick]:
+                    run()
+
+        return carry
+
+    lax.fori_loop(0, ready(0) + 1, step, 0)
+    spread_event(0)
+    lax.fori_loop(ready(0) + 1, ready(1) + 1, step, 0)
+    spread_event(1)
+    for sub in range(SUBS):
+        wide_event_three(sub)
+    for h in range(2):
+        spread_one_arrival(h).wait_recv()
+        spread_two(h, 1).start()
+        share_copy(h, 1).start()
+    for h in range(2):
+        for n in range(2):
+            spread_two_arrival(h, n).wait_recv()
+            share_copy(h, 2 + n).start()
+
+    def finish_lat(i, carry):
+        dpair_copy(i).wait_send()
+        back_copy(i).wait_send()
+        back_arrival(i).wait_recv()
+        back_keep(i).wait()
+        return carry
+
+    lax.fori_loop(0, lat_chunks, finish_lat, 0)
+
+    def finish_line(i, carry):
+        @pl.when(has_right)
+        def _():
+            right_copy(i).wait_send()
+
+        @pl.when(has_left)
+        def _():
+            left_copy(i).wait_send()
+
+        return carry
+
+    lax.fori_loop(0, all_chunks, finish_line, 0)
+    for copy in pairs:
+        copy.wait_send()
+    for h in range(2):
+        for n in range(2):
+            one_copy(h, n).wait_send()
+            spread_two(h, n).wait_send()
+        two_copy(h).wait_send()
+        spread_one(h).wait_send()
+        kv_keep(h).wait()
+        query_copy(h).wait_send()
+        query_arrival(h).wait_recv()
+        query_keep(h).wait()
+        for k in range(4):
+            share_copy(h, k).wait_send()
+            share_arrival(h, k).wait_recv()
+        for sub in range(SUBS):
+            for n in range(2):
+                wide_one_copy(h, n, sub).wait_send()
+                wide_core_copy(n, h, sub).wait_send()
+                wide_core_arrival(n, h, sub).wait_recv()
+            wide_two_copy(h, sub).wait_send()
+            wide_z_copy(h, sub).wait_send()
+            wide_keep(h, sub).wait()
+
+
+def gradients(dlat, dmid, latent, dwq, vec, dgain_q, place, tokens, tsort, dkv, gain_t, wk, wv):
+    rows, width = tokens.shape
+    half = dlat.shape[0] // 2
+    lat_chunks = half // ZROWS
+    wide_rows, wide_cols = latent.shape[1:]
+    share = width // 4
+    kv_rows, q_rows = share // 2, share // 4
+    block = kv_rows + q_rows + 16
+    all_chunks = lat_chunks + 2 * block // ZROWS
+    sds = jax.ShapeDtypeStruct
+    dma = pltpu.SemaphoreType.DMA
+    buf = lambda *shape: pltpu.VMEM(shape, F32)
+    both = lambda *shape: [dma(shape), dma(shape)]
+    return pl.pallas_call(
+        gradient_kernel,
+        name="gradients",
+        out_shape=(
+            sds((2, lat_chunks, ZROWS, width), F32),
+            sds((2, 2, wide_rows, wide_cols), F32),
+            sds((2, 4, 2, kv_rows // ZROWS, ZROWS, width), F32),
+            sds((2, 2, q_rows, width), F32),
+            sds((16, width), F32),
+            sds((rows, width), F32),
+        ),
+        in_specs=[anywhere(), vmem(), anywhere()] + [vmem()] * 10,
+        out_specs=(anywhere(),) * 4 + (vmem(),) * 2,
+        scratch_shapes=[
+            buf(all_chunks, ZROWS, width),
+            buf(all_chunks, ZROWS, width),
+            buf(all_chunks, ZROWS, width),
+            buf(lat_chunks, ZROWS, width),
+            buf(2, 2, wide_rows // 2, wide_cols),
+            buf(2, 2, wide_rows // 2, wide_cols),
+            buf(2, wide_rows // 2, wide_cols),
+            buf(2, 4, kv_rows, width),
+            buf(2, 4, block, width),
+            buf(2, 4, block, width),
+            buf(2, 2, block, width),
+            buf(2, block, width),
+            buf(4, 16, width),
+            dma,
+            dma((4,)),
+        ]
+        + both(lat_chunks)
+        + both(all_chunks)
+        + both(all_chunks)
+        + both(lat_chunks)
+        + [dma((lat_chunks,))]
+        + both(2, 2, SUBS)
+        + both(2, SUBS)
+        + both(2, SUBS)
+        + both(2, 2, SUBS)
+        + [dma((2, SUBS))]
+        + both(5)
+        + both(2, 2)
+        + both(2)
+        + both(3, 2)
+        + both(2, 4)
+        + both(2)
+        + [dma((4,))],
+        compiler_params=pltpu.CompilerParams(
+            vmem_limit_bytes=VMEM_BYTES, collective_id=2, has_side_effects=True
+        ),
+    )(
+        dlat.reshape(2, lat_chunks, ZROWS, width),
+        dmid.reshape(lat_chunks, ZROWS, width),
+        latent,
+        dwq.reshape(4, 2, 2, q_rows, width),
+        vec,
+        dgain_q,
+        place,
+        tokens,
+        tsort,
+        dkv,
+        gain_t.reshape(1, width),
+        wk,
+        wv,
+    )
+
+
 def local(
     latents,
     tokens,
@@ -892,61 +1537,57 @@
     result = result.reshape(latents.shape)
 
     core = lax.rem(tok_index, 2)
-    shares = 4
-    share = lax.rem(tok_index // 2, shares)
-    depth = width // shares
-    mine = lambda x: lax.dynamic_slice_in_dim(x, share * depth, depth, 1)
-    grad_up = jnp.einsum("rd,rf->df", mine(lefts[0]), rights[0], preferred_element_type=F32)
-    grad_down = jnp.einsum("rf,rd->df", rights[1], mine(lefts[1]), preferred_element_type=F32)
-    grad_out = jnp.einsum("re,rd->ed", mine(attended), lefts[2], preferred_element_type=F32)
-    both = jnp.concatenate((grad_up, grad_down), 0)
-    both = lax.psum_scatter(both, "stream", scatter_dimension=1, tiled=True)
-    grad_out = lax.psum_scatter(grad_out, "stream", scatter_dimension=1, tiled=True)
-    size = 2 * shares
-    groups = [list(range(g, g + size)) for g in range(0, members, size)]
-    both = lax.all_gather(both, "tok", axis_index_groups=groups)
-    both = both.reshape(shares, 2, 2 * depth, -1).sum(1)
-    grad_up = both[:, :depth].reshape(width, -1)
-    grad_down = both[:, depth:].reshape(width, -1).T
-    grad_out = lax.all_gather(grad_out, "tok", axis_index_groups=groups)
-    grad_out = grad_out.reshape(shares, 2, depth, -1).sum(1).reshape(width, -1)
-
-    dkey, dval, dlat, dgain_q, grad_query = attend_backward(
+    parity = lax.rem(tok_index // 2, 2)
+    half_rows = lefts.shape[1]
+    cols = w_up.shape[1] // streams // 2
+    rights = rights.reshape(2, half_rows, streams, 2, cols)
+    rights = lax.dynamic_index_in_dim(rights, parity, 3, keepdims=False)
+    attended = lax.dynamic_slice_in_dim(attended, parity * cols, cols, 1)
+    grad_out = jnp.einsum("rd,re->de", lefts[2], attended, preferred_element_type=F32)
+    grad_out = grad_out.reshape(streams, 2, -1, cols)
+
+    def part(which):
+        pick = lambda x: lax.dynamic_index_in_dim(x, which, 0, keepdims=False)
+        wide = jnp.einsum(
+            "rd,rsf->sdf", pick(lefts), pick(rights), preferred_element_type=F32
+        )
+        return jnp.concatenate(
+            (wide, lax.dynamic_index_in_dim(grad_out, which, 1, keepdims=False)), 1
+        )
+
+    swap = [(i, i ^ 1) for i in range(members)]
+    latent = part(core) + lax.ppermute(part(1 - core), "tok", swap)
+
+    dkv, dlat, dgain_q, dwq = attend_backward(
         bounds, latents, keys, values, query, normed, msg, gain_query, w_query
     )
-    d_tokens, dgain_t, grad_key, grad_value = token_backward(
-        place, tokens, tsort, dkey, dval, gain_token, w_key, w_value
+    d_latents, gather, kv, grad_query, small, d_tokens = gradients(
+        dlat, dmid, latent, dwq, vec, dgain_q, place, tokens, tsort, dkv, gain_token, w_key, w_value
     )
-    dlat = dlat.reshape(2, -1, width)
-    dlat = dlat.at[core].add(jnp.where(tok_index < 2, dmid, 0.0))
-    d_latents = lax.psum(dlat, "tok").reshape(latents.shape)
-    pairs = [[g, g + 1] for g in range(0, members, 2)]
-    vec = lax.psum(vec, "tok", axis_index_groups=pairs)
-    grad_bup, grad_bdown, grad_gmlp = vec[0], vec[1, :width], vec[2, :width]
-    grad_key, grad_value, grad_query, grad_gtoken, grad_gquery = lax.psum(
-        (grad_key, grad_value, grad_query, dgain_t[0], dgain_q[0]), ("stream", "tok")
-    )
-    grad_bup, grad_bdown, grad_gmlp = lax.psum((grad_bup, grad_bdown, grad_gmlp), "stream")
-
-    def own(x, axis):
-        size = x.shape[axis] // streams
-        return lax.dynamic_slice_in_dim(x, group_index * size, size, axis)
+    kv = kv.reshape(2, width, width)
+    grad_up = jnp.transpose(gather[0, :, :width], (1, 0, 2)).reshape(width, 2 * cols)
+    grad_down = jnp.transpose(gather[1, :, :width], (0, 2, 1)).reshape(2 * cols, width)
+    grad_out = jnp.transpose(gather[:, :, width:], (1, 3, 0, 2)).reshape(width, -1)
+
+    def own(x):
+        size = x.shape[0] // streams
+        return lax.dynamic_slice_in_dim(x, group_index * size, size, 0)
 
     return (
         result,
-        d_latents,
+        d_latents.reshape(latents.shape),
         d_tokens,
-        own(grad_gquery, 0),
-        own(grad_query, 1),
-        grad_gtoken,
-        grad_key,
-        grad_value,
+        own(small[1]),
+        grad_query.reshape(-1, width).T,
+        small[4],
+        kv[0],
+        kv[1],
         grad_out,
-        own(grad_gmlp, 0),
+        own(small[2]),
         grad_up,
-        own(grad_bup, 0),
+        small[0],
         grad_down,
-        own(grad_bdown, 0),
+        own(small[3]),
     )
 
 

time: 562 us -> 383 us (0.68)
  waiting for transfers between devices: 266 us -> 0.01 us
  Pallas kernels: 165 us -> 273 us
  blocking collectives: 57.3 us -> 0 us
  local copies, waits for them, and re-layouts: 33.7 us -> 85.6 us
  between operations: 15.6 us -> 1.02 us
  other arithmetic: 15.5 us -> 9.36 us
    psum x3 -> x0, waiting for transfers between devices: 233 us -> none  [the longest x1 169 us: local(): lax.psum((grad_key, grad_value, grad_query, dgain_t[0], dgain_q[0]), ('st...]
    pallas_call x2, Pallas kernels: 41.3 us -> 169 us  [the longest x1 146 us: gradients(): pl.pallas_call(gradient_kernel, name='gradients', out_shape=(sds((2, lat_...]
    psum x2 -> x0, blocking collectives: 57.3 us -> none  [the longest x1 39.9 us: local(): lax.psum((grad_key, grad_value, grad_query, dgain_t[0], dgain_q[0]), ('st...]
    reshape x0 -> x1, local copies, waits for them, and re-layouts: none -> 25.4 us  [local(): rights = rights.reshape(2, half_rows, streams, 2, cols)]
    dynamic_slice x5, local copies, waits for them, and re-layouts: 4.11 us -> 26.6 us  [the longest x3 25.3 us: part(): pick = lambda x: lax.dynamic_index_in_dim(x, which, 0, keepdims=False)]
    pallas_call x1, Pallas kernels: 93.4 us -> 74 us  [latent_block(): pl.pallas_call(latent_kernel, name='latent_block', out_shape=(sds((sample...]
    reduce_scatter x1 -> x0, waiting for transfers between devices: 17.2 us -> none  [local(): both = lax.psum_scatter(both, 'stream', scatter_dimension=1, tiled=True)]
    unnamed x8 -> x0, waiting for transfers between devices: 16.6 us -> none
  transfers between devices with their start and end apart: 7 -> 1, of which waited for: 4 -> 0; matrix products, arithmetic and copies ran while one was open for 6% -> 2% of each run, Pallas kernels for 7% -> 6%
where the time goes in v3:
time: 383 us; the launch traced here: 376 us
  Pallas kernels  273 us (71%)
  local copies, waits for them, and re-layouts  85.6 us (22%)
  other arithmetic  9.36 us (2%)
  matrix products  6.31 us (2%)
    pallas_call x1, Pallas kernels, gradients(): pl.pallas_call(gradient_kernel, name='gradients', out_shape=(sds((2, lat_...  146 us
    pallas_call x1, Pallas kernels, latent_block(): pl.pallas_call(latent_kernel, name='latent_block', out_shape=(sds((sample...  74 us
    pallas_call x1, Pallas kernels, attend_forward(): pl.pallas_call(forward_kernel, name='attend_forward', out_shape=(sds((sam...  29.9 us
    reshape x1, local copies, waits for them, and re-layouts, local(): rights = rights.reshape(2, half_rows, streams, 2, cols)  25.4 us
    dynamic_slice x3, local copies, waits for them, and re-layouts, part(): pick = lambda x: lax.dynamic_index_in_dim(x, which, 0, keepdims=False)  25.3 us
    pallas_call x1, Pallas kernels, attend_backward(): pl.pallas_call(backward_kernel, name='attend_backward', out_shape=(sds((2...  23.1 us
    unnamed x22, local copies, waits for them, and re-layouts  9.48 us
  transfers between devices with their start and end apart: 1, of which 0 were waited for; matrix products, arithmetic and copies ran while one was open for 2% of the time, Pallas kernels for 6%

profile of v3, /device:TPU:0, one launch (start us, length us, event | category | flops | bytes accessed | tf_op | source)
XLA Modules:
  0.0 375.8 jit_solution(2954386928613790883)
XLA Ops:
  0.7 1.3 reshape.105.gain_q_ref
  2.0 1.3 reshape.106.gain_t_ref
  3.2 1.3 reshape.109.gain_ref
  4.5 1.3 reshape.111.bdn_ref
  5.8 1.3 subtract_select_fusion
  7.1 29.9 %attend_forward.1 = (f32[8,4,208,128]{3,2,1,0:T(8,128)}, bf16[1280,768]{1,0:T(8,128)(2,1)}, bf16[1280,768]{1,0:T(8,128)(2,1)}, bf16[1024,768]{1,0:T(8,128)(2,1)}...) custom-call(s32[1,1024]{1,0:T(1,128)} %bitcast.85, ...), custom_call_target="tpu_custom_call" | custom-call | tf_op jit(solution)/shard_map/attend_forward/pallas_call | solution.py:208
  37.0 74.0 %latent_block.1 = (f32[8,800,128]{2,1,0:T(8,128)}, bf16[1024,768]{1,0:T(8,128)(2,1)}, f32[512,768]{1,0:T(8,128)}, bf16[3,512,768]{2,1,0:T(8,128)(2,1)}, bf16[2,5...) custom-call(f32[8,4,208,128]{3,2,1,0:T(8,128)} %get-tuple-element.39.part_ref, ...), custom_call_target="tpu_custom_call" | custom-call | tf_op jit(solution)/shard_map/latent_block/pallas_call | solution.py:741
  111.0 1.3 slice_bitcast_fusion.2
  113.1 1.1 dynamic-slice_bitcast_fusion.1
  114.2 25.4 %reshape.115 = bf16[2,512,4,2,384]{4,3,2,1,0:T(2,128)(2,1)} reshape(bf16[2,512,3072]{2,1,0:T(8,128)(2,1)} %get-tuple-element.49) | data formatting | bytes 12582912 | tf_op jit(solution)/shard_map/reshape | solution.py:1543
  139.6 11.0 %constant_dynamic-slice_fusion.4 = (bf16[1,512,4,1,384]{4,3,2,1,0:T(2,128)(2,1)S(1)}, bf16[1,512,4,1,384]{4,3,2,1,0:T(2,128)(2,1)}) fusion(bf16[2,512,4,2,384]{4,3,2,1,0:T(2,128)(2,1)} %reshape.115, s32[]{:T(128)S(6)} %select_n.46, s32[]{:T(128)S(6)} %select_n.49, s32[]{:T(128)S(6)} %select_n.53), kind=kLoop, calls=%fused_computation.29 | loop fusion | bytes 6291468 | tf_op jit(solution)/shard_map/jit(dynamic_index_in_dim)/dynamic_slice | solution.py:1550
  150.6 8.2 %copy.39 = bf16[1,512,4,1,384]{1,4,2,3,0:T(8,128)(2,1)} copy(bf16[1,512,4,1,384]{4,3,2,1,0:T(2,128)(2,1)} %get-tuple-element.81) | data formatting | bytes 3145728 | tf_op jit(solution)/shard_map/jit(dynamic_index_in_dim)/dynamic_slice | solution.py:1550
  158.8 3.1 convolution_bitcast_fusion
  161.9 2.7 pad_maximum_fusion
  165.0 6.1 %copy.36 = bf16[1,512,4,1,384]{1,4,2,3,0:T(8,128)(2,1)} copy(bf16[1,512,4,1,384]{4,3,2,1,0:T(2,128)(2,1)S(1)} %get-tuple-element.80) | data formatting | bytes 3145728 | tf_op jit(solution)/shard_map/jit(dynamic_index_in_dim)/dynamic_slice | solution.py:1550
  171.1 23.1 %attend_backward.1 = (bf16[2,1024,768]{2,1,0:T(8,128)(2,1)}, f32[1024,768]{1,0:T(8,128)}, f32[8,768]{1,0:T(8,128)}, f32[768,768]{1,0:T(8,128)}) custom-call(s32[16]{0:T(128)} %get-tuple-element.41.bounds_ref, bf16[1024,768]{1,0:T(8,128)(2,1)} %bitcast.70, bf16[1280,768]{1,0:T(8,128)(2,1)} %get-tuple-element.42.key_ref, ...), custom_call_target="tpu_custom_call" | custom-call | tf_op jit(solution)/shard_map/attend_backward/pallas_call | solution.py:344
  194.2 2.6 convolution_bitcast_fusion.1
  196.9 5.3 %maximum_add_fusion.latent_hbm = f32[4,864,384]{2,1,0:T(8,128)} fusion(f32[4,864,384]{2,1,0:T(8,128)} %collective-permute-done, f32[4,96,384]{2,1,0:T(8,128)S(1)} %copy-done.3, f32[4,768,384]{2,1,0:T(8,128)S(1)} %convolution_bitcast_fusion.1), kind=kLoop, calls=%fused_computation | loop fusion | flops 2654208 | bytes 15925248 | tf_op jit(solution)/shard_map/add | solution.py:1559
  202.2 146.2 %gradients.1 = (f32[2,16,32,768]{3,2,1,0:T(8,128)}, f32[2,2,864,384]{3,2,1,0:T(8,128)}, f32[2,4,2,3,32,768]{5,4,3,2,1,0:T(8,128)}, f32[2,2,48,768]{3,2,1,0:T(8,1...) custom-call(f32[2,16,32,768]{3,2,1,0:T(8,128)} %bitcast.73, f32[16,32,768]{2,1,0:T(8,128)} %bitcast.81, ...), custom_call_target="tpu_custom_call" | custom-call | tf_op jit(solution)/shard_map/gradients/pallas_call | solution.py:1439
  348.4 1.1 slice_bitcast_fusion.3
  349.5 4.1 %slice_bitcast_fusion = (f32[2,384,768]{1,2,0:T(8,128)S(1)}, f32[768,2,384]{2,0,1:T(8,128)}) fusion(f32[2,2,864,384]{3,2,1,0:T(8,128)} %get-tuple-element.63), kind=kLoop, calls=%fused_computation.2 | loop fusion | bytes 9437184 | tf_op jit(solution)/shard_map/transpose | solution.py:1569
  353.6 1.6 slice_reduce_fusion
  355.3 1.9 copy.43
  357.7 0.9 copy.48
  358.5 2.0 copy.42
  360.6 2.0 copy.44
  362.5 5.2 %fusion.12 = (f32[1,4,2,3,32,768]{5,4,3,2,1,0:T(8,128)}, f32[1,4,2,3,32,768]{5,4,3,2,1,0:T(8,128)}) fusion(f32[2,4,2,3,32,768]{5,4,3,2,1,0:T(8,128)} %get-tuple-element.62), kind=kLoop, calls=%fused_computation.30 | loop fusion | bytes 9437184 | tf_op jit(solution)/shard_map/slice | solution.py:1584
  369.0 1.1 copy.53
  370.1 1.7 copy.54
  371.8 1.4 copy-done.1
  373.2 1.7 copy.55
  374.8 0.8 copy.56
  (22 shorter events, 3.0 us)
Async XLA Ops:
  111.0 1.6 copy-start.7
  158.8 3.1 copy-start.4
  164.6 32.2 %collective-permute-start = (f32[4,864,384]{2,1,0:T(8,128)}, f32[4,864,384]{2,1,0:T(8,128)}, u32[]{:S(2)}, u32[]{:S(2)}) collective-permute-start(f32[4,864,384]{2,1,0:T(8,128)} %pad_maximum_fusion), channel_id=1, source_target_pairs={{0,1},{1,0},{2,3},{3,2},{4,5},{5,4},{6,7},{7,6},{8,9},{9,8},{10,11... | collective-permute-start | bytes 15925256 | tf_op jit(solution)/shard_map/ppermute | solution.py:1559
  171.1 23.1 %copy-start = (bf16[1,512,4,1,384]{1,4,2,3,0:T(8,128)(2,1)S(1)}, bf16[1,512,4,1,384]{1,4,2,3,0:T(8,128)(2,1)}, u32[]{:S(2)}) copy-start(bf16[1,512,4,1,384]{1,4,2,3,0:T(8,128)(2,1)} %copy.36) | copy-start | bytes 4718596
  194.2 2.7 copy-start.3
  362.5 6.5 %copy-start.5 = (bf16[1024,768]{1,0:T(8,128)(2,1)S(1)}, bf16[1024,768]{1,0:T(8,128)(2,1)}, u32[]{:S(2)}) copy-start(bf16[1024,768]{1,0:T(8,128)(2,1)} %get-tuple-element.40) | copy-start | bytes 4718596
  367.7 2.4 copy-start.2
  370.1 3.0 copy-start.1
  373.2 1.7 copy-start.6

commit v4 on v3

--- a/solution.py
+++ b/solution.py
@@ -17,13 +17,14 @@
 MSG_ROWS = HEADS * HEAD_DIM + 32
 BLOCK = 256
 LAG = 2
-TOKEN_TICKS = (1, 2, 3, 4, 5, 6, 7, 8)
-SMALL_TICK = 8
-PAIR_TICK = 9
-ONE_TICK = 12
-TWO_TICK = 15
-WIDE_ONE_TICKS = (7, 13)
-WIDE_TWO_TICKS = (11, 17)
+WIDE_START_TICKS = (0, 0, 0, 1)
+KV_TICKS = (2, 3)
+PAIR_TICK = 5
+ONE_TICK = 9
+TWO_TICK = 14
+WIDE_ONE_TICKS = (7, 12)
+WIDE_TWO_TICKS = (10, 17)
+TOKEN_TICKS = (4, 6, 6, 8, 8, 11, 11, 13)
 NEG = -1e30
 F32 = jnp.float32
 BF16 = jnp.bfloat16
@@ -49,12 +50,17 @@
     )
 
 
+def row(ref):
+    return ref[...].reshape(1, ref.shape[0])
+
+
 def piece_of(head):
     return head // PIECE_HEADS, head % PIECE_HEADS
 
 
 def forward_kernel(
-    ids_ref,
+    sample_ref,
+    mask_ref,
     tok_ref,
     lat_ref,
     gain_q_ref,
@@ -82,7 +88,8 @@
     lat_rows = 128
     step = 256
 
-    ids = ids_ref[...]
+    named = row(sample_ref) - lax.axis_index("stream") * samples
+    ids = jnp.where(row(mask_ref) == 1, named, -1)
     lane = lax.broadcasted_iota(jnp.int32, (samples, rows), 1)
     member = ids == lax.broadcasted_iota(jnp.int32, (samples, rows), 0)
     ones = jnp.where(member, 1.0, 0.0)
@@ -106,7 +113,7 @@
     def token_norm(i, carry):
         at = pl.ds(pl.multiple_of(i * step, step), step)
         unit, _ = norm_parts(tok_ref[at, :].astype(F32))
-        tnorm_ref[at, :] = (unit * gain_t_ref[...]).astype(BF16)
+        tnorm_ref[at, :] = (unit * row(gain_t_ref)).astype(BF16)
         return carry
 
     lax.fori_loop(0, rows // step, token_norm, 0)
@@ -129,7 +136,7 @@
     def sample_step(s, carry):
         at = pl.ds(pl.multiple_of(s * lat_rows, lat_rows), lat_rows)
         unit, _ = norm_parts(lat_ref[at, :].astype(F32))
-        normed = (unit * gain_q_ref[...]).astype(BF16)
+        normed = (unit * row(gain_q_ref)).astype(BF16)
         normed_ref[at, :] = normed
         query = dot(normed, wq_ref[...]) * 0.125
         turned = query.T.astype(BF16)
@@ -201,7 +208,7 @@
     return pl.BlockSpec(memory_space=pltpu.SMEM)
 
 
-def attend_forward(ids, tokens, latents, gain_q, wq, gain_t, wk, wv):
+def attend_forward(sample, mask, tokens, latents, gain_q, wq, gain_t, wk, wv):
     samples, lat_rows, width = latents.shape
     rows = tokens.shape[0]
     sds = jax.ShapeDtypeStruct
@@ -218,7 +225,7 @@
             sds((rows, 128), F32),
             sds((2 * samples,), jnp.int32),
         ),
-        in_specs=[vmem()] * 8,
+        in_specs=[vmem()] * 9,
         out_specs=(vmem(),) * 7 + (smem(),),
         scratch_shapes=[
             pltpu.VMEM((rows, width), BF16),
@@ -229,12 +236,13 @@
         ],
         compiler_params=pltpu.CompilerParams(vmem_limit_bytes=VMEM_BYTES),
     )(
-        ids.reshape(1, rows),
+        sample,
+        mask,
         tokens,
         latents.reshape(samples * lat_rows, width),
-        gain_q.reshape(1, width),
+        gain_q,
         wq,
-        gain_t.reshape(1, width),
+        gain_t,
         wk,
         wv,
     )
@@ -326,7 +334,7 @@
         unit, inv = norm_parts(lat_ref[at, :].astype(F32))
         dnormed = dot(dquery, wq_ref[...], (1, 1))
         dgain_ref[0:1, :] += jnp.sum(dnormed * unit, 0, keepdims=True)
-        dlat_ref[at, :] = norm_back(unit, inv, gain_q_ref[...], dnormed)
+        dlat_ref[at, :] = norm_back(unit, inv, row(gain_q_ref), dnormed)
         return carry
 
     lax.fori_loop(0, samples, sample_step, 0)
@@ -369,7 +377,7 @@
         query,
         normed,
         msg,
-        gain_q.reshape(1, width),
+        gain_q,
         wq,
     )
 
@@ -401,7 +409,7 @@
 
 
 def latent_kernel(
-    part_ref,
+    part_hbm,
     drop_ref,
     lat_ref,
     cot_ref,
@@ -416,7 +424,7 @@
     dmid_ref,
     a_ref,
     b_ref,
-    att_ref,
+    side_ref,
     vec_ref,
     wo_ref,
     wup_ref,
@@ -433,6 +441,23 @@
     mid_ref,
     acc_ref,
     dacc_ref,
+    hn_ref,
+    dm_ref,
+    da_ref,
+    att_ref,
+    hn_out,
+    hn_in,
+    half_out,
+    half_in,
+    side_all,
+    side_in,
+    hn_send,
+    hn_recv,
+    half_send,
+    half_recv,
+    side_send,
+    side_recv,
+    own_sem,
     weight_sem,
     pair_send,
     pair_recv,
@@ -445,7 +470,7 @@
     res_send,
     res_recv,
 ):
-    samples = part_ref.shape[0]
+    samples = msg_ref.shape[0]
     half = samples // 2
     lat_rows = 128
     width = lat_ref.shape[1]
@@ -455,11 +480,13 @@
     chips = lax.axis_size("tok") // 2
     core = lax.rem(tok, 2)
     chip = lax.div(tok, 2)
+    parity = lax.rem(chip, 2)
     partner = (stream, tok + 1 - 2 * core)
     right = (stream, tok + 2)
     left = (stream, tok - 2)
     has_right = chip < chips - 1
     has_left = chip > 0
+    on_first = core == 0
 
     barrier = pltpu.get_barrier_semaphore()
     pl.semaphore_signal(barrier, inc=1, device_id=partner, device_id_type=MESH)
@@ -472,6 +499,10 @@
     def _():
         pl.semaphore_signal(barrier, inc=1, device_id=left, device_id_type=MESH)
 
+    own_load = pltpu.make_async_copy(
+        part_hbm.at[pl.ds(core * chunks, chunks)], own_ref, own_sem
+    )
+    own_load.start()
     weights = [
         pltpu.make_async_copy(src, dst, weight_sem.at[i])
         for i, (src, dst) in enumerate(((wo_hbm, wo_ref), (wup_hbm, wup_ref), (wdn_hbm, wdn_ref)))
@@ -483,9 +514,8 @@
     )
 
     def pair_copy(i):
-        j, q = lax.div(i, PIECES), lax.rem(i, PIECES)
         return pltpu.make_async_remote_copy(
-            src_ref=part_ref.at[(1 - core) * half + j, q],
+            src_ref=part_hbm.at[(1 - core) * chunks + i],
             dst_ref=pair_ref.at[i],
             send_sem=pair_send.at[i],
             recv_sem=pair_recv.at[i],
@@ -545,13 +575,43 @@
             device_id_type=MESH,
         )
 
+    def hn_copy(j):
+        return pltpu.make_async_remote_copy(
+            src_ref=hn_out.at[j],
+            dst_ref=hn_in.at[j],
+            send_sem=hn_send.at[j],
+            recv_sem=hn_recv.at[j],
+            device_id=partner,
+            device_id_type=MESH,
+        )
+
+    def half_copy(i):
+        return pltpu.make_async_remote_copy(
+            src_ref=half_out.at[i],
+            dst_ref=half_in.at[i],
+            send_sem=half_send.at[i],
+            recv_sem=half_recv.at[i],
+            device_id=partner,
+            device_id_type=MESH,
+        )
+
+    side_copy = pltpu.make_async_remote_copy(
+        src_ref=side_all.at[:, 1 - core],
+        dst_ref=side_in,
+        send_sem=side_send,
+        recv_sem=side_recv,
+        device_id=partner,
+        device_id_type=MESH,
+    )
+
     def start_pair(i, carry):
         pair_copy(i).start()
         return carry
 
     lax.fori_loop(0, chunks, start_pair, 0)
-
-    drop = drop_ref[...].astype(F32)
+    own_load.wait()
+
+    drop = row(drop_ref).astype(F32)
     scale_all = drop * drop.shape[1] / jnp.sum(drop, 1, keepdims=True)
     drop_lane = lax.broadcasted_iota(jnp.int32, drop.shape, 1)
     vec_ref[...] = jnp.zeros_like(vec_ref)
@@ -574,26 +634,38 @@
                     at, i * HEAD_DIM : (i + 1) * HEAD_DIM, :
                 ] * (1.0 / den)
             att = att_t_ref[...].T.astype(BF16)
-            att_ref[mine, :] = att
+            att_ref[mine, :] = jnp.where(parity == 0, att[:, : width // 2], att[:, width // 2 :])
             mid = lat_ref[rows, :].astype(F32) + scale * dot(att, wo_ref[...])
             mid_ref[...] = mid
             unit, _ = norm_parts(mid)
-            a_ref[0, mine, :] = (unit * gain_ref[...]).astype(BF16)
+            hn = (unit * row(gain_ref)).astype(BF16)
             dm = (scale * cot_ref[rows, :].astype(F32)).astype(BF16)
-            a_ref[1, mine, :] = dm
+            hn_ref[...] = hn
+            dm_ref[...] = dm
+            a_ref[rows, :] = jnp.where(on_first, hn, dm)
+
+            @pl.when(jnp.logical_not(on_first))
+            def _():
+                hn_out[j] = hn.astype(F32)
+                hn_copy(j).start()
+
             vec_ref[1:2, :width] += jnp.sum(dm.astype(F32), 0, keepdims=True)
-            acc_ref[...] = jnp.broadcast_to(bdn_ref[...], acc_ref.shape)
+            acc_ref[...] = jnp.broadcast_to(row(bdn_ref), acc_ref.shape)
             dacc_ref[...] = jnp.zeros_like(dacc_ref)
 
         span = wup_ref.shape[1] // PIECES
         cols = pl.ds(pl.multiple_of(q * span, 128), span)
-        pre = dot(a_ref[0, mine, :], wup_ref[:, cols]) + bup_ref[:, cols]
+        pre = dot(hn_ref[...], wup_ref[:, cols]) + bup_ref[cols].reshape(1, span)
         active, slope = gelu_parts(pre)
         hidden = active.astype(BF16)
-        b_ref[1, mine, cols] = hidden
         acc_ref[...] += dot(hidden, wdn_ref[cols, :])
-        dpre = (slope * dot(a_ref[1, mine, :], wdn_ref[cols, :], (1, 1))).astype(BF16)
-        b_ref[0, mine, cols] = dpre
+        dpre = (slope * dot(dm_ref[...], wdn_ref[cols, :], (1, 1))).astype(BF16)
+        piece = j * PIECES + q
+        near_half = lambda x: jnp.where(parity == 0, x[:, : span // 2], x[:, span // 2 :])
+        hidden_half, dpre_half = near_half(hidden), near_half(dpre)
+        b_ref[q, rows, :] = jnp.where(on_first, dpre_half, hidden_half)
+        half_out[piece] = jnp.where(on_first, hidden_half, dpre_half).astype(F32)
+        half_copy(piece).start()
         vec_ref[0:1, cols] += jnp.sum(dpre.astype(F32), 0, keepdims=True)
         dacc_ref[...] += dot(dpre, wup_ref[:, cols], (1, 1))
 
@@ -607,10 +679,10 @@
             unit, inv = norm_parts(mid)
             dhn = dacc_ref[...]
             vec_ref[2:3, :width] += jnp.sum(dhn * unit, 0, keepdims=True)
-            dmid = cot_ref[rows, :].astype(F32) + norm_back(unit, inv, gain_ref[...], dhn)
+            dmid = cot_ref[rows, :].astype(F32) + norm_back(unit, inv, row(gain_ref), dhn)
             dmid_ref[mine, :] = dmid
             da = (scale * dmid).astype(BF16)
-            a_ref[2, mine, :] = da
+            da_ref[mine, :] = da
             datt_t = dot(wo_ref[...], da, (1, 1)).astype(BF16).astype(F32)
             msg_ref[sample, width:, :] = jnp.zeros((MSG_ROWS - width, lat_rows), F32)
             for h in range(HEADS):
@@ -631,8 +703,7 @@
         @pl.when(t < chunks)
         def _():
             pair_copy(t).wait_recv()
-            j, q = lax.div(t, PIECES), lax.rem(t, PIECES)
-            merge(part_ref.at[core * half + j, q], pair_ref.at[t], own_ref.at[t])
+            merge(own_ref.at[t], pair_ref.at[t], own_ref.at[t])
 
         r = t - LAG * chip
 
@@ -698,8 +769,21 @@
 
     lax.fori_loop(0, chunks + LAG * (chips - 1) + PIECES - 1, step, 0)
 
+    share = width // 8
+    for block in range(4):
+        at = slice(block * 2 * share, (block + 1) * 2 * share)
+        product = dot(da_ref[:, at], att_ref[...], (0, 0))
+        side_all[block, 0] = product[:share]
+        side_all[block, 1] = product[share:]
+    side_copy.start()
+
     def finish_chunk(i, carry):
         pair_copy(i).wait_send()
+        half_copy(i).wait_send()
+        half_copy(i).wait_recv()
+        at = ((1 - core) * half + lax.div(i, PIECES)) * lat_rows
+        rows = pl.ds(pl.multiple_of(at, lat_rows), lat_rows)
+        b_ref[lax.rem(i, PIECES), rows, :] = half_in[i].astype(BF16)
 
         @pl.when(has_right)
         def _():
@@ -718,12 +802,28 @@
         other = (1 - core) * half + j
         rows = pl.ds(pl.multiple_of(other * lat_rows, lat_rows), lat_rows)
         res_ref[rows, :] = res_in[j].astype(BF16)
+
+        @pl.when(on_first)
+        def _():
+            hn_copy(j).wait_recv()
+            a_ref[rows, :] = hn_in[j].astype(BF16)
+
+        @pl.when(jnp.logical_not(on_first))
+        def _():
+            hn_copy(j).wait_send()
+            scale = jnp.sum(
+                jnp.where(drop_lane == stream * samples + other, scale_all, 0.0), 1, keepdims=True
+            )
+            a_ref[rows, :] = (scale * cot_ref[rows, :].astype(F32)).astype(BF16)
+
         res_copy(j).wait_send()
         msg_copy(j).wait_send()
         msg_arrival(j).wait_recv()
         return carry
 
     lax.fori_loop(0, half, finish_sample, 0)
+    side_copy.wait()
+    side_ref[...] = side_all[:, core] + side_in[...]
 
 
 def anywhere():
@@ -745,13 +845,13 @@
             sds((samples, MSG_ROWS, lat_rows), F32),
             sds((samples * lat_rows, width), BF16),
             sds((half * lat_rows, width), F32),
-            sds((3, half * lat_rows, width), BF16),
-            sds((2, half * lat_rows, hidden), BF16),
-            sds((half * lat_rows, width), BF16),
+            sds((samples * lat_rows, width), BF16),
+            sds((PIECES, samples * lat_rows, hidden // PIECES // 2), BF16),
+            sds((4, width // 8, width // 2), F32),
             sds((8, hidden), F32),
         ),
         in_specs=[
-            vmem(),
+            anywhere(),
             vmem(),
             vmem(),
             vmem(),
@@ -779,6 +879,23 @@
             pltpu.VMEM((lat_rows, width), F32),
             pltpu.VMEM((lat_rows, width), F32),
             pltpu.VMEM((lat_rows, width), F32),
+            pltpu.VMEM((lat_rows, width), BF16),
+            pltpu.VMEM((lat_rows, width), BF16),
+            pltpu.VMEM((half * lat_rows, width), BF16),
+            pltpu.VMEM((half * lat_rows, width // 2), BF16),
+            pltpu.VMEM((half, lat_rows, width), F32),
+            pltpu.VMEM((half, lat_rows, width), F32),
+            pltpu.VMEM((chunks, lat_rows, hidden // PIECES // 2), F32),
+            pltpu.VMEM((chunks, lat_rows, hidden // PIECES // 2), F32),
+            pltpu.VMEM((4, 2, width // 8, width // 2), F32),
+            pltpu.VMEM((4, width // 8, width // 2), F32),
+            dma((half,)),
+            dma((half,)),
+            dma((chunks,)),
+            dma((chunks,)),
+            dma,
+            dma,
+            dma,
             dma((3,)),
             dma((chunks,)),
             dma((chunks,)),
@@ -795,16 +912,16 @@
             vmem_limit_bytes=VMEM_BYTES, collective_id=1, has_side_effects=True
         ),
     )(
-        part,
-        drop_mask.reshape(1, -1),
+        part.reshape(samples * PIECES, PIECE_ROWS, lat_rows),
+        drop_mask,
         latents.reshape(samples * lat_rows, width),
         cotangent.reshape(samples * lat_rows, width),
         wo,
-        gain.reshape(1, width),
+        gain,
         wup,
-        bup.reshape(1, hidden),
+        bup,
         wdn,
-        bdn.reshape(1, width),
+        bdn,
     )
 
 
@@ -815,7 +932,9 @@
 def gradient_kernel(
     dlat_hbm,
     dmid_ref,
-    latent_hbm,
+    a_ref,
+    b_ref,
+    side_ref,
     dwq_ref,
     vec_ref,
     dgain_q_ref,
@@ -845,8 +964,8 @@
     one_ref,
     two_ref,
     small_ref,
+    gain_ref,
     load_sem,
-    wide_load_sem,
     dpair_send,
     dpair_recv,
     right_send,
@@ -888,7 +1007,7 @@
     mix = kv_rows + q_rows
     half_chunks = (all_chunks - lat_chunks) // 2
     kv_chunks = kv_rows // ZROWS
-    wide_half = wide_ref.shape[2]
+    wide_half = wide_ref.shape[1] // 2
     sub_rows = wide_half // SUBS
 
     stream = lax.axis_index("stream")
@@ -934,16 +1053,6 @@
 
     load = pltpu.make_async_copy(dlat_hbm.at[core], dmine_ref, load_sem)
     load.start()
-    wide_loads = []
-    for h in range(2):
-        for n, block in enumerate((stream, first[1 - h])):
-            copy = pltpu.make_async_copy(
-                latent_hbm.at[block, pl.ds(h * wide_half, wide_half)],
-                wide_ref.at[h, n],
-                wide_load_sem.at[2 * h + n],
-            )
-            copy.start()
-            wide_loads.append(copy)
     pl.semaphore_wait(barrier, 3 + has_right.astype(jnp.int32) + has_left.astype(jnp.int32))
 
     def dpair_copy(i):
@@ -961,17 +1070,20 @@
         block = (first[h], flip_xy)[n]
         at = pl.ds(h * wide_half + sub * sub_rows, sub_rows)
         return remote(
-            latent_hbm.at[block, at],
+            wide_ref.at[block, at],
             wide_one.at[h, n, pl.ds(sub * sub_rows, sub_rows)],
             wide_one_send.at[h, n, sub],
             wide_one_recv.at[h, n, sub],
             near[h],
         )
 
+    def wide_at(block, h, sub):
+        return wide_ref.at[block, pl.ds(h * wide_half + sub * sub_rows, sub_rows)]
+
     def wide_two_copy(h, sub):
         at = pl.ds(sub * sub_rows, sub_rows)
         return remote(
-            wide_ref.at[h, 1, at],
+            wide_at(first[1 - h], h, sub),
             wide_two.at[h, at],
             wide_two_send.at[h, sub],
             wide_two_recv.at[h, sub],
@@ -983,7 +1095,7 @@
 
     def wide_z_copy(h, sub):
         return remote(
-            wide_ref.at[h, 0, pl.ds(sub * sub_rows, sub_rows)],
+            wide_at(stream, h, sub),
             gather_at(core, parity, h, sub),
             wide_z_send.at[h, sub],
             wide_z_recv.at[h, sub],
@@ -992,7 +1104,7 @@
 
     def wide_z_arrival(h, sub):
         return remote(
-            wide_ref.at[h, 0, pl.ds(sub * sub_rows, sub_rows)],
+            wide_at(stream, h, sub),
             gather_at(core, 1 - parity, h, sub),
             wide_z_send.at[h, sub],
             wide_z_recv.at[h, sub],
@@ -1004,7 +1116,7 @@
             src = gather_at(core, 1 - parity, h, sub)
             dst = gather_at(core, 1 - parity, h, sub)
         else:
-            src = wide_ref.at[h, 0, pl.ds(sub * sub_rows, sub_rows)]
+            src = wide_at(stream, h, sub)
             dst = gather_at(core, parity, h, sub)
         return remote(
             src, dst, wide_core_send.at[far, h, sub], wide_core_recv.at[far, h, sub], partner
@@ -1018,30 +1130,41 @@
 
     def wide_keep(h, sub):
         return pltpu.make_async_copy(
-            wide_ref.at[h, 0, pl.ds(sub * sub_rows, sub_rows)],
+            wide_at(stream, h, sub),
             gather_at(core, parity, h, sub),
             wide_local.at[h, sub],
         )
 
-    for sub in range(SUBS):
-        for h in range(2):
-            for n in range(2):
-                wide_one_copy(h, n, sub).start()
+    def wide_product(block):
+        wide_ref[block, :width, :] = dot(a_ref[...], b_ref[block], (0, 0))
+        wide_ref[block, width:, :] = side_ref[block]
+
+    def wide_start(k):
+        wide_product((flip_xy, first[0], first[1], stream)[k])
+        if k < 3:
+            for sub in range(SUBS):
+                for h in range(2):
+                    if k == 0:
+                        wide_one_copy(h, 1, sub).start()
+                    elif k == 1 + h:
+                        wide_one_copy(h, 0, sub).start()
 
     def wide_event_one(sub):
         at = slice(sub * sub_rows, (sub + 1) * sub_rows)
         for h in range(2):
             for n in range(2):
                 wide_one_copy(h, n, sub).wait_recv()
-            wide_ref[h, 1, at, :] += wide_one[h, 1, at, :]
+            span = pl.ds(h * wide_half + sub * sub_rows, sub_rows)
+            wide_ref[first[1 - h], span, :] += wide_one[h, 1, at, :]
             wide_two_copy(h, sub).start()
-            wide_ref[h, 0, at, :] += wide_one[h, 0, at, :]
+            wide_ref[stream, span, :] += wide_one[h, 0, at, :]
 
     def wide_event_two(sub):
         at = slice(sub * sub_rows, (sub + 1) * sub_rows)
         for h in range(2):
             wide_two_copy(h, sub).wait_recv()
-            wide_ref[h, 0, at, :] += wide_two[h, at, :]
+            span = pl.ds(h * wide_half + sub * sub_rows, sub_rows)
+            wide_ref[stream, span, :] += wide_two[h, at, :]
             wide_z_copy(h, sub).start()
             wide_core_copy(0, h, sub).start()
             wide_keep(h, sub).start()
@@ -1051,13 +1174,26 @@
             wide_z_arrival(h, sub).wait_recv()
             wide_core_copy(1, h, sub).start()
 
-    turned = tsort_ref[...].T
     share = width // 4
-    for block in range(4):
+
+    def gain_part(which, block, product):
         at = slice(block * share, (block + 1) * share)
-        product = dot(turned[at], dkv_ref[other])
-        for h in range(2):
-            send_ref[h, block] = product[h * kv_rows : (h + 1) * kv_rows]
+        weight = jnp.where(which == 0, wk_ref[at, :], wv_ref[at, :]).astype(F32)
+        gain_ref[at, 0:1] += jnp.sum(product * weight, 1, keepdims=True)
+
+    def token_product(block, which):
+        at = slice(block * share, (block + 1) * share)
+        return dot(tsort_ref[:, at], dkv_ref[which], (0, 0))
+
+    def token_other():
+        gain_ref[...] = jnp.zeros_like(gain_ref)
+        for block in range(4):
+            product = token_product(block, other)
+            for h in range(2):
+                send_ref[h, block] = product[h * kv_rows : (h + 1) * kv_rows]
+            gain_part(other, block, product)
+        for copy in pairs[:4]:
+            copy.start()
 
     def pair_copies():
         out = []
@@ -1092,22 +1228,29 @@
         return out
 
     pairs = pair_copies()
-    for copy in pairs[:4]:
-        copy.start()
-
-    for block in range(4):
-        at = slice(block * share, (block + 1) * share)
-        product = dot(turned[at], dkv_ref[core])
-        for h in range(2):
-            piece = product[h * kv_rows : (h + 1) * kv_rows]
-            mine_ref[h, block, :kv_rows, :] = piece
-            mine_ref[h, block, kv_rows:mix, :] = dwq_ref[block, core, h]
-    mine_ref[1, :, mix:, :] = jnp.zeros((4, 16, width), F32)
+
+    def token_own():
+        for block in range(4):
+            product = token_product(block, core)
+            for h in range(2):
+                piece = product[h * kv_rows : (h + 1) * kv_rows]
+                mine_ref[h, block, :kv_rows, :] = piece
+                mine_ref[h, block, kv_rows:mix, :] = dwq_ref[block, core, h]
+            gain_part(core, block, product)
+        mine_ref[1, :, mix:, :] = jnp.zeros((4, 16, width), F32)
+        small_ref[...] = jnp.zeros_like(small_ref)
+        gain = jnp.broadcast_to(gain_ref[:, 0:1], gain_ref.shape).T[0:1, :] / row(gain_t_ref)
+        for block in range(4):
+            small_ref[block, 0:1, :] = vec_ref[0:1, block * width : (block + 1) * width] * here
+            small_ref[block, 1:2, :] = dgain_q_ref[0:1, :]
+            small_ref[block, 2:3, :] = vec_ref[2:3, :width] * here
+            small_ref[block, 3:4, :] = vec_ref[1:2, :width] * here
+            small_ref[block, 4:5, :] = gain
+        pairs[4].start()
 
     here = (chip == 0).astype(F32)
 
     token_step = 128
-    small_ref[...] = jnp.zeros_like(small_ref)
 
     def token_part(i):
         at = pl.ds(pl.multiple_of(i * token_step, token_step), token_step)
@@ -1117,18 +1260,7 @@
         dval = dot(pick, dkv_ref[1]).astype(BF16)
         dnormed = dot(dkey, wk_ref[...], (1, 1)) + dot(dval, wv_ref[...], (1, 1))
         unit, inv = norm_parts(tok_ref[at, :].astype(F32))
-        small_ref[0, 4:5, :] += jnp.sum(dnormed * unit, 0, keepdims=True)
-        dtok_ref[at, :] = norm_back(unit, inv, gain_t_ref[...], dnormed)
-
-    def small_start():
-        for block in range(4):
-            small_ref[block, 0:1, :] = vec_ref[0:1, block * width : (block + 1) * width] * here
-            small_ref[block, 1:2, :] = dgain_q_ref[0:1, :]
-            small_ref[block, 2:3, :] = vec_ref[2:3, :width] * here
-            small_ref[block, 3:4, :] = vec_ref[1:2, :width] * here
-            if block:
-                small_ref[block, 4:5, :] = small_ref[0, 4:5, :]
-        pairs[4].start()
+        dtok_ref[at, :] = norm_back(unit, inv, row(gain_t_ref), dnormed)
 
     def one_copy(h, n):
         block = (first[h], flip_xy)[n]
@@ -1340,7 +1472,10 @@
     parts = rows // token_step
     for i in range(parts):
         at_tick(TOKEN_TICKS[i % len(TOKEN_TICKS)], functools.partial(token_part, i))
-    at_tick(SMALL_TICK, small_start)
+    for k in range(4):
+        at_tick(WIDE_START_TICKS[k], functools.partial(wide_start, k))
+    at_tick(KV_TICKS[0], token_other)
+    at_tick(KV_TICKS[1], token_own)
     at_tick(PAIR_TICK, pair_event)
     at_tick(ONE_TICK, one_event)
     at_tick(TWO_TICK, two_event)
@@ -1348,8 +1483,6 @@
         at_tick(WIDE_ONE_TICKS[sub], functools.partial(wide_event_one, sub))
         at_tick(WIDE_TWO_TICKS[sub], functools.partial(wide_event_two, sub))
     load.wait()
-    for copy in wide_loads:
-        copy.wait()
 
     def step(t, carry):
         line_step(t)
@@ -1423,11 +1556,13 @@
             wide_keep(h, sub).wait()
 
 
-def gradients(dlat, dmid, latent, dwq, vec, dgain_q, place, tokens, tsort, dkv, gain_t, wk, wv):
+def gradients(
+    dlat, dmid, a, b, side, dwq, vec, dgain_q, place, tokens, tsort, dkv, gain_t, wk, wv
+):
     rows, width = tokens.shape
     half = dlat.shape[0] // 2
     lat_chunks = half // ZROWS
-    wide_rows, wide_cols = latent.shape[1:]
+    wide_rows, wide_cols = a.shape[1] + side.shape[1], b.shape[2]
     share = width // 4
     kv_rows, q_rows = share // 2, share // 4
     block = kv_rows + q_rows + 16
@@ -1447,14 +1582,14 @@
             sds((16, width), F32),
             sds((rows, width), F32),
         ),
-        in_specs=[anywhere(), vmem(), anywhere()] + [vmem()] * 10,
+        in_specs=[anywhere()] + [vmem()] * 14,
         out_specs=(anywhere(),) * 4 + (vmem(),) * 2,
         scratch_shapes=[
             buf(all_chunks, ZROWS, width),
             buf(all_chunks, ZROWS, width),
             buf(all_chunks, ZROWS, width),
             buf(lat_chunks, ZROWS, width),
-            buf(2, 2, wide_rows // 2, wide_cols),
+            buf(4, wide_rows, wide_cols),
             buf(2, 2, wide_rows // 2, wide_cols),
             buf(2, wide_rows // 2, wide_cols),
             buf(2, 4, kv_rows, width),
@@ -1463,8 +1598,8 @@
             buf(2, 2, block, width),
             buf(2, block, width),
             buf(4, 16, width),
+            buf(width, 128),
             dma,
-            dma((4,)),
         ]
         + both(lat_chunks)
         + both(all_chunks)
@@ -1489,7 +1624,9 @@
     )(
         dlat.reshape(2, lat_chunks, ZROWS, width),
         dmid.reshape(lat_chunks, ZROWS, width),
-        latent,
+        a,
+        b,
+        side,
         dwq.reshape(4, 2, 2, q_rows, width),
         vec,
         dgain_q,
@@ -1497,10 +1634,105 @@
         tokens,
         tsort,
         dkv,
-        gain_t.reshape(1, width),
+        gain_t,
         wk,
         wv,
     )
+
+
+def closing_kernel(
+    dlat_hbm,
+    gather_hbm,
+    kv_hbm,
+    query_ref,
+    small_ref,
+    dtok_hbm,
+    dlat_out,
+    dtok_out,
+    up_out,
+    key_out,
+    val_out,
+    down_ref,
+    out_ref,
+    wq_ref,
+    gain_q_ref,
+    gain_t_ref,
+    gain_mlp_ref,
+    bup_ref,
+    bdn_ref,
+    wide_ref,
+    side_ref,
+    sems,
+):
+    width = small_ref.shape[1]
+    cols = wide_ref.shape[2]
+    moves = [
+        (gather_hbm.at[1], wide_ref),
+        (gather_hbm.at[0, :, pl.ds(width, side_ref.shape[1])], side_ref),
+        (kv_hbm.at[0], key_out),
+        (kv_hbm.at[1], val_out),
+        (dlat_hbm, dlat_out),
+        (dtok_hbm, dtok_out),
+    ]
+    for e in range(2):
+        moves.append((gather_hbm.at[0, e, pl.ds(0, width)], up_out.at[:, pl.ds(e * cols, cols)]))
+    copies = [pltpu.make_async_copy(a, b, sems.at[i]) for i, (a, b) in enumerate(moves)]
+    for copy in copies:
+        copy.start()
+    stream = lax.axis_index("stream")
+    gain_t_ref[...] = small_ref[4]
+    bup_ref[...] = small_ref[0]
+    size = gain_q_ref.shape[0]
+    for i, ref in ((1, gain_q_ref), (2, gain_mlp_ref), (3, bdn_ref)):
+        line = small_ref[i : i + 1, :]
+        piece = line[:, :size]
+        for k in range(1, width // size):
+            piece = jnp.where(stream == k, line[:, k * size : (k + 1) * size], piece)
+        ref[...] = piece[0]
+    wq_ref[...] = query_ref[...].T
+    copies[0].wait()
+    copies[1].wait()
+    for e in range(2):
+        span = slice(e * cols, (e + 1) * cols)
+        down_ref[span, :] = wide_ref[e, :width, :].T
+        out_ref[span, :] = jnp.concatenate((side_ref[e], wide_ref[e, width:, :]), 0).T
+    for copy in copies[2:]:
+        copy.wait()
+
+
+def closing(dlat, gather, kv, query, small, dtok):
+    width = small.shape[1]
+    wide_rows, cols = gather.shape[2:]
+    share = query.shape[0]
+    rows = dtok.shape[0]
+    sds = lambda *shape: jax.ShapeDtypeStruct(shape, F32)
+    return pl.pallas_call(
+        closing_kernel,
+        name="closing",
+        out_shape=(
+            sds(*dlat.shape),
+            sds(rows, width),
+            sds(width, 2 * cols),
+            sds(width, width),
+            sds(width, width),
+            sds(2 * cols, width),
+            sds(width, share),
+            sds(width, share),
+            sds(share),
+            sds(width),
+            sds(share),
+            sds(2 * cols),
+            sds(share),
+        ),
+        in_specs=[anywhere()] * 3 + [vmem()] * 2 + [anywhere()],
+        out_specs=(anywhere(),) * 5 + (vmem(),) * 8,
+        scratch_shapes=[
+            pltpu.VMEM((2, wide_rows, cols), F32),
+            pltpu.VMEM((2, wide_rows - width, cols), F32),
+            pltpu.SemaphoreType.DMA((8,)),
+        ],
+        compiler_params=pltpu.CompilerParams(vmem_limit_bytes=VMEM_BYTES),
+    )(dlat, gather, kv, query, small, dtok)
 
 
 def local(
@@ -1523,71 +1755,56 @@
     cotangent,
 ):
     samples, lat_rows, width = latents.shape
-    group_index = lax.axis_index("stream")
-    tok_index = lax.axis_index("tok")
-    streams = lax.axis_size("stream")
-    members = lax.axis_size("tok")
-    ids = jnp.where(token_mask == 1, token_sample - group_index * samples, -1)
     part, keys, values, tsort, query, normed, place, bounds = attend_forward(
-        ids, tokens, latents, gain_query, w_query, gain_token, w_key, w_value
+        token_sample, token_mask, tokens, latents, gain_query, w_query, gain_token, w_key, w_value
     )
-    msg, result, dmid, lefts, rights, attended, vec = latent_block(
+    msg, result, dmid, a, b, side, vec = latent_block(
         part, drop_mask, latents, cotangent, w_out, gain_mlp, w_up, b_up, w_down, b_down
     )
-    result = result.reshape(latents.shape)
-
-    core = lax.rem(tok_index, 2)
-    parity = lax.rem(tok_index // 2, 2)
-    half_rows = lefts.shape[1]
-    cols = w_up.shape[1] // streams // 2
-    rights = rights.reshape(2, half_rows, streams, 2, cols)
-    rights = lax.dynamic_index_in_dim(rights, parity, 3, keepdims=False)
-    attended = lax.dynamic_slice_in_dim(attended, parity * cols, cols, 1)
-    grad_out = jnp.einsum("rd,re->de", lefts[2], attended, preferred_element_type=F32)
-    grad_out = grad_out.reshape(streams, 2, -1, cols)
-
-    def part(which):
-        pick = lambda x: lax.dynamic_index_in_dim(x, which, 0, keepdims=False)
-        wide = jnp.einsum(
-            "rd,rsf->sdf", pick(lefts), pick(rights), preferred_element_type=F32
-        )
-        return jnp.concatenate(
-            (wide, lax.dynamic_index_in_dim(grad_out, which, 1, keepdims=False)), 1
-        )
-
-    swap = [(i, i ^ 1) for i in range(members)]
-    latent = part(core) + lax.ppermute(part(1 - core), "tok", swap)
-
     dkv, dlat, dgain_q, dwq = attend_backward(
         bounds, latents, keys, values, query, normed, msg, gain_query, w_query
     )
-    d_latents, gather, kv, grad_query, small, d_tokens = gradients(
-        dlat, dmid, latent, dwq, vec, dgain_q, place, tokens, tsort, dkv, gain_token, w_key, w_value
+    dlat, gather, kv, dwq, small, d_tokens = gradients(
+        dlat, dmid, a, b, side, dwq, vec, dgain_q, place, tokens, tsort, dkv, gain_token,
+        w_key, w_value,
     )
-    kv = kv.reshape(2, width, width)
-    grad_up = jnp.transpose(gather[0, :, :width], (1, 0, 2)).reshape(width, 2 * cols)
-    grad_down = jnp.transpose(gather[1, :, :width], (0, 2, 1)).reshape(2 * cols, width)
-    grad_out = jnp.transpose(gather[:, :, width:], (1, 3, 0, 2)).reshape(width, -1)
-
-    def own(x):
-        size = x.shape[0] // streams
-        return lax.dynamic_slice_in_dim(x, group_index * size, size, 0)
-
+    (
+        d_latents,
+        d_tokens,
+        grad_up,
+        grad_key,
+        grad_value,
+        grad_down,
+        grad_out,
+        grad_query,
+        grad_gquery,
+        grad_gtoken,
+        grad_gmlp,
+        grad_bup,
+        grad_bdown,
+    ) = closing(
+        dlat.reshape(samples * lat_rows, width),
+        gather,
+        kv.reshape(2, width, width),
+        dwq.reshape(-1, width),
+        small,
+        d_tokens,
+    )
     return (
-        result,
+        result.reshape(latents.shape),
         d_latents.reshape(latents.shape),
         d_tokens,
-        own(small[1]),
-        grad_query.reshape(-1, width).T,
-        small[4],
-        kv[0],
-        kv[1],
+        grad_gquery,
+        grad_query,
+        grad_gtoken,
+        grad_key,
+        grad_value,
         grad_out,
-        own(small[2]),
+        grad_gmlp,
         grad_up,
-        small[0],
+        grad_bup,
         grad_down,
-        own(small[3]),
+        grad_bdown,
     )
 
 

time: 383 us -> 721 us (1.88)
  Pallas kernels: 273 us -> 711 us
  local copies, waits for them, and re-layouts: 85.6 us -> 5.66 us
  other arithmetic: 9.36 us -> 0 us
    pallas_call x0 -> x1, Pallas kernels: none -> 409 us  [closing(): pl.pallas_call(closing_kernel, name='closing', out_shape=(sds(*dlat.shape...]
    reshape x5 -> x0, local copies, waits for them, and re-layouts: 30.4 us -> none  [the longest x1 25.4 us: local(): rights = rights.reshape(2, half_rows, streams, 2, cols)]
    pallas_call x1, Pallas kernels: 146 us -> 174 us  [gradients(): pl.pallas_call(gradient_kernel, name='gradients', out_shape=(sds((2, lat_...]
    dynamic_slice x5 -> x0, local copies, waits for them, and re-layouts: 26.6 us -> none  [the longest x3 25.3 us: part(): pick = lambda x: lax.dynamic_index_in_dim(x, which, 0, keepdims=False)]
    transpose x5 -> x0, local copies, waits for them, and re-layouts: 9.68 us -> none  [the longest x2 6.08 us: local(): jnp.transpose(gather[1, :, :width], (0, 2, 1)).reshape(2 * cols, width)]
  transfers between devices with their start and end apart: 1 -> 0, of which waited for: 0 -> 0; matrix products, arithmetic and copies ran while one was open for 2% -> 0% of each run, Pallas kernels for 6% -> 0%
where the time goes in v4:
time: 721 us; the launch traced here: 718 us
  Pallas kernels  711 us (99%)
    pallas_call x1, Pallas kernels, closing(): pl.pallas_call(closing_kernel, name='closing', out_shape=(sds(*dlat.shape...  409 us
    pallas_call x1, Pallas kernels, gradients(): pl.pallas_call(gradient_kernel, name='gradients', out_shape=(sds((2, lat_...  174 us
    pallas_call x1, Pallas kernels, latent_block(): pl.pallas_call(latent_kernel, name='latent_block', out_shape=(sds((sample...  78.7 us
    pallas_call x1, Pallas kernels, attend_forward(): pl.pallas_call(forward_kernel, name='attend_forward', out_shape=(sds((sam...  28.2 us
    pallas_call x1, Pallas kernels, attend_backward(): pl.pallas_call(backward_kernel, name='attend_backward', out_shape=(sds((2...  21.4 us

profile of v4, /device:TPU:0, one launch (start us, length us, event | category | flops | bytes accessed | tf_op | source)
XLA Modules:
  0.0 717.7 jit_solution(16604015794274294684)
XLA Ops:
  0.6 28.2 %attend_forward.1 = (f32[8,4,208,128]{3,2,1,0:T(8,128)}, bf16[1280,768]{1,0:T(8,128)(2,1)}, bf16[1280,768]{1,0:T(8,128)(2,1)}, bf16[1024,768]{1,0:T(8,128)(2,1)}...) custom-call(s32[1024]{0:T(1024)} %sample_ref.1, ...), custom_call_target="tpu_custom_call" | custom-call | tf_op jit(solution)/shard_map/attend_forward/pallas_call | solution.py:215
  28.8 78.7 %latent_block.1 = (f32[8,800,128]{2,1,0:T(8,128)}, bf16[1024,768]{1,0:T(8,128)(2,1)}, f32[512,768]{1,0:T(8,128)}, bf16[1024,768]{1,0:T(8,128)(2,1)}, bf16[4,1024...) custom-call(f32[32,208,128]{2,1,0:T(8,128)} %bitcast.15, s32[32]{0:T(128)} %drop_ref.1, ...), custom_call_target="tpu_custom_call" | custom-call | tf_op jit(solution)/shard_map/latent_block/pallas_call | solution.py:841
  107.6 21.4 %attend_backward.1 = (bf16[2,1024,768]{2,1,0:T(8,128)(2,1)}, f32[1024,768]{1,0:T(8,128)}, f32[8,768]{1,0:T(8,128)}, f32[768,768]{1,0:T(8,128)}) custom-call(s32[16]{0:T(128)} %get-tuple-element.54.bounds_ref, bf16[1024,768]{1,0:T(8,128)(2,1)} %bitcast.13, bf16[1280,768]{1,0:T(8,128)(2,1)} %get-tuple-element.55.key_ref, ...), custom_call_target="tpu_custom_call" | custom-call | tf_op jit(solution)/shard_map/attend_backward/pallas_call | solution.py:352
  129.0 173.7 %gradients.1 = (f32[2,16,32,768]{3,2,1,0:T(8,128)}, f32[2,2,864,384]{3,2,1,0:T(8,128)}, f32[2,4,2,3,32,768]{5,4,3,2,1,0:T(8,128)}, f32[2,2,48,768]{3,2,1,0:T(8,1...) custom-call(f32[2,16,32,768]{3,2,1,0:T(8,128)} %bitcast.17, f32[16,32,768]{2,1,0:T(8,128)} %bitcast.20, ...), custom_call_target="tpu_custom_call" | custom-call | tf_op jit(solution)/shard_map/gradients/pallas_call | solution.py:1574
  302.7 409.2 %closing.1 = (f32[1024,768]{1,0:T(8,128)}, f32[1024,768]{1,0:T(8,128)}, f32[768,768]{1,0:T(8,128)}, f32[768,768]{1,0:T(8,128)}, f32[768,768]{1,0:T(8,128)}, /*in...) custom-call(f32[1024,768]{1,0:T(8,128)} %bitcast.16, ...), custom_call_target="tpu_custom_call" | custom-call | tf_op jit(solution)/shard_map/closing/pallas_call | solution.py:1709
  711.9 0.0 copy-start
  711.9 2.3 copy.31
  714.2 2.2 copy.32
  716.4 0.0 copy-done
  716.4 1.1 copy.34
Async XLA Ops:
  711.9 4.5 copy-start

commit v5 on v4

--- a/solution.py
+++ b/solution.py
@@ -17,14 +17,20 @@
 MSG_ROWS = HEADS * HEAD_DIM + 32
 BLOCK = 256
 LAG = 2
-WIDE_START_TICKS = (0, 0, 0, 1)
-KV_TICKS = (2, 3)
+GAP = 6
+SUBS = 3
+EARLY_SUBS = 1
+SPREAD_LAG = 3
+WIDE_START_TICKS = (1, 2, 2, 4)
+KV_TICKS = (0, 3)
 PAIR_TICK = 5
-ONE_TICK = 9
-TWO_TICK = 14
-WIDE_ONE_TICKS = (7, 12)
-WIDE_TWO_TICKS = (10, 17)
-TOKEN_TICKS = (4, 6, 6, 8, 8, 11, 11, 13)
+MORE_TICK = 21
+ONE_TICK = 15
+TWO_TICK = 20
+WIDE_ONE_TICKS = (10, 27, 30)
+WIDE_TWO_TICKS = (16, 32, 35)
+WIDE_THREE_TICKS = (25, -1, -1)
+TOKEN_TICKS = (6, 7, 8, 9, 11, 12, 13, 16)
 NEG = -1e30
 F32 = jnp.float32
 BF16 = jnp.bfloat16
@@ -256,18 +262,23 @@
     query_ref,
     normed_ref,
     msg_ref,
+    dmid_ref,
     gain_q_ref,
     wq_ref,
+    res_hbm,
     dkv_ref,
     dlat_ref,
     dgain_ref,
     dwq_ref,
+    res_out,
     dk_ref,
     dv_ref,
     grad_ref,
     dquery_ref,
     turn_ref,
     stat_ref,
+    res_ref,
+    res_sems,
 ):
     samples = query_ref.shape[0]
     rows = dkv_ref.shape[1]
@@ -277,6 +288,10 @@
     for r in range(0, rows + BLOCK, step):
         dk_ref[r : r + step, :] = jnp.zeros((step, dk_ref.shape[1]), F32)
         dv_ref[r : r + step, :] = jnp.zeros((step, dv_ref.shape[1]), F32)
+    res_load = pltpu.make_async_copy(res_hbm, res_ref, res_sems.at[0])
+    res_store = pltpu.make_async_copy(res_ref, res_out, res_sems.at[1])
+    res_load.start()
+    member = lax.axis_index("tok")
     grad_ref[...] = jnp.zeros_like(grad_ref)
     dgain_ref[...] = jnp.zeros_like(dgain_ref)
 
@@ -334,18 +349,29 @@
         unit, inv = norm_parts(lat_ref[at, :].astype(F32))
         dnormed = dot(dquery, wq_ref[...], (1, 1))
         dgain_ref[0:1, :] += jnp.sum(dnormed * unit, 0, keepdims=True)
-        dlat_ref[at, :] = norm_back(unit, inv, row(gain_q_ref), dnormed)
+        dlat = norm_back(unit, inv, row(gain_q_ref), dnormed)
+        dlat_ref[at, :] = dlat
+        j = s - lax.rem(member, 2) * (samples // 2)
+
+        @pl.when((member < 2) & (j >= 0) & (j < samples // 2))
+        def _():
+            mine = pl.ds(pl.multiple_of(j * lat_rows, lat_rows), lat_rows)
+            dlat_ref[at, :] = dlat + dmid_ref[mine, :]
+
         return carry
 
     lax.fori_loop(0, samples, sample_step, 0)
+    res_load.wait()
+    res_store.start()
     for r in range(0, rows, step):
         dkv_ref[0, r : r + step, :] = dk_ref[r : r + step, :].astype(BF16)
         dkv_ref[1, r : r + step, :] = dv_ref[r : r + step, :].astype(BF16)
     for c in range(0, width, 256):
         dwq_ref[c : c + 256, :] = dot(dquery_ref[:, c : c + 256], normed_ref[...], (0, 0))
-
-
-def attend_backward(bounds, latents, keys, values, query, normed, msg, gain_q, wq):
+    res_store.wait()
+
+
+def attend_backward(bounds, latents, keys, values, query, normed, msg, dmid, gain_q, wq, result):
     samples, lat_rows, width = latents.shape
     rows = keys.shape[0] - BLOCK
     sds = jax.ShapeDtypeStruct
@@ -357,9 +383,10 @@
             sds((samples * lat_rows, width), F32),
             sds((8, width), F32),
             sds((width, width), F32),
+            sds(result.shape, BF16),
         ),
-        in_specs=[smem()] + [vmem()] * 8,
-        out_specs=(vmem(),) * 4,
+        in_specs=[smem()] + [vmem()] * 9 + [anywhere()],
+        out_specs=(vmem(),) * 4 + (anywhere(),),
         scratch_shapes=[
             pltpu.VMEM((rows + BLOCK, width), F32),
             pltpu.VMEM((rows + BLOCK, width), F32),
@@ -367,6 +394,8 @@
             pltpu.VMEM((samples * lat_rows, width), BF16),
             pltpu.VMEM((width, lat_rows), F32),
             pltpu.VMEM((16, 2 * lat_rows), F32),
+            pltpu.VMEM(result.shape, BF16),
+            pltpu.SemaphoreType.DMA((2,)),
         ],
         compiler_params=pltpu.CompilerParams(vmem_limit_bytes=VMEM_BYTES),
     )(
@@ -377,8 +406,10 @@
         query,
         normed,
         msg,
+        dmid,
         gain_q,
         wq,
+        result,
     )
 
 
@@ -926,22 +957,20 @@
 
 
 ZROWS = 32
-SUBS = 2
 
 
 def gradient_kernel(
     dlat_hbm,
-    dmid_ref,
-    a_ref,
-    b_ref,
+    a_hbm,
+    b_hbm,
     side_ref,
-    dwq_ref,
+    dwq_hbm,
     vec_ref,
     dgain_q_ref,
     place_ref,
-    tok_ref,
-    tsort_ref,
-    dkv_ref,
+    tok_hbm,
+    tsort_hbm,
+    dkv_hbm,
     gain_t_ref,
     wk_ref,
     wv_ref,
@@ -950,7 +979,7 @@
     kv_out,
     query_out,
     small_out,
-    dtok_ref,
+    dtok_out,
     line_ref,
     right_ref,
     left_ref,
@@ -965,6 +994,16 @@
     two_ref,
     small_ref,
     gain_ref,
+    wide_far,
+    spread_ref,
+    stage_ref,
+    stage_sem,
+    a_ref,
+    b_ref,
+    dwq_ref,
+    tok_ref,
+    tsort_ref,
+    dkv_ref,
     load_sem,
     dpair_send,
     dpair_recv,
@@ -996,10 +1035,10 @@
     share_recv,
     query_send,
     query_recv,
+    query_local,
     keep_local,
 ):
-    width = tok_ref.shape[1]
-    rows = tok_ref.shape[0]
+    rows, width = tok_ref.shape
     lat_chunks = dmine_ref.shape[0]
     all_chunks = line_ref.shape[0]
     kv_rows = send_ref.shape[2]
@@ -1051,8 +1090,22 @@
             device_id_type=MESH,
         )
 
-    load = pltpu.make_async_copy(dlat_hbm.at[core], dmine_ref, load_sem)
-    load.start()
+    pulls = [
+        pltpu.make_async_copy(src, dst, load_sem.at[i])
+        for i, (src, dst) in enumerate(
+            (
+                (tsort_hbm, tsort_ref),
+                (dkv_hbm, dkv_ref),
+                (dlat_hbm.at[core], dmine_ref),
+                (a_hbm, a_ref),
+                (b_hbm, b_ref),
+                (dwq_hbm, dwq_ref),
+                (tok_hbm, tok_ref),
+            )
+        )
+    ]
+    for copy in pulls:
+        copy.start()
     pl.semaphore_wait(barrier, 3 + has_right.astype(jnp.int32) + has_left.astype(jnp.int32))
 
     def dpair_copy(i):
@@ -1093,27 +1146,21 @@
     def gather_at(c, e, h, sub):
         return gather_out.at[c, e, pl.ds(h * wide_half + sub * sub_rows, sub_rows)]
 
+    def far_at(h, sub):
+        return wide_far.at[pl.ds(h * wide_half + sub * sub_rows, sub_rows)]
+
     def wide_z_copy(h, sub):
         return remote(
             wide_at(stream, h, sub),
-            gather_at(core, parity, h, sub),
+            far_at(h, sub),
             wide_z_send.at[h, sub],
             wide_z_recv.at[h, sub],
             beside,
         )
 
-    def wide_z_arrival(h, sub):
-        return remote(
-            wide_at(stream, h, sub),
-            gather_at(core, 1 - parity, h, sub),
-            wide_z_send.at[h, sub],
-            wide_z_recv.at[h, sub],
-            beside,
-        )
-
     def wide_core_copy(far, h, sub):
         if far:
-            src = gather_at(core, 1 - parity, h, sub)
+            src = far_at(h, sub)
             dst = gather_at(core, 1 - parity, h, sub)
         else:
             src = wide_at(stream, h, sub)
@@ -1128,11 +1175,11 @@
             place, place, wide_core_send.at[far, h, sub], wide_core_recv.at[far, h, sub], partner
         )
 
-    def wide_keep(h, sub):
+    def wide_keep(far, h, sub):
         return pltpu.make_async_copy(
-            wide_at(stream, h, sub),
-            gather_at(core, parity, h, sub),
-            wide_local.at[h, sub],
+            far_at(h, sub) if far else wide_at(stream, h, sub),
+            gather_at(core, 1 - parity if far else parity, h, sub),
+            wide_local.at[far, h, sub],
         )
 
     def wide_product(block):
@@ -1141,13 +1188,18 @@
 
     def wide_start(k):
         wide_product((flip_xy, first[0], first[1], stream)[k])
-        if k < 3:
-            for sub in range(SUBS):
-                for h in range(2):
-                    if k == 0:
-                        wide_one_copy(h, 1, sub).start()
-                    elif k == 1 + h:
-                        wide_one_copy(h, 0, sub).start()
+        for sub in range(EARLY_SUBS):
+            for h in range(2):
+                if k == 0:
+                    wide_one_copy(h, 1, sub).start()
+                elif k == 1 + h:
+                    wide_one_copy(h, 0, sub).start()
+
+    def wide_more():
+        for sub in range(EARLY_SUBS, SUBS):
+            for h in range(2):
+                for n in range(2):
+                    wide_one_copy(h, 1 - n, sub).start()
 
     def wide_event_one(sub):
         at = slice(sub * sub_rows, (sub + 1) * sub_rows)
@@ -1167,12 +1219,13 @@
             wide_ref[stream, span, :] += wide_two[h, at, :]
             wide_z_copy(h, sub).start()
             wide_core_copy(0, h, sub).start()
-            wide_keep(h, sub).start()
+            wide_keep(0, h, sub).start()
 
     def wide_event_three(sub):
         for h in range(2):
-            wide_z_arrival(h, sub).wait_recv()
+            wide_z_copy(h, sub).wait_recv()
             wide_core_copy(1, h, sub).start()
+            wide_keep(1, h, sub).start()
 
     share = width // 4
 
@@ -1192,42 +1245,28 @@
             for h in range(2):
                 send_ref[h, block] = product[h * kv_rows : (h + 1) * kv_rows]
             gain_part(other, block, product)
-        for copy in pairs[:4]:
-            copy.start()
-
-    def pair_copies():
-        out = []
-        for h in range(2):
-            out.append(
-                remote(
-                    send_ref.at[h],
-                    pair_ref.at[h, :, pl.ds(0, kv_rows)],
-                    pair_send.at[h],
-                    pair_recv.at[h],
-                    partner,
-                )
-            )
-            out.append(
-                remote(
-                    dwq_ref.at[:, other, h],
-                    pair_ref.at[h, :, pl.ds(kv_rows, q_rows)],
-                    pair_send.at[2 + h],
-                    pair_recv.at[2 + h],
-                    partner,
-                )
-            )
-        out.append(
-            remote(
-                small_ref,
-                pair_ref.at[0, :, pl.ds(mix, 16)],
-                pair_send.at[4],
-                pair_recv.at[4],
-                partner,
-            )
-        )
-        return out
-
-    pairs = pair_copies()
+        for k, h, what in pairs:
+            if what < 2:
+                pair_copy(k, h, what).start()
+
+    order = (flip_xy, first[0], first[1], stream)
+
+    def pair_copy(k, h, what):
+        block = order[k]
+        src, at, size = (
+            (send_ref.at[h, block], 0, kv_rows),
+            (dwq_ref.at[block, other, h], kv_rows, q_rows),
+            (small_ref.at[block], mix, 16),
+        )[what]
+        return remote(
+            src,
+            pair_ref.at[h, block, pl.ds(at, size)],
+            pair_send.at[k, h, what],
+            pair_recv.at[k, h, what],
+            partner,
+        )
+
+    pairs = [(k, h, what) for k in range(4) for h in range(2) for what in range(3 - h)]
 
     def token_own():
         for block in range(4):
@@ -1246,11 +1285,19 @@
             small_ref[block, 2:3, :] = vec_ref[2:3, :width] * here
             small_ref[block, 3:4, :] = vec_ref[1:2, :width] * here
             small_ref[block, 4:5, :] = gain
-        pairs[4].start()
+        for k in range(4):
+            pair_copy(k, 0, 2).start()
 
     here = (chip == 0).astype(F32)
 
     token_step = 128
+
+    def stage_copy(i):
+        return pltpu.make_async_copy(
+            stage_ref.at[i % 2],
+            dtok_out.at[pl.ds(i * token_step, token_step)],
+            stage_sem.at[i % 2],
+        )
 
     def token_part(i):
         at = pl.ds(pl.multiple_of(i * token_step, token_step), token_step)
@@ -1260,7 +1307,10 @@
         dval = dot(pick, dkv_ref[1]).astype(BF16)
         dnormed = dot(dkey, wk_ref[...], (1, 1)) + dot(dval, wv_ref[...], (1, 1))
         unit, inv = norm_parts(tok_ref[at, :].astype(F32))
-        dtok_ref[at, :] = norm_back(unit, inv, row(gain_t_ref), dnormed)
+        if i >= 2:
+            stage_copy(i - 2).wait()
+        stage_ref[i % 2] = norm_back(unit, inv, row(gain_t_ref), dnormed)
+        stage_copy(i).start()
 
     def one_copy(h, n):
         block = (first[h], flip_xy)[n]
@@ -1274,16 +1324,18 @@
         )
 
     def pair_event():
-        for copy in pairs:
-            copy.wait_recv()
-        for h in range(2):
-            for block in range(4):
+        for k in range(4):
+            block = order[k]
+            for h in range(2):
+                for what in range(3 - h):
+                    pair_copy(k, h, what).wait_recv()
                 mine_ref[h, block, :mix, :] += pair_ref[h, block, :mix, :]
                 if h == 0:
                     mine_ref[h, block, mix:, :] = small_ref[block] + pair_ref[h, block, mix:, :]
-        for h in range(2):
-            for n in range(2):
-                one_copy(h, n).start()
+                if k == 0:
+                    one_copy(h, 1).start()
+                elif k == 1 + h:
+                    one_copy(h, 0).start()
 
     def one_event():
         for h in range(2):
@@ -1318,15 +1370,20 @@
     def back_keep(i):
         return pltpu.make_async_copy(line_ref.at[i], dlat_out.at[core, i], back_local.at[i])
 
+    def placed(t):
+        late = t >= lat_chunks + GAP
+        index = jnp.where(late, t - GAP, t)
+        return index, (t >= 0) & (late | (t < lat_chunks)) & (index < all_chunks)
+
     def line_step(t):
         @pl.when(t < lat_chunks)
         def _():
             dpair_copy(t).wait_recv()
-            line_ref[t] += dmine_ref[t] + dmid_ref[t] * here
-
-        r = t - LAG * chip
-
-        @pl.when((r >= 0) & (r < all_chunks))
+            line_ref[t] += dmine_ref[t]
+
+        r, r_due = placed(t - LAG * chip)
+
+        @pl.when(r_due)
         def _():
             @pl.when(has_left)
             def _():
@@ -1341,9 +1398,9 @@
             def _():
                 right_copy(r).start()
 
-        u = t - LAG * (chips - 1 - chip)
-
-        @pl.when((u >= 0) & (u < all_chunks))
+        u, u_due = placed(t - LAG * (chips - 1 - chip))
+
+        @pl.when(u_due)
         def _():
             @pl.when(has_right)
             def _():
@@ -1358,9 +1415,9 @@
             def _():
                 left_copy(u).start()
 
-        w = t - LAG * jnp.maximum(chip, chips - 1 - chip)
-
-        @pl.when((w >= 0) & (w < all_chunks))
+        w, w_due = placed(t - LAG * jnp.maximum(chip, chips - 1 - chip))
+
+        @pl.when(w_due)
         def _():
             line_ref[w] = right_ref[w] + left_ref[w] - line_ref[w]
 
@@ -1369,55 +1426,95 @@
                 back_copy(w).start()
                 back_keep(w).start()
 
-    def own_piece(h):
-        return line_ref.at[pl.ds(lat_chunks + h * half_chunks, kv_chunks)]
-
-    def spread_one(h):
+    def spot(i):
+        k = i - lat_chunks
+        h = lax.div(k, half_chunks)
+        return h, lax.rem(k, half_chunks)
+
+    def by_half(h, pair):
+        return jnp.where(h == 0, pair[0], pair[1])
+
+    def block_of(h, k):
+        return (stream, by_half(h, (flip_y, flip_x)), by_half(h, first), flip_xy)[k]
+
+    def spread_src(i, k):
+        h, c = spot(i)
+        return line_ref.at[i] if k == 0 else spread_ref.at[k - 1, h, c]
+
+    def spread_copy(i, k):
+        h, c = spot(i)
+        target = by_half(h, (flip_y, flip_x)) if k == 1 else by_half(h, first)
         return remote(
-            own_piece(h),
-            kv_out.at[core, stream, h],
-            spread_send.at[0, h],
-            spread_recv.at[0, h],
-            near[1 - h],
-        )
-
-    def spread_two(h, n):
-        block = (stream, first[1 - h])[n]
-        src = own_piece(h) if n == 0 else kv_out.at[core, block, h]
+            spread_src(i, 1 if k == 3 else 0),
+            spread_ref.at[k - 1, h, c],
+            spread_send.at[k - 1, i - lat_chunks],
+            spread_recv.at[k - 1, i - lat_chunks],
+            (target, tok),
+        )
+
+    def share_copy(i, k):
+        h, c = spot(i)
         return remote(
-            src,
-            kv_out.at[core, block, h],
-            spread_send.at[1 + n, h],
-            spread_recv.at[1 + n, h],
-            near[h],
-        )
-
-    def spread_one_arrival(h):
-        place = kv_out.at[core, first[1 - h], h]
+            spread_src(i, k),
+            kv_out.at[core, block_of(h, k), h, c],
+            share_send.at[k, i - lat_chunks],
+            share_recv.at[k, i - lat_chunks],
+            partner,
+        )
+
+    def share_arrival(i, k):
+        h, c = spot(i)
+        place = kv_out.at[other, block_of(h, k), h, c]
         return remote(
-            place, place, spread_send.at[0, h], spread_recv.at[0, h], near[1 - h]
-        )
-
-    def spread_two_arrival(h, n):
-        place = kv_out.at[core, (first[h], flip_xy)[n], h]
-        return remote(place, place, spread_send.at[1 + n, h], spread_recv.at[1 + n, h], near[h])
-
-    def block_of(h, k):
-        return (stream, first[1 - h], first[h], flip_xy)[k]
-
-    def share_copy(h, k):
-        block = block_of(h, k)
-        src = own_piece(h) if k == 0 else kv_out.at[core, block, h]
-        return remote(
-            src, kv_out.at[core, block, h], share_send.at[h, k], share_recv.at[h, k], partner
-        )
-
-    def share_arrival(h, k):
-        place = kv_out.at[other, block_of(h, k), h]
-        return remote(place, place, share_send.at[h, k], share_recv.at[h, k], partner)
-
-    def kv_keep(h):
-        return pltpu.make_async_copy(own_piece(h), kv_out.at[core, stream, h], keep_local.at[h])
+            place,
+            place,
+            share_send.at[k, i - lat_chunks],
+            share_recv.at[k, i - lat_chunks],
+            partner,
+        )
+
+    def kv_keep(i, k):
+        h, c = spot(i)
+        return pltpu.make_async_copy(
+            spread_src(i, k),
+            kv_out.at[core, block_of(h, k), h, c],
+            keep_local.at[k, i - lat_chunks],
+        )
+
+    def spread_due(t):
+        i, due = placed(t)
+        i = jnp.maximum(i, lat_chunks)
+        _, c = spot(i)
+        return i, due & (t >= lat_chunks + GAP) & (c < kv_chunks)
+
+    def spread_step(t):
+        lag = LAG * jnp.maximum(chip, chips - 1 - chip)
+        i, due = spread_due(t - lag)
+
+        @pl.when(due)
+        def _():
+            spread_copy(i, 1).start()
+            spread_copy(i, 2).start()
+            share_copy(i, 0).start()
+            kv_keep(i, 0).start()
+
+        j, due_one = spread_due(t - lag - SPREAD_LAG)
+
+        @pl.when(due_one)
+        def _():
+            spread_copy(j, 1).wait_recv()
+            spread_copy(j, 3).start()
+            share_copy(j, 1).start()
+            kv_keep(j, 1).start()
+
+        m, due_two = spread_due(t - lag - 2 * SPREAD_LAG)
+
+        @pl.when(due_two)
+        def _():
+            for k in (2, 3):
+                spread_copy(m, k).wait_recv()
+                share_copy(m, k).start()
+                kv_keep(m, k).start()
 
     def query_piece(h):
         return mine_ref.at[h, stream, pl.ds(kv_rows, q_rows)]
@@ -1441,16 +1538,12 @@
         )
 
     def query_keep(h):
-        return pltpu.make_async_copy(query_piece(h), query_out.at[core, h], keep_local.at[2 + h])
-
-    def spread_event(h):
-        spread_one(h).start()
-        spread_two(h, 0).start()
-        share_copy(h, 0).start()
-        kv_keep(h).start()
+        return pltpu.make_async_copy(query_piece(h), query_out.at[core, h], query_local.at[h])
+
+    def query_event(h):
         flat = lat_chunks + h * half_chunks + kv_chunks
         for k in range(0, q_rows, 16):
-            at = flat * ZROWS + kv_rows * 0 + k
+            at = flat * ZROWS + k
             chunk, row = at // ZROWS, at % ZROWS
             mine_ref[h, stream, kv_rows + k : kv_rows + k + 16, :] = line_ref[
                 chunk, row : row + 16, :
@@ -1463,7 +1556,7 @@
             small_out[...] = line_ref[chunk, row : row + 16, :]
 
     tail = LAG * (chips - 1)
-    ready = lambda h: lat_chunks + (h + 1) * half_chunks - 1 + tail
+    ready = lambda h: lat_chunks + GAP + (h + 1) * half_chunks - 1 + tail
     events = {}
 
     def at_tick(tick, run):
@@ -1477,15 +1570,20 @@
     at_tick(KV_TICKS[0], token_other)
     at_tick(KV_TICKS[1], token_own)
     at_tick(PAIR_TICK, pair_event)
+    at_tick(MORE_TICK, wide_more)
     at_tick(ONE_TICK, one_event)
     at_tick(TWO_TICK, two_event)
     for sub in range(SUBS):
         at_tick(WIDE_ONE_TICKS[sub], functools.partial(wide_event_one, sub))
         at_tick(WIDE_TWO_TICKS[sub], functools.partial(wide_event_two, sub))
-    load.wait()
+        if WIDE_THREE_TICKS[sub] >= 0:
+            at_tick(WIDE_THREE_TICKS[sub], functools.partial(wide_event_three, sub))
+    for copy in pulls:
+        copy.wait()
 
     def step(t, carry):
         line_step(t)
+        spread_step(t)
         for tick in sorted(events):
 
             @pl.when(t == tick)
@@ -1495,20 +1593,12 @@
 
         return carry
 
-    lax.fori_loop(0, ready(0) + 1, step, 0)
-    spread_event(0)
-    lax.fori_loop(ready(0) + 1, ready(1) + 1, step, 0)
-    spread_event(1)
+    lax.fori_loop(0, ready(1) + 2 * SPREAD_LAG + 1, step, 0)
+    for h in range(2):
+        query_event(h)
     for sub in range(SUBS):
-        wide_event_three(sub)
-    for h in range(2):
-        spread_one_arrival(h).wait_recv()
-        spread_two(h, 1).start()
-        share_copy(h, 1).start()
-    for h in range(2):
-        for n in range(2):
-            spread_two_arrival(h, n).wait_recv()
-            share_copy(h, 2 + n).start()
+        if WIDE_THREE_TICKS[sub] < 0:
+            wide_event_three(sub)
 
     def finish_lat(i, carry):
         dpair_copy(i).wait_send()
@@ -1531,21 +1621,30 @@
         return carry
 
     lax.fori_loop(0, all_chunks, finish_line, 0)
-    for copy in pairs:
-        copy.wait_send()
+
+    def finish_spread(n, carry):
+        h = lax.div(n, kv_chunks)
+        i = lat_chunks + h * half_chunks + lax.rem(n, kv_chunks)
+        for k in range(4):
+            if k:
+                spread_copy(i, k).wait_send()
+            share_copy(i, k).wait_send()
+            share_arrival(i, k).wait_recv()
+            kv_keep(i, k).wait()
+        return carry
+
+    lax.fori_loop(0, 2 * kv_chunks, finish_spread, 0)
+    for i in range(parts - 2, parts):
+        stage_copy(i).wait()
+    for k, h, what in pairs:
+        pair_copy(k, h, what).wait_send()
     for h in range(2):
         for n in range(2):
             one_copy(h, n).wait_send()
-            spread_two(h, n).wait_send()
         two_copy(h).wait_send()
-        spread_one(h).wait_send()
-        kv_keep(h).wait()
         query_copy(h).wait_send()
         query_arrival(h).wait_recv()
         query_keep(h).wait()
-        for k in range(4):
-            share_copy(h, k).wait_send()
-            share_arrival(h, k).wait_recv()
         for sub in range(SUBS):
             for n in range(2):
                 wide_one_copy(h, n, sub).wait_send()
@@ -1553,11 +1652,12 @@
                 wide_core_arrival(n, h, sub).wait_recv()
             wide_two_copy(h, sub).wait_send()
             wide_z_copy(h, sub).wait_send()
-            wide_keep(h, sub).wait()
+            wide_keep(0, h, sub).wait()
+            wide_keep(1, h, sub).wait()
 
 
 def gradients(
-    dlat, dmid, a, b, side, dwq, vec, dgain_q, place, tokens, tsort, dkv, gain_t, wk, wv
+    dlat, a, b, side, dwq, vec, dgain_q, place, tokens, tsort, dkv, gain_t, wk, wv
 ):
     rows, width = tokens.shape
     half = dlat.shape[0] // 2
@@ -1582,8 +1682,12 @@
             sds((16, width), F32),
             sds((rows, width), F32),
         ),
-        in_specs=[anywhere()] + [vmem()] * 14,
-        out_specs=(anywhere(),) * 4 + (vmem(),) * 2,
+        in_specs=[anywhere()] * 3
+        + [vmem(), anywhere()]
+        + [vmem()] * 3
+        + [anywhere()] * 3
+        + [vmem()] * 3,
+        out_specs=(anywhere(),) * 4 + (vmem(), anywhere()),
         scratch_shapes=[
             buf(all_chunks, ZROWS, width),
             buf(all_chunks, ZROWS, width),
@@ -1599,7 +1703,17 @@
             buf(2, block, width),
             buf(4, 16, width),
             buf(width, 128),
-            dma,
+            buf(wide_rows, wide_cols),
+            buf(3, 2, kv_rows // ZROWS, ZROWS, width),
+            buf(2, 128, width),
+            dma((2,)),
+            pltpu.VMEM(a.shape, BF16),
+            pltpu.VMEM(b.shape, BF16),
+            buf(4, 2, 2, q_rows, width),
+            pltpu.VMEM(tokens.shape, BF16),
+            pltpu.VMEM(tsort.shape, BF16),
+            pltpu.VMEM(dkv.shape, BF16),
+            dma((7,)),
         ]
         + both(lat_chunks)
         + both(all_chunks)
@@ -1610,20 +1724,19 @@
         + both(2, SUBS)
         + both(2, SUBS)
         + both(2, 2, SUBS)
-        + [dma((2, SUBS))]
-        + both(5)
+        + [dma((2, 2, SUBS))]
+        + both(4, 2, 3)
         + both(2, 2)
         + both(2)
-        + both(3, 2)
-        + both(2, 4)
+        + both(3, all_chunks - lat_chunks)
+        + both(4, all_chunks - lat_chunks)
         + both(2)
-        + [dma((4,))],
+        + [dma((2,)), dma((4, all_chunks - lat_chunks))],
         compiler_params=pltpu.CompilerParams(
             vmem_limit_bytes=VMEM_BYTES, collective_id=2, has_side_effects=True
         ),
     )(
         dlat.reshape(2, lat_chunks, ZROWS, width),
-        dmid.reshape(lat_chunks, ZROWS, width),
         a,
         b,
         side,
@@ -1652,7 +1765,7 @@
     up_out,
     key_out,
     val_out,
-    down_ref,
+    down_out,
     out_ref,
     wq_ref,
     gain_q_ref,
@@ -1661,24 +1774,44 @@
     bup_ref,
     bdn_ref,
     wide_ref,
-    side_ref,
-    sems,
+    up_ref,
+    dlat_ref,
+    kv_ref,
+    dtok_ref,
+    down_ref,
+    load_sems,
+    store_sems,
 ):
     width = small_ref.shape[1]
     cols = wide_ref.shape[2]
-    moves = [
-        (gather_hbm.at[1], wide_ref),
-        (gather_hbm.at[0, :, pl.ds(width, side_ref.shape[1])], side_ref),
-        (kv_hbm.at[0], key_out),
-        (kv_hbm.at[1], val_out),
-        (dlat_hbm, dlat_out),
-        (dtok_hbm, dtok_out),
+    loads = [
+        pltpu.make_async_copy(src, dst, load_sems.at[i])
+        for i, (src, dst) in enumerate(
+            (
+                (gather_hbm.at[1], wide_ref),
+                (gather_hbm.at[0], up_ref),
+                (dlat_hbm, dlat_ref),
+                (kv_hbm, kv_ref),
+                (dtok_hbm, dtok_ref),
+            )
+        )
     ]
-    for e in range(2):
-        moves.append((gather_hbm.at[0, e, pl.ds(0, width)], up_out.at[:, pl.ds(e * cols, cols)]))
-    copies = [pltpu.make_async_copy(a, b, sems.at[i]) for i, (a, b) in enumerate(moves)]
-    for copy in copies:
+    for copy in loads:
         copy.start()
+    stores = [
+        pltpu.make_async_copy(src, dst, store_sems.at[i])
+        for i, (src, dst) in enumerate(
+            (
+                (up_ref.at[0, pl.ds(0, width)], up_out.at[:, pl.ds(0, cols)]),
+                (up_ref.at[1, pl.ds(0, width)], up_out.at[:, pl.ds(cols, cols)]),
+                (dlat_ref, dlat_out),
+                (kv_ref.at[0], key_out),
+                (kv_ref.at[1], val_out),
+                (dtok_ref, dtok_out),
+                (down_ref, down_out),
+            )
+        )
+    ]
     stream = lax.axis_index("stream")
     gain_t_ref[...] = small_ref[4]
     bup_ref[...] = small_ref[0]
@@ -1689,14 +1822,26 @@
         for k in range(1, width // size):
             piece = jnp.where(stream == k, line[:, k * size : (k + 1) * size], piece)
         ref[...] = piece[0]
-    wq_ref[...] = query_ref[...].T
-    copies[0].wait()
-    copies[1].wait()
+    wq_ref[...] = query_ref[...]
+    loads[0].wait()
     for e in range(2):
-        span = slice(e * cols, (e + 1) * cols)
-        down_ref[span, :] = wide_ref[e, :width, :].T
-        out_ref[span, :] = jnp.concatenate((side_ref[e], wide_ref[e, width:, :]), 0).T
-    for copy in copies[2:]:
+        down_ref[e * cols : (e + 1) * cols, :] = wide_ref[e, :width, :].T
+    stores[6].start()
+    loads[1].wait()
+    stores[0].start()
+    stores[1].start()
+    half = up_ref.shape[1] - width
+    for e in range(2):
+        out_ref[:half, e * cols : (e + 1) * cols] = up_ref[e, width:, :]
+        out_ref[half:, e * cols : (e + 1) * cols] = wide_ref[e, width:, :]
+    loads[2].wait()
+    stores[2].start()
+    loads[3].wait()
+    stores[3].start()
+    stores[4].start()
+    loads[4].wait()
+    stores[5].start()
+    for copy in stores:
         copy.wait()
 
 
@@ -1716,8 +1861,8 @@
             sds(width, width),
             sds(width, width),
             sds(2 * cols, width),
-            sds(width, share),
-            sds(width, share),
+            sds(share, width),
+            sds(share, width),
             sds(share),
             sds(width),
             sds(share),
@@ -1725,11 +1870,16 @@
             sds(share),
         ),
         in_specs=[anywhere()] * 3 + [vmem()] * 2 + [anywhere()],
-        out_specs=(anywhere(),) * 5 + (vmem(),) * 8,
+        out_specs=(anywhere(),) * 6 + (vmem(),) * 7,
         scratch_shapes=[
             pltpu.VMEM((2, wide_rows, cols), F32),
-            pltpu.VMEM((2, wide_rows - width, cols), F32),
-            pltpu.SemaphoreType.DMA((8,)),
+            pltpu.VMEM((2, wide_rows, cols), F32),
+            pltpu.VMEM(dlat.shape, F32),
+            pltpu.VMEM(kv.shape, F32),
+            pltpu.VMEM(dtok.shape, F32),
+            pltpu.VMEM((2 * cols, width), F32),
+            pltpu.SemaphoreType.DMA((5,)),
+            pltpu.SemaphoreType.DMA((7,)),
         ],
         compiler_params=pltpu.CompilerParams(vmem_limit_bytes=VMEM_BYTES),
     )(dlat, gather, kv, query, small, dtok)
@@ -1761,11 +1911,11 @@
     msg, result, dmid, a, b, side, vec = latent_block(
         part, drop_mask, latents, cotangent, w_out, gain_mlp, w_up, b_up, w_down, b_down
     )
-    dkv, dlat, dgain_q, dwq = attend_backward(
-        bounds, latents, keys, values, query, normed, msg, gain_query, w_query
+    dkv, dlat, dgain_q, dwq, result = attend_backward(
+        bounds, latents, keys, values, query, normed, msg, dmid, gain_query, w_query, result
     )
     dlat, gather, kv, dwq, small, d_tokens = gradients(
-        dlat, dmid, a, b, side, dwq, vec, dgain_q, place, tokens, tsort, dkv, gain_token,
+        dlat, a, b, side, dwq, vec, dgain_q, place, tokens, tsort, dkv, gain_token,
         w_key, w_value,
     )
     (
@@ -1795,11 +1945,11 @@
         d_latents.reshape(latents.shape),
         d_tokens,
         grad_gquery,
-        grad_query,
+        grad_query.T,
         grad_gtoken,
         grad_key,
         grad_value,
-        grad_out,
+        grad_out.T,
         grad_gmlp,
         grad_up,
         grad_bup,

time: 721 us -> 270 us (0.37)
  Pallas kernels: 711 us -> 269 us
    pallas_call x1, Pallas kernels: 409 us -> 13 us  [closing(): pl.pallas_call(closing_kernel, name='closing', out_shape=(sds(*dlat.shape...]
    pallas_call x1, Pallas kernels: 174 us -> 126 us  [gradients(): pl.pallas_call(gradient_kernel, name='gradients', out_shape=(sds((2, lat_...]
where the time goes in v5:
time: 270 us
  Pallas kernels  269 us (100%)
    pallas_call x1, Pallas kernels, gradients(): pl.pallas_call(gradient_kernel, name='gradients', out_shape=(sds((2, lat_...  126 us
    pallas_call x1, Pallas kernels, latent_block(): pl.pallas_call(latent_kernel, name='latent_block', out_shape=(sds((sample...  75.4 us
    pallas_call x1, Pallas kernels, attend_forward(): pl.pallas_call(forward_kernel, name='attend_forward', out_shape=(sds((sam...  29.9 us
    pallas_call x1, Pallas kernels, attend_backward(): pl.pallas_call(backward_kernel, name='attend_backward', out_shape=(sds((2...  24.9 us
    pallas_call x1, Pallas kernels, closing(): pl.pallas_call(closing_kernel, name='closing', out_shape=(sds(*dlat.shape...  13 us

profile of v5, /device:TPU:0, one launch (start us, length us, event | category | flops | bytes accessed | tf_op | source)
XLA Modules:
  0.0 270.1 jit_solution(4663561834795251946)
XLA Ops:
  0.6 29.9 %attend_forward.1 = (f32[8,4,208,128]{3,2,1,0:T(8,128)}, bf16[1280,768]{1,0:T(8,128)(2,1)}, bf16[1280,768]{1,0:T(8,128)(2,1)}, bf16[1024,768]{1,0:T(8,128)(2,1)}...) custom-call(s32[1024]{0:T(1024)} %sample_ref.1, ...), custom_call_target="tpu_custom_call" | custom-call | tf_op jit(solution)/shard_map/attend_forward/pallas_call | solution.py:221
  30.6 75.4 %latent_block.1 = (f32[8,800,128]{2,1,0:T(8,128)}, bf16[1024,768]{1,0:T(8,128)(2,1)}, f32[512,768]{1,0:T(8,128)}, bf16[1024,768]{1,0:T(8,128)(2,1)}, bf16[4,1024...) custom-call(f32[32,208,128]{2,1,0:T(8,128)} %bitcast.16, s32[32]{0:T(128)} %drop_ref.1, ...), custom_call_target="tpu_custom_call" | custom-call | tf_op jit(solution)/shard_map/latent_block/pallas_call | solution.py:872
  106.0 24.9 %attend_backward.1 = (bf16[2,1024,768]{2,1,0:T(8,128)(2,1)}, f32[1024,768]{1,0:T(8,128)}, f32[8,768]{1,0:T(8,128)}, f32[768,768]{1,0:T(8,128)}, bf16[1024,768]{1,0:T(8,128)(2,1)}) custom-call(s32[16]{0:T(128)} %get-tuple-element.53.bounds_ref, bf16[1024,768]{1,0:T(8,128)(2,1)} %bitcast.14, bf16[1280,768]{1,0:T(8,128)(2,1)} %get-tuple-element.54.key_ref, ...), custom_call_target="tpu_custom_call" | custom-call | tf_op jit(solution)/shard_map/attend_backward/pallas_call | solution.py:378
  130.9 126.0 %gradients.1 = (f32[2,16,32,768]{3,2,1,0:T(8,128)}, f32[2,2,864,384]{3,2,1,0:T(8,128)}, f32[2,4,2,3,32,768]{5,4,3,2,1,0:T(8,128)}, f32[2,2,48,768]{3,2,1,0:T(8,1...) custom-call(f32[2,16,32,768]{3,2,1,0:T(8,128)} %bitcast.18, bf16[1024,768]{1,0:T(8,128)(2,1)} %get-tuple-element.64.a_hbm, ...), custom_call_target="tpu_custom_call" | custom-call | tf_op jit(solution)/shard_map/gradients/pallas_call | solution.py:1674
  256.9 13.0 %closing.1 = (f32[1024,768]{1,0:T(8,128)}, f32[1024,768]{1,0:T(8,128)}, f32[768,768]{1,0:T(8,128)}, f32[768,768]{1,0:T(8,128)}, f32[768,768]{1,0:T(8,128)}, /*in...) custom-call(f32[1024,768]{1,0:T(8,128)} %bitcast.17, ...), custom_call_target="tpu_custom_call" | custom-call | tf_op jit(solution)/shard_map/closing/pallas_call | solution.py:1854

commit v6 on v5

--- a/solution.py
+++ b/solution.py
@@ -16,6 +16,8 @@
 PIECE_ROWS = NUM_ROWS + 16
 MSG_ROWS = HEADS * HEAD_DIM + 32
 BLOCK = 256
+FWD_BLOCK = 128
+PAD = 256
 LAG = 2
 GAP = 6
 SUBS = 3
@@ -67,11 +69,29 @@
 def forward_kernel(
     sample_ref,
     mask_ref,
+    tok_hbm,
+    lat_hbm,
+    gain_q_ref,
+    wq_hbm,
+    gain_t_ref,
+    wk_hbm,
+    wv_hbm,
+    part_out,
+    key_out,
+    val_out,
+    tsort_out,
+    query_out,
+    normed_out,
+    place_ref,
+    bounds_ref,
+    tnorm_ref,
+    pos_ref,
+    top_ref,
+    den_ref,
+    num_ref,
     tok_ref,
     lat_ref,
-    gain_q_ref,
     wq_ref,
-    gain_t_ref,
     wk_ref,
     wv_ref,
     part_ref,
@@ -80,15 +100,45 @@
     tsort_ref,
     query_ref,
     normed_ref,
-    place_ref,
-    bounds_ref,
-    tnorm_ref,
-    pos_ref,
-    top_ref,
-    den_ref,
-    num_ref,
+    load_sem,
+    store_sem,
+    sample_sem,
 ):
+    loads = [
+        pltpu.make_async_copy(src, dst, load_sem.at[i])
+        for i, (src, dst) in enumerate(
+            (
+                (tok_hbm, tok_ref),
+                (wk_hbm, wk_ref),
+                (wv_hbm, wv_ref),
+                (lat_hbm, lat_ref),
+                (wq_hbm, wq_ref),
+            )
+        )
+    ]
+    for copy in loads:
+        copy.start()
+    stores = [
+        pltpu.make_async_copy(src, dst, store_sem.at[i])
+        for i, (src, dst) in enumerate(
+            ((key_ref, key_out), (val_ref, val_out), (tsort_ref, tsort_out))
+        )
+    ]
     samples = part_ref.shape[0]
+
+    def sample_stores(s):
+        at = pl.ds(pl.multiple_of(s * 128, 128), 128)
+        return [
+            pltpu.make_async_copy(src, dst, sample_sem.at[i, s])
+            for i, (src, dst) in enumerate(
+                (
+                    (part_ref.at[s], part_out.at[s]),
+                    (query_ref.at[s], query_out.at[s]),
+                    (normed_ref.at[at], normed_out.at[at]),
+                )
+            )
+        ]
+
     rows = tok_ref.shape[0]
     width = tok_ref.shape[1]
     lat_rows = 128
@@ -122,7 +172,10 @@
         tnorm_ref[at, :] = (unit * row(gain_t_ref)).astype(BF16)
         return carry
 
+    loads[0].wait()
     lax.fori_loop(0, rows // step, token_norm, 0)
+    loads[1].wait()
+    loads[2].wait()
 
     def token_sort(i, carry):
         at = pl.ds(pl.multiple_of(i * step, step), step)
@@ -136,8 +189,12 @@
         return carry
 
     lax.fori_loop(0, rows // step, token_sort, 0)
-    key_ref[rows:, :] = jnp.zeros((BLOCK, width), BF16)
-    val_ref[rows:, :] = jnp.zeros((BLOCK, width), BF16)
+    key_ref[rows:, :] = jnp.zeros((PAD, width), BF16)
+    val_ref[rows:, :] = jnp.zeros((PAD, width), BF16)
+    for copy in stores:
+        copy.start()
+    loads[3].wait()
+    loads[4].wait()
 
     def sample_step(s, carry):
         at = pl.ds(pl.multiple_of(s * lat_rows, lat_rows), lat_rows)
@@ -156,7 +213,7 @@
         start = bounds_ref[s]
         total = bounds_ref[samples + s]
         base = lax.div(start, 16) * 16
-        blocks = jnp.where(total > 0, lax.div(start + total - base + BLOCK - 1, BLOCK), 0)
+        blocks = jnp.where(total > 0, lax.div(start + total - base + FWD_BLOCK - 1, FWD_BLOCK), 0)
         for piece in range(PIECES):
             part_ref[s, piece, NUM_ROWS:, :] = jnp.zeros((16, lat_rows), F32)
         num_ref[...] = jnp.zeros_like(num_ref)
@@ -164,12 +221,12 @@
         den_ref[...] = jnp.zeros_like(den_ref)
 
         def block_step(b, carry):
-            row = pl.multiple_of(base + b * BLOCK, 16)
-            index = lax.broadcasted_iota(jnp.int32, (BLOCK, 2 * lat_rows), 0) + row
+            row = pl.multiple_of(base + b * FWD_BLOCK, 16)
+            index = lax.broadcasted_iota(jnp.int32, (FWD_BLOCK, 2 * lat_rows), 0) + row
             inside = (index >= start) & (index < start + total)
             for p in range(PAIRS):
                 cols = slice(p * 128, (p + 1) * 128)
-                score = dot(key_ref[pl.ds(row, BLOCK), cols], query_ref[s, p])
+                score = dot(key_ref[pl.ds(row, FWD_BLOCK), cols], query_ref[s, p])
                 score = jnp.where(inside, score, NEG)
                 old = top_ref[p : p + 1, :]
                 new = jnp.maximum(old, jnp.max(score, 0, keepdims=True))
@@ -179,7 +236,7 @@
                 den_ref[p : p + 1, :] = den_ref[p : p + 1, :] * fade + jnp.sum(
                     weight, 0, keepdims=True
                 )
-                both = dot(val_ref[pl.ds(row, BLOCK), cols], weight.astype(BF16), (0, 0))
+                both = dot(val_ref[pl.ds(row, FWD_BLOCK), cols], weight.astype(BF16), (0, 0))
                 for half in range(2):
                     at_rows = slice(p * 128 + half * HEAD_DIM, p * 128 + (half + 1) * HEAD_DIM)
                     at_cols = slice(half * lat_rows, (half + 1) * lat_rows)
@@ -201,13 +258,28 @@
             part_ref[s, piece, NUM_ROWS + 8 + i : NUM_ROWS + 9 + i, :] = den_ref[
                 p : p + 1, at_cols
             ]
+        for copy in sample_stores(s):
+            copy.start()
         return carry
 
     lax.fori_loop(0, samples, sample_step, 0)
+    for copy in stores:
+        copy.wait()
+
+    def finish(s, carry):
+        for copy in sample_stores(s):
+            copy.wait()
+        return carry
+
+    lax.fori_loop(0, samples, finish, 0)
 
 
 def vmem():
     return pl.BlockSpec(memory_space=pltpu.VMEM)
+
+
+def anywhere():
+    return pl.BlockSpec(memory_space=pl.ANY)
 
 
 def smem():
@@ -223,22 +295,39 @@
         name="attend_forward",
         out_shape=(
             sds((samples, PIECES, PIECE_ROWS, lat_rows), F32),
-            sds((rows + BLOCK, width), BF16),
-            sds((rows + BLOCK, width), BF16),
+            sds((rows + PAD, width), BF16),
+            sds((rows + PAD, width), BF16),
             sds((rows, width), BF16),
             sds((samples, PAIRS, 128, 2 * lat_rows), BF16),
             sds((samples * lat_rows, width), BF16),
             sds((rows, 128), F32),
             sds((2 * samples,), jnp.int32),
         ),
-        in_specs=[vmem()] * 9,
-        out_specs=(vmem(),) * 7 + (smem(),),
+        in_specs=[vmem()] * 2
+        + [anywhere()] * 2
+        + [vmem(), anywhere(), vmem()]
+        + [anywhere()] * 2,
+        out_specs=(anywhere(),) * 6 + (vmem(), smem()),
         scratch_shapes=[
             pltpu.VMEM((rows, width), BF16),
             pltpu.VMEM((8, rows), F32),
             pltpu.VMEM((8, 2 * lat_rows), F32),
             pltpu.VMEM((8, 2 * lat_rows), F32),
             pltpu.VMEM((width, lat_rows), F32),
+            pltpu.VMEM((rows, width), BF16),
+            pltpu.VMEM((samples * lat_rows, width), BF16),
+            pltpu.VMEM((width, width), BF16),
+            pltpu.VMEM((width, width), BF16),
+            pltpu.VMEM((width, width), BF16),
+            pltpu.VMEM((samples, PIECES, PIECE_ROWS, lat_rows), F32),
+            pltpu.VMEM((rows + PAD, width), BF16),
+            pltpu.VMEM((rows + PAD, width), BF16),
+            pltpu.VMEM((rows, width), BF16),
+            pltpu.VMEM((samples, PAIRS, 128, 2 * lat_rows), BF16),
+            pltpu.VMEM((samples * lat_rows, width), BF16),
+            pltpu.SemaphoreType.DMA((5,)),
+            pltpu.SemaphoreType.DMA((3,)),
+            pltpu.SemaphoreType.DMA((3, samples)),
         ],
         compiler_params=pltpu.CompilerParams(vmem_limit_bytes=VMEM_BYTES),
     )(
@@ -256,20 +345,20 @@
 
 def backward_kernel(
     bounds_ref,
-    lat_ref,
-    key_ref,
-    val_ref,
-    query_ref,
-    normed_ref,
-    msg_ref,
-    dmid_ref,
+    lat_hbm,
+    key_hbm,
+    val_hbm,
+    query_hbm,
+    normed_hbm,
+    msg_hbm,
+    dmid_hbm,
     gain_q_ref,
-    wq_ref,
+    wq_hbm,
     res_hbm,
-    dkv_ref,
-    dlat_ref,
+    dkv_out,
+    dlat_out,
     dgain_ref,
-    dwq_ref,
+    dwq_out,
     res_out,
     dk_ref,
     dv_ref,
@@ -279,15 +368,66 @@
     stat_ref,
     res_ref,
     res_sems,
+    lat_ref,
+    key_ref,
+    val_ref,
+    query_ref,
+    normed_ref,
+    msg_ref,
+    dmid_ref,
+    wq_ref,
+    dkv_ref,
+    dlat_ref,
+    dwq_ref,
+    load_sem,
+    sample_sem,
+    dlat_sem,
+    store_sem,
 ):
     samples = query_ref.shape[0]
     rows = dkv_ref.shape[1]
     lat_rows = 128
     step = 256
     width = dwq_ref.shape[0]
-    for r in range(0, rows + BLOCK, step):
+    for r in range(0, rows + PAD, step):
         dk_ref[r : r + step, :] = jnp.zeros((step, dk_ref.shape[1]), F32)
         dv_ref[r : r + step, :] = jnp.zeros((step, dv_ref.shape[1]), F32)
+    loads = [
+        pltpu.make_async_copy(src, dst, load_sem.at[i])
+        for i, (src, dst) in enumerate(
+            (
+                (key_hbm, key_ref),
+                (val_hbm, val_ref),
+                (lat_hbm, lat_ref),
+                (wq_hbm, wq_ref),
+                (dmid_hbm, dmid_ref),
+                (normed_hbm, normed_ref),
+            )
+        )
+    ]
+
+    def sample_loads(s):
+        return [
+            pltpu.make_async_copy(msg_hbm.at[s], msg_ref.at[s], sample_sem.at[0, s]),
+            pltpu.make_async_copy(query_hbm.at[s], query_ref.at[s], sample_sem.at[1, s]),
+        ]
+
+    def dlat_store(s):
+        at = pl.ds(pl.multiple_of(s * 128, 128), 128)
+        return pltpu.make_async_copy(dlat_ref.at[at], dlat_out.at[at], dlat_sem.at[s])
+
+    for copy in loads[:2] + sample_loads(0):
+        copy.start()
+
+    def start_sample(s, carry):
+        for copy in sample_loads(s):
+            copy.start()
+        return carry
+
+    for copy in loads[2:5]:
+        copy.start()
+    lax.fori_loop(1, query_ref.shape[0], start_sample, 0)
+    loads[5].start()
     res_load = pltpu.make_async_copy(res_hbm, res_ref, res_sems.at[0])
     res_store = pltpu.make_async_copy(res_ref, res_out, res_sems.at[1])
     res_load.start()
@@ -295,7 +435,18 @@
     grad_ref[...] = jnp.zeros_like(grad_ref)
     dgain_ref[...] = jnp.zeros_like(dgain_ref)
 
+    loads[0].wait()
+    loads[1].wait()
+
     def sample_step(s, carry):
+        for copy in sample_loads(s):
+            copy.wait()
+
+        @pl.when(s == 0)
+        def _():
+            for copy in loads[2:5]:
+                copy.wait()
+
         start = bounds_ref[s]
         total = bounds_ref[samples + s]
         base = lax.div(start, 16) * 16
@@ -358,6 +509,7 @@
             mine = pl.ds(pl.multiple_of(j * lat_rows, lat_rows), lat_rows)
             dlat_ref[at, :] = dlat + dmid_ref[mine, :]
 
+        dlat_store(s).start()
         return carry
 
     lax.fori_loop(0, samples, sample_step, 0)
@@ -366,14 +518,32 @@
     for r in range(0, rows, step):
         dkv_ref[0, r : r + step, :] = dk_ref[r : r + step, :].astype(BF16)
         dkv_ref[1, r : r + step, :] = dv_ref[r : r + step, :].astype(BF16)
+    dkv_store = pltpu.make_async_copy(dkv_ref, dkv_out, store_sem.at[0])
+    dkv_store.start()
+    loads[5].wait()
+    stores = []
     for c in range(0, width, 256):
         dwq_ref[c : c + 256, :] = dot(dquery_ref[:, c : c + 256], normed_ref[...], (0, 0))
+        copy = pltpu.make_async_copy(
+            dwq_ref.at[pl.ds(c, 256)], dwq_out.at[pl.ds(c, 256)], store_sem.at[1 + c // 256]
+        )
+        copy.start()
+        stores.append(copy)
     res_store.wait()
+    dkv_store.wait()
+    for copy in stores:
+        copy.wait()
+
+    def finish(s, carry):
+        dlat_store(s).wait()
+        return carry
+
+    lax.fori_loop(0, samples, finish, 0)
 
 
 def attend_backward(bounds, latents, keys, values, query, normed, msg, dmid, gain_q, wq, result):
     samples, lat_rows, width = latents.shape
-    rows = keys.shape[0] - BLOCK
+    rows = keys.shape[0] - PAD
     sds = jax.ShapeDtypeStruct
     return pl.pallas_call(
         backward_kernel,
@@ -385,17 +555,32 @@
             sds((width, width), F32),
             sds(result.shape, BF16),
         ),
-        in_specs=[smem()] + [vmem()] * 9 + [anywhere()],
-        out_specs=(vmem(),) * 4 + (anywhere(),),
+        in_specs=[smem()] + [anywhere()] * 7 + [vmem()] + [anywhere()] * 2,
+        out_specs=(anywhere(),) * 2 + (vmem(),) + (anywhere(),) * 2,
         scratch_shapes=[
-            pltpu.VMEM((rows + BLOCK, width), F32),
-            pltpu.VMEM((rows + BLOCK, width), F32),
+            pltpu.VMEM((rows + PAD, width), F32),
+            pltpu.VMEM((rows + PAD, width), F32),
             pltpu.VMEM((PAIRS, 128, 2 * lat_rows), BF16),
             pltpu.VMEM((samples * lat_rows, width), BF16),
             pltpu.VMEM((width, lat_rows), F32),
             pltpu.VMEM((16, 2 * lat_rows), F32),
             pltpu.VMEM(result.shape, BF16),
             pltpu.SemaphoreType.DMA((2,)),
+            pltpu.VMEM((samples * lat_rows, width), BF16),
+            pltpu.VMEM((rows + PAD, width), BF16),
+            pltpu.VMEM((rows + PAD, width), BF16),
+            pltpu.VMEM(query.shape, BF16),
+            pltpu.VMEM(normed.shape, BF16),
+            pltpu.VMEM(msg.shape, F32),
+            pltpu.VMEM(dmid.shape, F32),
+            pltpu.VMEM(wq.shape, BF16),
+            pltpu.VMEM((2, rows, width), BF16),
+            pltpu.VMEM((samples * lat_rows, width), F32),
+            pltpu.VMEM((width, width), F32),
+            pltpu.SemaphoreType.DMA((6,)),
+            pltpu.SemaphoreType.DMA((2, samples)),
+            pltpu.SemaphoreType.DMA((samples,)),
+            pltpu.SemaphoreType.DMA((1 + width // 256,)),
         ],
         compiler_params=pltpu.CompilerParams(vmem_limit_bytes=VMEM_BYTES),
     )(
@@ -442,21 +627,29 @@
 def latent_kernel(
     part_hbm,
     drop_ref,
-    lat_ref,
-    cot_ref,
+    lat_hbm,
+    cot_hbm,
     wo_hbm,
     gain_ref,
     wup_hbm,
     bup_ref,
     wdn_hbm,
     bdn_ref,
+    msg_out,
+    res_all,
+    dmid_out,
+    a_out,
+    b_out,
+    side_ref,
+    vec_ref,
+    lat_ref,
+    cot_ref,
     msg_ref,
     res_ref,
     dmid_ref,
     a_ref,
     b_ref,
-    side_ref,
-    vec_ref,
+    store_sem,
     wo_ref,
     wup_ref,
     wdn_ref,
@@ -501,7 +694,7 @@
     res_send,
     res_recv,
 ):
-    samples = msg_ref.shape[0]
+    samples = msg_out.shape[0]
     half = samples // 2
     lat_rows = 128
     width = lat_ref.shape[1]
@@ -512,6 +705,7 @@
     core = lax.rem(tok, 2)
     chip = lax.div(tok, 2)
     parity = lax.rem(chip, 2)
+    other = 1 - core
     partner = (stream, tok + 1 - 2 * core)
     right = (stream, tok + 2)
     left = (stream, tok - 2)
@@ -536,7 +730,15 @@
     own_load.start()
     weights = [
         pltpu.make_async_copy(src, dst, weight_sem.at[i])
-        for i, (src, dst) in enumerate(((wo_hbm, wo_ref), (wup_hbm, wup_ref), (wdn_hbm, wdn_ref)))
+        for i, (src, dst) in enumerate(
+            (
+                (lat_hbm, lat_ref),
+                (cot_hbm, cot_ref),
+                (wo_hbm, wo_ref),
+                (wup_hbm, wup_ref),
+                (wdn_hbm, wdn_ref),
+            )
+        )
     ]
     for copy in weights:
         copy.start()
@@ -574,11 +776,28 @@
             device_id_type=MESH,
         )
 
+    def stores(j, far):
+        at = (other if far else core) * half + j
+        rows = pl.ds(pl.multiple_of(at * lat_rows, lat_rows), lat_rows)
+        mine = pl.ds(pl.multiple_of(j * lat_rows, lat_rows), lat_rows)
+        pairs = [
+            (res_ref.at[rows], res_all.at[rows]),
+            (a_ref.at[rows], a_out.at[rows]),
+            (b_ref.at[:, rows], b_out.at[:, rows]),
+        ]
+        if not far:
+            pairs.append((msg_ref.at[j], msg_out.at[at]))
+            pairs.append((dmid_ref.at[mine], dmid_out.at[mine]))
+        return [
+            pltpu.make_async_copy(src, dst, store_sem.at[far, i, j])
+            for i, (src, dst) in enumerate(pairs)
+        ]
+
     def msg_copy(j):
         at = core * half + j
         return pltpu.make_async_remote_copy(
-            src_ref=msg_ref.at[at],
-            dst_ref=msg_ref.at[at],
+            src_ref=msg_ref.at[j],
+            dst_ref=msg_out.at[at],
             send_sem=msg_send.at[j],
             recv_sem=msg_recv.at[j],
             device_id=partner,
@@ -586,10 +805,9 @@
         )
 
     def msg_arrival(j):
-        at = (1 - core) * half + j
         return pltpu.make_async_remote_copy(
-            src_ref=msg_ref.at[at],
-            dst_ref=msg_ref.at[at],
+            src_ref=msg_ref.at[j],
+            dst_ref=msg_out.at[other * half + j],
             send_sem=msg_send.at[j],
             recv_sem=msg_recv.at[j],
             device_id=partner,
@@ -646,6 +864,30 @@
     scale_all = drop * drop.shape[1] / jnp.sum(drop, 1, keepdims=True)
     drop_lane = lax.broadcasted_iota(jnp.int32, drop.shape, 1)
     vec_ref[...] = jnp.zeros_like(vec_ref)
+
+    def take(j):
+        at = other * half + j
+        rows = pl.ds(pl.multiple_of(at * lat_rows, lat_rows), lat_rows)
+        for q in range(PIECES):
+            half_copy(j * PIECES + q).wait_recv()
+            b_ref[q, rows, :] = half_in[j * PIECES + q].astype(BF16)
+        res_copy(j).wait_recv()
+        res_ref[rows, :] = res_in[j].astype(BF16)
+
+        @pl.when(on_first)
+        def _():
+            hn_copy(j).wait_recv()
+            a_ref[rows, :] = hn_in[j].astype(BF16)
+
+        @pl.when(jnp.logical_not(on_first))
+        def _():
+            scale = jnp.sum(
+                jnp.where(drop_lane == stream * samples + at, scale_all, 0.0), 1, keepdims=True
+            )
+            a_ref[rows, :] = (scale * cot_ref[rows, :].astype(F32)).astype(BF16)
+
+        for copy in stores(j, 1):
+            copy.start()
 
     def mlp(j, q):
         sample = core * half + j
@@ -715,20 +957,26 @@
             da = (scale * dmid).astype(BF16)
             da_ref[mine, :] = da
             datt_t = dot(wo_ref[...], da, (1, 1)).astype(BF16).astype(F32)
-            msg_ref[sample, width:, :] = jnp.zeros((MSG_ROWS - width, lat_rows), F32)
+            msg_ref[j, width:, :] = jnp.zeros((MSG_ROWS - width, lat_rows), F32)
             for h in range(HEADS):
                 piece, i = piece_of(h)
                 at = j * PIECES + piece
                 inverse = 1.0 / own_ref[at, NUM_ROWS + 8 + i : NUM_ROWS + 9 + i, :]
                 span_h = slice(h * HEAD_DIM, (h + 1) * HEAD_DIM)
                 one = datt_t[span_h]
-                msg_ref[sample, span_h, :] = (one * inverse).astype(BF16).astype(F32)
+                msg_ref[j, span_h, :] = (one * inverse).astype(BF16).astype(F32)
                 delta = jnp.sum(one * att_t_ref[span_h, :], 0, keepdims=True) * inverse
-                msg_ref[sample, width + h : width + h + 1, :] = own_ref[
+                msg_ref[j, width + h : width + h + 1, :] = own_ref[
                     at, NUM_ROWS + i : NUM_ROWS + i + 1, :
                 ]
-                msg_ref[sample, width + 16 + h : width + 17 + h, :] = delta
+                msg_ref[j, width + 16 + h : width + 17 + h, :] = delta
             msg_copy(j).start()
+            for copy in stores(j, 0):
+                copy.start()
+
+            @pl.when(j > 0)
+            def _():
+                take(j - 1)
 
     def step(t, carry):
         @pl.when(t < chunks)
@@ -808,13 +1056,11 @@
         side_all[block, 1] = product[share:]
     side_copy.start()
 
+    take(half - 1)
+
     def finish_chunk(i, carry):
         pair_copy(i).wait_send()
         half_copy(i).wait_send()
-        half_copy(i).wait_recv()
-        at = ((1 - core) * half + lax.div(i, PIECES)) * lat_rows
-        rows = pl.ds(pl.multiple_of(at, lat_rows), lat_rows)
-        b_ref[lax.rem(i, PIECES), rows, :] = half_in[i].astype(BF16)
 
         @pl.when(has_right)
         def _():
@@ -829,36 +1075,20 @@
     lax.fori_loop(0, chunks, finish_chunk, 0)
 
     def finish_sample(j, carry):
-        res_copy(j).wait_recv()
-        other = (1 - core) * half + j
-        rows = pl.ds(pl.multiple_of(other * lat_rows, lat_rows), lat_rows)
-        res_ref[rows, :] = res_in[j].astype(BF16)
-
-        @pl.when(on_first)
-        def _():
-            hn_copy(j).wait_recv()
-            a_ref[rows, :] = hn_in[j].astype(BF16)
-
         @pl.when(jnp.logical_not(on_first))
         def _():
             hn_copy(j).wait_send()
-            scale = jnp.sum(
-                jnp.where(drop_lane == stream * samples + other, scale_all, 0.0), 1, keepdims=True
-            )
-            a_ref[rows, :] = (scale * cot_ref[rows, :].astype(F32)).astype(BF16)
 
         res_copy(j).wait_send()
         msg_copy(j).wait_send()
         msg_arrival(j).wait_recv()
+        for copy in stores(j, 0) + stores(j, 1):
+            copy.wait()
         return carry
 
     lax.fori_loop(0, half, finish_sample, 0)
     side_copy.wait()
     side_ref[...] = side_all[:, core] + side_in[...]
-
-
-def anywhere():
-    return pl.BlockSpec(memory_space=pl.ANY)
 
 
 def latent_block(part, drop_mask, latents, cotangent, wo, gain, wup, bup, wdn, bdn):
@@ -884,8 +1114,8 @@
         in_specs=[
             anywhere(),
             vmem(),
-            vmem(),
-            vmem(),
+            anywhere(),
+            anywhere(),
             anywhere(),
             vmem(),
             anywhere(),
@@ -893,8 +1123,16 @@
             anywhere(),
             vmem(),
         ],
-        out_specs=(vmem(),) * 7,
+        out_specs=(anywhere(),) * 5 + (vmem(),) * 2,
         scratch_shapes=[
+            pltpu.VMEM((samples * lat_rows, width), BF16),
+            pltpu.VMEM((samples * lat_rows, width), BF16),
+            pltpu.VMEM((half, MSG_ROWS, lat_rows), F32),
+            pltpu.VMEM((samples * lat_rows, width), BF16),
+            pltpu.VMEM((half * lat_rows, width), F32),
+            pltpu.VMEM((samples * lat_rows, width), BF16),
+            pltpu.VMEM((PIECES, samples * lat_rows, hidden // PIECES // 2), BF16),
+            dma((2, 5, half)),
             pltpu.VMEM(wo.shape, BF16),
             pltpu.VMEM(wup.shape, BF16),
             pltpu.VMEM(wdn.shape, BF16),
@@ -927,7 +1165,7 @@
             dma,
             dma,
             dma,
-            dma((3,)),
+            dma((5,)),
             dma((chunks,)),
             dma((chunks,)),
             dma((chunks,)),

time: 270 us -> 255 us (0.944)
  Pallas kernels: 269 us -> 254 us
    pallas_call x1, Pallas kernels: 29.9 us -> 20.7 us  [attend_forward(): pl.pallas_call(forward_kernel, name='attend_forward', out_shape=(sds((sam...]
    pallas_call x1, Pallas kernels: 24.9 us -> 20.3 us  [attend_backward(): pl.pallas_call(backward_kernel, name='attend_backward', out_shape=(sds((2...]
where the time goes in v6:
time: 255 us
  Pallas kernels  254 us (100%)
    pallas_call x1, Pallas kernels, gradients(): pl.pallas_call(gradient_kernel, name='gradients', out_shape=(sds((2, lat_...  128 us
    pallas_call x1, Pallas kernels, latent_block(): pl.pallas_call(latent_kernel, name='latent_block', out_shape=(sds((sample...  72.7 us
    pallas_call x1, Pallas kernels, attend_forward(): pl.pallas_call(forward_kernel, name='attend_forward', out_shape=(sds((sam...  20.7 us
    pallas_call x1, Pallas kernels, attend_backward(): pl.pallas_call(backward_kernel, name='attend_backward', out_shape=(sds((2...  20.3 us
    pallas_call x1, Pallas kernels, closing(): pl.pallas_call(closing_kernel, name='closing', out_shape=(sds(*dlat.shape...  13 us

profile of v6, /device:TPU:0, one launch (start us, length us, event | category | flops | bytes accessed | tf_op | source)
XLA Modules:
  0.0 255.3 jit_solution(9652389402978188305)
XLA Ops:
  0.6 20.7 %attend_forward.1 = (f32[8,4,208,128]{3,2,1,0:T(8,128)}, bf16[1280,768]{1,0:T(8,128)(2,1)}, bf16[1280,768]{1,0:T(8,128)(2,1)}, bf16[1024,768]{1,0:T(8,128)(2,1)}...) custom-call(s32[1024]{0:T(1024)} %sample_ref.1, ...), custom_call_target="tpu_custom_call" | custom-call | tf_op jit(solution)/shard_map/attend_forward/pallas_call | solution.py:293
  21.4 72.7 %latent_block.1 = (f32[8,800,128]{2,1,0:T(8,128)}, bf16[1024,768]{1,0:T(8,128)(2,1)}, f32[512,768]{1,0:T(8,128)}, bf16[1024,768]{1,0:T(8,128)(2,1)}, bf16[4,1024...) custom-call(f32[32,208,128]{2,1,0:T(8,128)} %bitcast.16, s32[32]{0:T(128)} %drop_ref.1, ...), custom_call_target="tpu_custom_call" | custom-call | tf_op jit(solution)/shard_map/latent_block/pallas_call | solution.py:1102
  94.1 20.3 %attend_backward.1 = (bf16[2,1024,768]{2,1,0:T(8,128)(2,1)}, f32[1024,768]{1,0:T(8,128)}, f32[8,768]{1,0:T(8,128)}, f32[768,768]{1,0:T(8,128)}, bf16[1024,768]{1,0:T(8,128)(2,1)}) custom-call(s32[16]{0:T(128)} %get-tuple-element.53.bounds_ref, bf16[1024,768]{1,0:T(8,128)(2,1)} %bitcast.14, bf16[1280,768]{1,0:T(8,128)(2,1)} %get-tuple-element.54.key_hbm, ...), custom_call_target="tpu_custom_call" | custom-call | tf_op jit(solution)/shard_map/attend_backward/pallas_call | solution.py:548
  114.4 127.8 %gradients.1 = (f32[2,16,32,768]{3,2,1,0:T(8,128)}, f32[2,2,864,384]{3,2,1,0:T(8,128)}, f32[2,4,2,3,32,768]{5,4,3,2,1,0:T(8,128)}, f32[2,2,48,768]{3,2,1,0:T(8,1...) custom-call(f32[2,16,32,768]{3,2,1,0:T(8,128)} %bitcast.18, bf16[1024,768]{1,0:T(8,128)(2,1)} %get-tuple-element.64.a_hbm, ...), custom_call_target="tpu_custom_call" | custom-call | tf_op jit(solution)/shard_map/gradients/pallas_call | solution.py:1912
  242.1 13.0 %closing.1 = (f32[1024,768]{1,0:T(8,128)}, f32[1024,768]{1,0:T(8,128)}, f32[768,768]{1,0:T(8,128)}, f32[768,768]{1,0:T(8,128)}, f32[768,768]{1,0:T(8,128)}, /*in...) custom-call(f32[1024,768]{1,0:T(8,128)} %bitcast.17, ...), custom_call_target="tpu_custom_call" | custom-call | tf_op jit(solution)/shard_map/closing/pallas_call | solution.py:2092

commit v7 on v6

--- a/solution.py
+++ b/solution.py
@@ -19,24 +19,27 @@
 FWD_BLOCK = 128
 PAD = 256
 LAG = 2
+ZROWS = 32
+LINE_LAG = 2
 GAP = 6
 SUBS = 3
 EARLY_SUBS = 1
-SPREAD_LAG = 3
+SPREAD_LAG = 4
 WIDE_START_TICKS = (1, 2, 2, 4)
 KV_TICKS = (0, 3)
 PAIR_TICK = 5
-MORE_TICK = 21
+MORE_TICK = 16
 ONE_TICK = 15
 TWO_TICK = 20
 WIDE_ONE_TICKS = (10, 27, 30)
 WIDE_TWO_TICKS = (16, 32, 35)
 WIDE_THREE_TICKS = (25, -1, -1)
+LAT_TICKS = (0, 4, 8)
 TOKEN_TICKS = (6, 7, 8, 9, 11, 12, 13, 16)
 NEG = -1e30
 F32 = jnp.float32
 BF16 = jnp.bfloat16
-VMEM_BYTES = 56 * 1024 * 1024
+VMEM_BYTES = 60 * 1024 * 1024
 
 
 def norm_parts(values):
@@ -116,8 +119,8 @@
             )
         )
     ]
-    for copy in loads:
-        copy.start()
+    for n in (0, 3, 4, 1, 2):
+        loads[n].start()
     stores = [
         pltpu.make_async_copy(src, dst, store_sem.at[i])
         for i, (src, dst) in enumerate(
@@ -172,8 +175,36 @@
         tnorm_ref[at, :] = (unit * row(gain_t_ref)).astype(BF16)
         return carry
 
+    def lat_norm(i, carry):
+        at = pl.ds(pl.multiple_of(i * step, step), step)
+        unit, _ = norm_parts(lat_ref[at, :].astype(F32))
+        normed = (unit * row(gain_q_ref)).astype(BF16)
+        normed_ref[at, :] = normed
+        turned = (dot(normed, wq_ref[...]) * 0.125).T.astype(BF16)
+        blank = jnp.zeros((HEAD_DIM, lat_rows), BF16)
+        for n in range(step // lat_rows):
+            s = i * (step // lat_rows) + n
+            span = slice(n * lat_rows, (n + 1) * lat_rows)
+            for p in range(PAIRS):
+                lo = 2 * p * HEAD_DIM
+                mid, hi = lo + HEAD_DIM, lo + 2 * HEAD_DIM
+                query_ref[s, p, :HEAD_DIM, :lat_rows] = turned[lo:mid, span]
+                query_ref[s, p, :HEAD_DIM, lat_rows:] = blank
+                query_ref[s, p, HEAD_DIM:, :lat_rows] = blank
+                query_ref[s, p, HEAD_DIM:, lat_rows:] = turned[mid:hi, span]
+        return carry
+
+    def both_norm(i, carry):
+        return token_norm(i, lat_norm(i, carry))
+
     loads[0].wait()
-    lax.fori_loop(0, rows // step, token_norm, 0)
+    loads[3].wait()
+    loads[4].wait()
+    if rows == samples * lat_rows:
+        lax.fori_loop(0, rows // step, both_norm, 0)
+    else:
+        lax.fori_loop(0, rows // step, token_norm, 0)
+        lax.fori_loop(0, samples * lat_rows // step, lat_norm, 0)
     loads[1].wait()
     loads[2].wait()
 
@@ -193,23 +224,8 @@
     val_ref[rows:, :] = jnp.zeros((PAD, width), BF16)
     for copy in stores:
         copy.start()
-    loads[3].wait()
-    loads[4].wait()
 
     def sample_step(s, carry):
-        at = pl.ds(pl.multiple_of(s * lat_rows, lat_rows), lat_rows)
-        unit, _ = norm_parts(lat_ref[at, :].astype(F32))
-        normed = (unit * row(gain_q_ref)).astype(BF16)
-        normed_ref[at, :] = normed
-        query = dot(normed, wq_ref[...]) * 0.125
-        turned = query.T.astype(BF16)
-        blank = jnp.zeros((HEAD_DIM, lat_rows), BF16)
-        for p in range(PAIRS):
-            lo = 2 * p * HEAD_DIM
-            query_ref[s, p, :HEAD_DIM, :lat_rows] = turned[lo : lo + HEAD_DIM]
-            query_ref[s, p, :HEAD_DIM, lat_rows:] = blank
-            query_ref[s, p, HEAD_DIM:, :lat_rows] = blank
-            query_ref[s, p, HEAD_DIM:, lat_rows:] = turned[lo + HEAD_DIM : lo + 2 * HEAD_DIM]
         start = bounds_ref[s]
         total = bounds_ref[samples + s]
         base = lax.div(start, 16) * 16
@@ -345,18 +361,16 @@
 
 def backward_kernel(
     bounds_ref,
-    lat_hbm,
     key_hbm,
     val_hbm,
     query_hbm,
     normed_hbm,
     msg_hbm,
-    dmid_hbm,
     gain_q_ref,
     wq_hbm,
     res_hbm,
     dkv_out,
-    dlat_out,
+    dquery_out,
     dgain_ref,
     dwq_out,
     res_out,
@@ -368,16 +382,13 @@
     stat_ref,
     res_ref,
     res_sems,
-    lat_ref,
     key_ref,
     val_ref,
     query_ref,
     normed_ref,
     msg_ref,
-    dmid_ref,
     wq_ref,
     dkv_ref,
-    dlat_ref,
     dwq_ref,
     load_sem,
     sample_sem,
@@ -398,9 +409,7 @@
             (
                 (key_hbm, key_ref),
                 (val_hbm, val_ref),
-                (lat_hbm, lat_ref),
                 (wq_hbm, wq_ref),
-                (dmid_hbm, dmid_ref),
                 (normed_hbm, normed_ref),
             )
         )
@@ -412,9 +421,9 @@
             pltpu.make_async_copy(query_hbm.at[s], query_ref.at[s], sample_sem.at[1, s]),
         ]
 
-    def dlat_store(s):
+    def dquery_store(s):
         at = pl.ds(pl.multiple_of(s * 128, 128), 128)
-        return pltpu.make_async_copy(dlat_ref.at[at], dlat_out.at[at], dlat_sem.at[s])
+        return pltpu.make_async_copy(dquery_ref.at[at], dquery_out.at[at], dlat_sem.at[s])
 
     for copy in loads[:2] + sample_loads(0):
         copy.start()
@@ -424,14 +433,12 @@
             copy.start()
         return carry
 
-    for copy in loads[2:5]:
-        copy.start()
     lax.fori_loop(1, query_ref.shape[0], start_sample, 0)
-    loads[5].start()
+    loads[2].start()
+    loads[3].start()
     res_load = pltpu.make_async_copy(res_hbm, res_ref, res_sems.at[0])
     res_store = pltpu.make_async_copy(res_ref, res_out, res_sems.at[1])
     res_load.start()
-    member = lax.axis_index("tok")
     grad_ref[...] = jnp.zeros_like(grad_ref)
     dgain_ref[...] = jnp.zeros_like(dgain_ref)
 
@@ -441,12 +448,6 @@
     def sample_step(s, carry):
         for copy in sample_loads(s):
             copy.wait()
-
-        @pl.when(s == 0)
-        def _():
-            for copy in loads[2:5]:
-                copy.wait()
-
         start = bounds_ref[s]
         total = bounds_ref[samples + s]
         base = lax.div(start, 16) * 16
@@ -497,19 +498,7 @@
         at = pl.ds(pl.multiple_of(s * lat_rows, lat_rows), lat_rows)
         dquery = (turn_ref[...].T * 0.125).astype(BF16)
         dquery_ref[at, :] = dquery
-        unit, inv = norm_parts(lat_ref[at, :].astype(F32))
-        dnormed = dot(dquery, wq_ref[...], (1, 1))
-        dgain_ref[0:1, :] += jnp.sum(dnormed * unit, 0, keepdims=True)
-        dlat = norm_back(unit, inv, row(gain_q_ref), dnormed)
-        dlat_ref[at, :] = dlat
-        j = s - lax.rem(member, 2) * (samples // 2)
-
-        @pl.when((member < 2) & (j >= 0) & (j < samples // 2))
-        def _():
-            mine = pl.ds(pl.multiple_of(j * lat_rows, lat_rows), lat_rows)
-            dlat_ref[at, :] = dlat + dmid_ref[mine, :]
-
-        dlat_store(s).start()
+        dquery_store(s).start()
         return carry
 
     lax.fori_loop(0, samples, sample_step, 0)
@@ -520,7 +509,9 @@
         dkv_ref[1, r : r + step, :] = dv_ref[r : r + step, :].astype(BF16)
     dkv_store = pltpu.make_async_copy(dkv_ref, dkv_out, store_sem.at[0])
     dkv_store.start()
-    loads[5].wait()
+    loads[2].wait()
+    loads[3].wait()
+    gain = jnp.zeros((1, width), F32)
     stores = []
     for c in range(0, width, 256):
         dwq_ref[c : c + 256, :] = dot(dquery_ref[:, c : c + 256], normed_ref[...], (0, 0))
@@ -529,20 +520,24 @@
         )
         copy.start()
         stores.append(copy)
+        weight = wq_ref[:, c : c + 256].astype(F32).T
+        gain += jnp.sum(weight * dwq_ref[c : c + 256, :], 0, keepdims=True)
+    dgain_ref[0:1, :] = gain / row(gain_q_ref)
     res_store.wait()
     dkv_store.wait()
     for copy in stores:
         copy.wait()
 
     def finish(s, carry):
-        dlat_store(s).wait()
+        dquery_store(s).wait()
         return carry
 
     lax.fori_loop(0, samples, finish, 0)
 
 
-def attend_backward(bounds, latents, keys, values, query, normed, msg, dmid, gain_q, wq, result):
-    samples, lat_rows, width = latents.shape
+def attend_backward(bounds, keys, values, query, normed, msg, gain_q, wq, result):
+    samples, _, lat_rows = msg.shape
+    width = wq.shape[0]
     rows = keys.shape[0] - PAD
     sds = jax.ShapeDtypeStruct
     return pl.pallas_call(
@@ -550,12 +545,12 @@
         name="attend_backward",
         out_shape=(
             sds((2, rows, width), BF16),
-            sds((samples * lat_rows, width), F32),
+            sds((samples * lat_rows, width), BF16),
             sds((8, width), F32),
             sds((width, width), F32),
             sds(result.shape, BF16),
         ),
-        in_specs=[smem()] + [anywhere()] * 7 + [vmem()] + [anywhere()] * 2,
+        in_specs=[smem()] + [anywhere()] * 5 + [vmem()] + [anywhere()] * 2,
         out_specs=(anywhere(),) * 2 + (vmem(),) + (anywhere(),) * 2,
         scratch_shapes=[
             pltpu.VMEM((rows + PAD, width), F32),
@@ -566,18 +561,15 @@
             pltpu.VMEM((16, 2 * lat_rows), F32),
             pltpu.VMEM(result.shape, BF16),
             pltpu.SemaphoreType.DMA((2,)),
-            pltpu.VMEM((samples * lat_rows, width), BF16),
             pltpu.VMEM((rows + PAD, width), BF16),
             pltpu.VMEM((rows + PAD, width), BF16),
             pltpu.VMEM(query.shape, BF16),
             pltpu.VMEM(normed.shape, BF16),
             pltpu.VMEM(msg.shape, F32),
-            pltpu.VMEM(dmid.shape, F32),
             pltpu.VMEM(wq.shape, BF16),
             pltpu.VMEM((2, rows, width), BF16),
-            pltpu.VMEM((samples * lat_rows, width), F32),
             pltpu.VMEM((width, width), F32),
-            pltpu.SemaphoreType.DMA((6,)),
+            pltpu.SemaphoreType.DMA((4,)),
             pltpu.SemaphoreType.DMA((2, samples)),
             pltpu.SemaphoreType.DMA((samples,)),
             pltpu.SemaphoreType.DMA((1 + width // 256,)),
@@ -585,13 +577,11 @@
         compiler_params=pltpu.CompilerParams(vmem_limit_bytes=VMEM_BYTES),
     )(
         bounds,
-        latents.reshape(samples * lat_rows, width),
         keys,
         values,
         query,
         normed,
         msg,
-        dmid,
         gain_q,
         wq,
         result,
@@ -1194,11 +1184,12 @@
     )
 
 
-ZROWS = 32
-
-
 def gradient_kernel(
-    dlat_hbm,
+    dquery_hbm,
+    dmid_hbm,
+    lat_hbm,
+    gain_q_ref,
+    wq_hbm,
     a_hbm,
     b_hbm,
     side_ref,
@@ -1236,6 +1227,10 @@
     spread_ref,
     stage_ref,
     stage_sem,
+    dsend_ref,
+    dquery_ref,
+    lat_ref,
+    wq_ref,
     a_ref,
     b_ref,
     dwq_ref,
@@ -1305,6 +1300,7 @@
     first = (flip_x, flip_y)
     has_right = chip < chips - 1
     has_left = chip > 0
+    here = (chip == 0).astype(F32)
 
     barrier = pltpu.get_barrier_semaphore()
     for target in (partner,) + near:
@@ -1334,28 +1330,45 @@
             (
                 (tsort_hbm, tsort_ref),
                 (dkv_hbm, dkv_ref),
-                (dlat_hbm.at[core], dmine_ref),
+                (dmid_hbm, dmine_ref),
                 (a_hbm, a_ref),
                 (b_hbm, b_ref),
                 (dwq_hbm, dwq_ref),
                 (tok_hbm, tok_ref),
+                (dquery_hbm, dquery_ref),
+                (lat_hbm, lat_ref),
+                (wq_hbm, wq_ref),
             )
         )
     ]
-    for copy in pulls:
-        copy.start()
+    for n in (7, 8, 9, 2, 0, 1, 5, 3, 4, 6):
+        pulls[n].start()
     pl.semaphore_wait(barrier, 3 + has_right.astype(jnp.int32) + has_left.astype(jnp.int32))
 
     def dpair_copy(i):
         return remote(
-            dlat_hbm.at[other, i], line_ref.at[i], dpair_send.at[i], dpair_recv.at[i], partner
-        )
-
-    def start_dpair(i, carry):
-        dpair_copy(i).start()
-        return carry
-
-    lax.fori_loop(0, lat_chunks, start_dpair, 0)
+            dsend_ref.at[i], line_ref.at[i], dpair_send.at[i], dpair_recv.at[i], partner
+        )
+
+    lat_rows = 128
+    per_sample = lat_rows // ZROWS
+
+    def lat_gradient(which, j):
+        sample = which * (lat_chunks // per_sample) + j
+        at = pl.ds(pl.multiple_of(sample * lat_rows, lat_rows), lat_rows)
+        unit, inv = norm_parts(lat_ref[at, :].astype(F32))
+        dnormed = dot(dquery_ref[at, :], wq_ref[...], (1, 1))
+        return norm_back(unit, inv, row(gain_q_ref), dnormed)
+
+    def lat_event(j):
+        grad = lat_gradient(other, j)
+        for c in range(per_sample):
+            dsend_ref[j * per_sample + c] = grad[c * ZROWS : (c + 1) * ZROWS]
+            dpair_copy(j * per_sample + c).start()
+        grad = lat_gradient(core, j)
+        for c in range(per_sample):
+            i = j * per_sample + c
+            dmine_ref[i] = grad[c * ZROWS : (c + 1) * ZROWS] + dmine_ref[i] * here
 
     def wide_one_copy(h, n, sub):
         block = (first[h], flip_xy)[n]
@@ -1425,6 +1438,9 @@
         wide_ref[block, width:, :] = side_ref[block]
 
     def wide_start(k):
+        if k == 0:
+            pulls[3].wait()
+            pulls[4].wait()
         wide_product((flip_xy, first[0], first[1], stream)[k])
         for sub in range(EARLY_SUBS):
             for h in range(2):
@@ -1477,6 +1493,8 @@
         return dot(tsort_ref[:, at], dkv_ref[which], (0, 0))
 
     def token_other():
+        for n in (0, 1, 5):
+            pulls[n].wait()
         gain_ref[...] = jnp.zeros_like(gain_ref)
         for block in range(4):
             product = token_product(block, other)
@@ -1526,8 +1544,6 @@
         for k in range(4):
             pair_copy(k, 0, 2).start()
 
-    here = (chip == 0).astype(F32)
-
     token_step = 128
 
     def stage_copy(i):
@@ -1538,6 +1554,8 @@
         )
 
     def token_part(i):
+        if i == 0:
+            pulls[6].wait()
         at = pl.ds(pl.multiple_of(i * token_step, token_step), token_step)
         target = lax.broadcasted_iota(jnp.int32, (token_step, rows), 1).astype(F32)
         pick = jnp.where(target == place_ref[at, 0:1], 1.0, 0.0).astype(BF16)
@@ -1619,7 +1637,7 @@
             dpair_copy(t).wait_recv()
             line_ref[t] += dmine_ref[t]
 
-        r, r_due = placed(t - LAG * chip)
+        r, r_due = placed(t - LINE_LAG * chip)
 
         @pl.when(r_due)
         def _():
@@ -1636,7 +1654,7 @@
             def _():
                 right_copy(r).start()
 
-        u, u_due = placed(t - LAG * (chips - 1 - chip))
+        u, u_due = placed(t - LINE_LAG * (chips - 1 - chip))
 
         @pl.when(u_due)
         def _():
@@ -1653,7 +1671,7 @@
             def _():
                 left_copy(u).start()
 
-        w, w_due = placed(t - LAG * jnp.maximum(chip, chips - 1 - chip))
+        w, w_due = placed(t - LINE_LAG * jnp.maximum(chip, chips - 1 - chip))
 
         @pl.when(w_due)
         def _():
@@ -1726,7 +1744,7 @@
         return i, due & (t >= lat_chunks + GAP) & (c < kv_chunks)
 
     def spread_step(t):
-        lag = LAG * jnp.maximum(chip, chips - 1 - chip)
+        lag = LINE_LAG * jnp.maximum(chip, chips - 1 - chip)
         i, due = spread_due(t - lag)
 
         @pl.when(due)
@@ -1793,7 +1811,7 @@
             chunk, row = at // ZROWS, at % ZROWS
             small_out[...] = line_ref[chunk, row : row + 16, :]
 
-    tail = LAG * (chips - 1)
+    tail = LINE_LAG * (chips - 1)
     ready = lambda h: lat_chunks + GAP + (h + 1) * half_chunks - 1 + tail
     events = {}
 
@@ -1816,8 +1834,11 @@
         at_tick(WIDE_TWO_TICKS[sub], functools.partial(wide_event_two, sub))
         if WIDE_THREE_TICKS[sub] >= 0:
             at_tick(WIDE_THREE_TICKS[sub], functools.partial(wide_event_three, sub))
-    for copy in pulls:
-        copy.wait()
+    for n in (7, 8, 9, 2):
+        pulls[n].wait()
+    lat_event(0)
+    for j in range(1, lat_chunks // per_sample):
+        at_tick(LAT_TICKS[j - 1], functools.partial(lat_event, j))
 
     def step(t, carry):
         line_step(t)
@@ -1895,10 +1916,11 @@
 
 
 def gradients(
-    dlat, a, b, side, dwq, vec, dgain_q, place, tokens, tsort, dkv, gain_t, wk, wv
+    dquery, dmid, latents, gain_q, wq, a, b, side, dwq, vec, dgain_q, place, tokens, tsort, dkv,
+    gain_t, wk, wv,
 ):
     rows, width = tokens.shape
-    half = dlat.shape[0] // 2
+    half = dquery.shape[0] // 2
     lat_chunks = half // ZROWS
     wide_rows, wide_cols = a.shape[1] + side.shape[1], b.shape[2]
     share = width // 4
@@ -1921,6 +1943,8 @@
             sds((rows, width), F32),
         ),
         in_specs=[anywhere()] * 3
+        + [vmem()]
+        + [anywhere()] * 3
         + [vmem(), anywhere()]
         + [vmem()] * 3
         + [anywhere()] * 3
@@ -1945,13 +1969,17 @@
             buf(3, 2, kv_rows // ZROWS, ZROWS, width),
             buf(2, 128, width),
             dma((2,)),
+            buf(lat_chunks, ZROWS, width),
+            pltpu.VMEM(dquery.shape, BF16),
+            pltpu.VMEM(dquery.shape, BF16),
+            pltpu.VMEM(wq.shape, BF16),
             pltpu.VMEM(a.shape, BF16),
             pltpu.VMEM(b.shape, BF16),
             buf(4, 2, 2, q_rows, width),
             pltpu.VMEM(tokens.shape, BF16),
             pltpu.VMEM(tsort.shape, BF16),
             pltpu.VMEM(dkv.shape, BF16),
-            dma((7,)),
+            dma((10,)),
         ]
         + both(lat_chunks)
         + both(all_chunks)
@@ -1974,7 +2002,11 @@
             vmem_limit_bytes=VMEM_BYTES, collective_id=2, has_side_effects=True
         ),
     )(
-        dlat.reshape(2, lat_chunks, ZROWS, width),
+        dquery,
+        dmid.reshape(lat_chunks, ZROWS, width),
+        latents.reshape(2 * half, width),
+        gain_q,
+        wq,
         a,
         b,
         side,
@@ -2149,11 +2181,12 @@
     msg, result, dmid, a, b, side, vec = latent_block(
         part, drop_mask, latents, cotangent, w_out, gain_mlp, w_up, b_up, w_down, b_down
     )
-    dkv, dlat, dgain_q, dwq, result = attend_backward(
-        bounds, latents, keys, values, query, normed, msg, dmid, gain_query, w_query, result
+    dkv, dquery, dgain_q, dwq, result = attend_backward(
+        bounds, keys, values, query, normed, msg, gain_query, w_query, result
     )
     dlat, gather, kv, dwq, small, d_tokens = gradients(
-        dlat, a, b, side, dwq, vec, dgain_q, place, tokens, tsort, dkv, gain_token,
+        dquery, dmid, latents, gain_query, w_query, a, b, side, dwq, vec, dgain_q, place, tokens,
+        tsort, dkv, gain_token,
         w_key, w_value,
     )
     (

time: 255 us -> 247 us (0.969)
  Pallas kernels: 254 us -> 247 us
    pallas_call x1, Pallas kernels: 128 us -> 122 us  [gradients(): pl.pallas_call(gradient_kernel, name='gradients', out_shape=(sds((2, lat_...]
where the time goes in v7:
time: 247 us; the launch traced here: 248 us
  Pallas kernels  247 us (100%)
    pallas_call x1, Pallas kernels, gradients(): pl.pallas_call(gradient_kernel, name='gradients', out_shape=(sds((2, lat_...  122 us
    pallas_call x1, Pallas kernels, latent_block(): pl.pallas_call(latent_kernel, name='latent_block', out_shape=(sds((sample...  72.4 us
    pallas_call x1, Pallas kernels, attend_forward(): pl.pallas_call(forward_kernel, name='attend_forward', out_shape=(sds((sam...  21.4 us
    pallas_call x1, Pallas kernels, attend_backward(): pl.pallas_call(backward_kernel, name='attend_backward', out_shape=(sds((2...  17.9 us
    pallas_call x1, Pallas kernels, closing(): pl.pallas_call(closing_kernel, name='closing', out_shape=(sds(*dlat.shape...  13 us

profile of v7, /device:TPU:0, one launch (start us, length us, event | category | flops | bytes accessed | tf_op | source)
XLA Modules:
  0.0 247.9 jit_solution(15844918894048242609)
XLA Ops:
  0.6 21.4 %attend_forward.1 = (f32[8,4,208,128]{3,2,1,0:T(8,128)}, bf16[1280,768]{1,0:T(8,128)(2,1)}, bf16[1280,768]{1,0:T(8,128)(2,1)}, bf16[1024,768]{1,0:T(8,128)(2,1)}...) custom-call(s32[1024]{0:T(1024)} %sample_ref.1, ...), custom_call_target="tpu_custom_call" | custom-call | tf_op jit(solution)/shard_map/attend_forward/pallas_call | solution.py:309
  22.1 72.4 %latent_block.1 = (f32[8,800,128]{2,1,0:T(8,128)}, bf16[1024,768]{1,0:T(8,128)(2,1)}, f32[512,768]{1,0:T(8,128)}, bf16[1024,768]{1,0:T(8,128)(2,1)}, bf16[4,1024...) custom-call(f32[32,208,128]{2,1,0:T(8,128)} %bitcast.16, s32[32]{0:T(128)} %drop_ref.1, ...), custom_call_target="tpu_custom_call" | custom-call | tf_op jit(solution)/shard_map/latent_block/pallas_call | solution.py:1092
  94.5 17.9 %attend_backward.1 = (bf16[2,1024,768]{2,1,0:T(8,128)(2,1)}, bf16[1024,768]{1,0:T(8,128)(2,1)}, f32[8,768]{1,0:T(8,128)}, f32[768,768]{1,0:T(8,128)}, bf16[1024,768]{1,0:T(8,128)(2,1)}) custom-call(s32[16]{0:T(128)} %get-tuple-element.53.bounds_ref, bf16[1280,768]{1,0:T(8,128)(2,1)} %get-tuple-element.54.key_hbm, ...), custom_call_target="tpu_custom_call" | custom-call | tf_op jit(solution)/shard_map/attend_backward/pallas_call | solution.py:543
  112.4 122.3 %gradients.1 = (f32[2,16,32,768]{3,2,1,0:T(8,128)}, f32[2,2,864,384]{3,2,1,0:T(8,128)}, f32[2,4,2,3,32,768]{5,4,3,2,1,0:T(8,128)}, f32[2,2,48,768]{3,2,1,0:T(8,1...) custom-call(bf16[1024,768]{1,0:T(8,128)(2,1)} %get-tuple-element.62.dquery_hbm, f32[16,32,768]{2,1,0:T(8,128)} %bitcast.20, ...), custom_call_target="tpu_custom_call" | custom-call | tf_op jit(solution)/shard_map/gradients/pallas_call | solution.py:1934
  234.8 13.0 %closing.1 = (f32[1024,768]{1,0:T(8,128)}, f32[1024,768]{1,0:T(8,128)}, f32[768,768]{1,0:T(8,128)}, f32[768,768]{1,0:T(8,128)}, f32[768,768]{1,0:T(8,128)}, /*in...) custom-call(f32[1024,768]{1,0:T(8,128)} %bitcast.17, ...), custom_call_target="tpu_custom_call" | custom-call | tf_op jit(solution)/shard_map/closing/pallas_call | solution.py:2124

commit v8 on v7

--- a/solution.py
+++ b/solution.py
@@ -24,18 +24,18 @@
 GAP = 6
 SUBS = 3
 EARLY_SUBS = 1
-SPREAD_LAG = 4
+SPREAD_LAG = 5
 WIDE_START_TICKS = (1, 2, 2, 4)
 KV_TICKS = (0, 3)
 PAIR_TICK = 5
-MORE_TICK = 16
+MORE_TICK = 20
 ONE_TICK = 15
 TWO_TICK = 20
 WIDE_ONE_TICKS = (10, 27, 30)
 WIDE_TWO_TICKS = (16, 32, 35)
 WIDE_THREE_TICKS = (25, -1, -1)
 LAT_TICKS = (0, 4, 8)
-TOKEN_TICKS = (6, 7, 8, 9, 11, 12, 13, 16)
+TOKEN_TICKS = (22, 23, 24, 25, 26, 27, 28, 29)
 NEG = -1e30
 F32 = jnp.float32
 BF16 = jnp.bfloat16

time: 247 us -> 247 us (level)
  no operation moved by 1% of the time
where the time goes in v8:
time: 247 us
  Pallas kernels  246 us (100%)
    pallas_call x1, Pallas kernels, gradients(): pl.pallas_call(gradient_kernel, name='gradients', out_shape=(sds((2, lat_...  125 us
    pallas_call x1, Pallas kernels, latent_block(): pl.pallas_call(latent_kernel, name='latent_block', out_shape=(sds((sample...  71.7 us
    pallas_call x1, Pallas kernels, attend_forward(): pl.pallas_call(forward_kernel, name='attend_forward', out_shape=(sds((sam...  20.4 us
    pallas_call x1, Pallas kernels, attend_backward(): pl.pallas_call(backward_kernel, name='attend_backward', out_shape=(sds((2...  16.5 us
    pallas_call x1, Pallas kernels, closing(): pl.pallas_call(closing_kernel, name='closing', out_shape=(sds(*dlat.shape...  13 us

profile of v8, /device:TPU:0, one launch (start us, length us, event | category | flops | bytes accessed | tf_op | source)
XLA Modules:
  0.0 247.0 jit_solution(18317873044175795721)
XLA Ops:
  0.6 20.4 %attend_forward.1 = (f32[8,4,208,128]{3,2,1,0:T(8,128)}, bf16[1280,768]{1,0:T(8,128)(2,1)}, bf16[1280,768]{1,0:T(8,128)(2,1)}, bf16[1024,768]{1,0:T(8,128)(2,1)}...) custom-call(s32[1024]{0:T(1024)} %sample_ref.1, ...), custom_call_target="tpu_custom_call" | custom-call | tf_op jit(solution)/shard_map/attend_forward/pallas_call | solution.py:309
  21.0 71.7 %latent_block.1 = (f32[8,800,128]{2,1,0:T(8,128)}, bf16[1024,768]{1,0:T(8,128)(2,1)}, f32[512,768]{1,0:T(8,128)}, bf16[1024,768]{1,0:T(8,128)(2,1)}, bf16[4,1024...) custom-call(f32[32,208,128]{2,1,0:T(8,128)} %bitcast.16, s32[32]{0:T(128)} %drop_ref.1, ...), custom_call_target="tpu_custom_call" | custom-call | tf_op jit(solution)/shard_map/latent_block/pallas_call | solution.py:1092
  92.7 16.5 %attend_backward.1 = (bf16[2,1024,768]{2,1,0:T(8,128)(2,1)}, bf16[1024,768]{1,0:T(8,128)(2,1)}, f32[8,768]{1,0:T(8,128)}, f32[768,768]{1,0:T(8,128)}, bf16[1024,768]{1,0:T(8,128)(2,1)}) custom-call(s32[16]{0:T(128)} %get-tuple-element.53.bounds_ref, bf16[1280,768]{1,0:T(8,128)(2,1)} %get-tuple-element.54.key_hbm, ...), custom_call_target="tpu_custom_call" | custom-call | tf_op jit(solution)/shard_map/attend_backward/pallas_call | solution.py:543
  109.2 124.6 %gradients.1 = (f32[2,16,32,768]{3,2,1,0:T(8,128)}, f32[2,2,864,384]{3,2,1,0:T(8,128)}, f32[2,4,2,3,32,768]{5,4,3,2,1,0:T(8,128)}, f32[2,2,48,768]{3,2,1,0:T(8,1...) custom-call(bf16[1024,768]{1,0:T(8,128)(2,1)} %get-tuple-element.62.dquery_hbm, f32[16,32,768]{2,1,0:T(8,128)} %bitcast.20, ...), custom_call_target="tpu_custom_call" | custom-call | tf_op jit(solution)/shard_map/gradients/pallas_call | solution.py:1934
  233.9 13.0 %closing.1 = (f32[1024,768]{1,0:T(8,128)}, f32[1024,768]{1,0:T(8,128)}, f32[768,768]{1,0:T(8,128)}, f32[768,768]{1,0:T(8,128)}, f32[768,768]{1,0:T(8,128)}, /*in...) custom-call(f32[1024,768]{1,0:T(8,128)} %bitcast.17, ...), custom_call_target="tpu_custom_call" | custom-call | tf_op jit(solution)/shard_map/closing/pallas_call | solution.py:2124

commit v9 on v8

--- a/solution.py
+++ b/solution.py
@@ -2054,34 +2054,43 @@
 ):
     width = small_ref.shape[1]
     cols = wide_ref.shape[2]
-    loads = [
-        pltpu.make_async_copy(src, dst, load_sems.at[i])
-        for i, (src, dst) in enumerate(
-            (
-                (gather_hbm.at[1], wide_ref),
-                (gather_hbm.at[0], up_ref),
-                (dlat_hbm, dlat_ref),
-                (kv_hbm, kv_ref),
-                (dtok_hbm, dtok_ref),
+    wide_load = pltpu.make_async_copy(gather_hbm.at[1], wide_ref, load_sems.at[0])
+    up_load = pltpu.make_async_copy(gather_hbm.at[0], up_ref, load_sems.at[1])
+    up_stores = [
+        pltpu.make_async_copy(
+            up_ref.at[e, pl.ds(0, width)], up_out.at[:, pl.ds(e * cols, cols)], store_sems.at[e]
+        )
+        for e in range(2)
+    ]
+    down_stores = [
+        pltpu.make_async_copy(
+            down_ref.at[pl.ds(e * cols, cols)],
+            down_out.at[pl.ds(e * cols, cols)],
+            store_sems.at[2 + e],
+        )
+        for e in range(2)
+    ]
+    moves = []
+    for src, mid, dst in (
+        (kv_hbm.at[0], kv_ref.at[0], key_out),
+        (kv_hbm.at[1], kv_ref.at[1], val_out),
+        (dlat_hbm, dlat_ref, dlat_out),
+        (dtok_hbm, dtok_ref, dtok_out),
+    ):
+        span = mid.shape[0] // 4
+        for n in range(4):
+            at = pl.ds(n * span, span)
+            k = len(moves)
+            moves.append(
+                (
+                    pltpu.make_async_copy(src.at[at], mid.at[at], load_sems.at[2 + k]),
+                    pltpu.make_async_copy(mid.at[at], dst.at[at], store_sems.at[4 + k]),
+                )
             )
-        )
-    ]
-    for copy in loads:
-        copy.start()
-    stores = [
-        pltpu.make_async_copy(src, dst, store_sems.at[i])
-        for i, (src, dst) in enumerate(
-            (
-                (up_ref.at[0, pl.ds(0, width)], up_out.at[:, pl.ds(0, cols)]),
-                (up_ref.at[1, pl.ds(0, width)], up_out.at[:, pl.ds(cols, cols)]),
-                (dlat_ref, dlat_out),
-                (kv_ref.at[0], key_out),
-                (kv_ref.at[1], val_out),
-                (dtok_ref, dtok_out),
-                (down_ref, down_out),
-            )
-        )
-    ]
+    wide_load.start()
+    for load, _ in moves:
+        load.start()
+    up_load.start()
     stream = lax.axis_index("stream")
     gain_t_ref[...] = small_ref[4]
     bup_ref[...] = small_ref[0]
@@ -2093,26 +2102,26 @@
             piece = jnp.where(stream == k, line[:, k * size : (k + 1) * size], piece)
         ref[...] = piece[0]
     wq_ref[...] = query_ref[...]
-    loads[0].wait()
+    wide_load.wait()
     for e in range(2):
         down_ref[e * cols : (e + 1) * cols, :] = wide_ref[e, :width, :].T
-    stores[6].start()
-    loads[1].wait()
-    stores[0].start()
-    stores[1].start()
+        down_stores[e].start()
+        for load, store in moves[2 * e : 2 * e + 2]:
+            load.wait()
+            store.start()
+    for load, store in moves[4:]:
+        load.wait()
+        store.start()
+    up_load.wait()
     half = up_ref.shape[1] - width
     for e in range(2):
+        up_stores[e].start()
         out_ref[:half, e * cols : (e + 1) * cols] = up_ref[e, width:, :]
         out_ref[half:, e * cols : (e + 1) * cols] = wide_ref[e, width:, :]
-    loads[2].wait()
-    stores[2].start()
-    loads[3].wait()
-    stores[3].start()
-    stores[4].start()
-    loads[4].wait()
-    stores[5].start()
-    for copy in stores:
+    for copy in up_stores + down_stores:
         copy.wait()
+    for _, store in moves:
+        store.wait()
 
 
 def closing(dlat, gather, kv, query, small, dtok):
@@ -2148,8 +2157,8 @@
             pltpu.VMEM(kv.shape, F32),
             pltpu.VMEM(dtok.shape, F32),
             pltpu.VMEM((2 * cols, width), F32),
-            pltpu.SemaphoreType.DMA((5,)),
-            pltpu.SemaphoreType.DMA((7,)),
+            pltpu.SemaphoreType.DMA((18,)),
+            pltpu.SemaphoreType.DMA((20,)),
         ],
         compiler_params=pltpu.CompilerParams(vmem_limit_bytes=VMEM_BYTES),
     )(dlat, gather, kv, query, small, dtok)

time: 247 us -> 248 us (level)
  no operation moved by 1% of the time
where the time goes in v9:
time: 248 us; the launch traced here: 247 us
  Pallas kernels  247 us (100%)
    pallas_call x1, Pallas kernels, gradients(): pl.pallas_call(gradient_kernel, name='gradients', out_shape=(sds((2, lat_...  122 us
    pallas_call x1, Pallas kernels, latent_block(): pl.pallas_call(latent_kernel, name='latent_block', out_shape=(sds((sample...  70.7 us
    pallas_call x1, Pallas kernels, attend_forward(): pl.pallas_call(forward_kernel, name='attend_forward', out_shape=(sds((sam...  21.2 us
    pallas_call x1, Pallas kernels, attend_backward(): pl.pallas_call(backward_kernel, name='attend_backward', out_shape=(sds((2...  18 us
    pallas_call x1, Pallas kernels, closing(): pl.pallas_call(closing_kernel, name='closing', out_shape=(sds(*dlat.shape...  14.2 us

profile of v9, /device:TPU:0, one launch (start us, length us, event | category | flops | bytes accessed | tf_op | source)
XLA Modules:
  0.0 247.4 jit_solution(7800139440733388567)
XLA Ops:
  0.6 21.2 %attend_forward.1 = (f32[8,4,208,128]{3,2,1,0:T(8,128)}, bf16[1280,768]{1,0:T(8,128)(2,1)}, bf16[1280,768]{1,0:T(8,128)(2,1)}, bf16[1024,768]{1,0:T(8,128)(2,1)}...) custom-call(s32[1024]{0:T(1024)} %sample_ref.1, ...), custom_call_target="tpu_custom_call" | custom-call | tf_op jit(solution)/shard_map/attend_forward/pallas_call | solution.py:309
  21.8 70.7 %latent_block.1 = (f32[8,800,128]{2,1,0:T(8,128)}, bf16[1024,768]{1,0:T(8,128)(2,1)}, f32[512,768]{1,0:T(8,128)}, bf16[1024,768]{1,0:T(8,128)(2,1)}, bf16[4,1024...) custom-call(f32[32,208,128]{2,1,0:T(8,128)} %bitcast.16, s32[32]{0:T(128)} %drop_ref.1, ...), custom_call_target="tpu_custom_call" | custom-call | tf_op jit(solution)/shard_map/latent_block/pallas_call | solution.py:1092
  92.5 18.0 %attend_backward.1 = (bf16[2,1024,768]{2,1,0:T(8,128)(2,1)}, bf16[1024,768]{1,0:T(8,128)(2,1)}, f32[8,768]{1,0:T(8,128)}, f32[768,768]{1,0:T(8,128)}, bf16[1024,768]{1,0:T(8,128)(2,1)}) custom-call(s32[16]{0:T(128)} %get-tuple-element.53.bounds_ref, bf16[1280,768]{1,0:T(8,128)(2,1)} %get-tuple-element.54.key_hbm, ...), custom_call_target="tpu_custom_call" | custom-call | tf_op jit(solution)/shard_map/attend_backward/pallas_call | solution.py:543
  110.6 122.4 %gradients.1 = (f32[2,16,32,768]{3,2,1,0:T(8,128)}, f32[2,2,864,384]{3,2,1,0:T(8,128)}, f32[2,4,2,3,32,768]{5,4,3,2,1,0:T(8,128)}, f32[2,2,48,768]{3,2,1,0:T(8,1...) custom-call(bf16[1024,768]{1,0:T(8,128)(2,1)} %get-tuple-element.62.dquery_hbm, f32[16,32,768]{2,1,0:T(8,128)} %bitcast.20, ...), custom_call_target="tpu_custom_call" | custom-call | tf_op jit(solution)/shard_map/gradients/pallas_call | solution.py:1934
  233.0 14.2 %closing.1 = (f32[1024,768]{1,0:T(8,128)}, f32[1024,768]{1,0:T(8,128)}, f32[768,768]{1,0:T(8,128)}, f32[768,768]{1,0:T(8,128)}, f32[768,768]{1,0:T(8,128)}, /*in...) custom-call(f32[1024,768]{1,0:T(8,128)} %bitcast.17, ...), custom_call_target="tpu_custom_call" | custom-call | tf_op jit(solution)/shard_map/closing/pallas_call | solution.py:2133
